TPU v7x, 32 devices: a whole 2x2x4 slice. The times are simulated.
32 devices in a mesh: rows: 16 (over z, x, core), img: 2 (over y).
Axes of the slice: x: 2, y: 2, z: 4, core: 2. Of those that a mesh axis runs over, the one named last changes fastest.
Arguments:
- triplane: bfloat16 [12288, 1024], P(('rows', 'img')), may hold values from -6 to 6
- cotangent: bfloat16 [12288, 1024], P(('rows', 'img')), may hold values from -6 to 6
- image_tokens: bfloat16 [16640, 768], P(('rows', 'img')), may hold values from -6 to 6
- modulation: float32 [16, 6, 1024], replicated, may hold values from -1.75 to 1.75
- image_counts: int32 [16], replicated, may hold values from 257 to 1025, as said below
- owner_slots: int32 [248], replicated, may hold values from 0 to 255, as said below
- master_weights: float32 [256, 256, 256], P(('rows', 'img')), as said below
- first_moment: float32 [256, 256, 256], P(('rows', 'img')), as said below
- second_moment: float32 [256, 256, 256], P(('rows', 'img')), as said below
- left_basis: float32 [256, 256, 256], P(('rows', 'img')), may hold values from -0.375 to 0.375
- right_basis: float32 [256, 256, 256], P(('rows', 'img')), may hold values from -0.375 to 0.375
Outputs:
- layer_out: bfloat16 [12288, 1024], P(('rows', 'img'))
- grad_triplane: float32 [12288, 1024], P(('rows', 'img'))
- grad_image: float32 [16640, 768], P(('rows', 'img'))
- weight_grads: float32 [256, 256, 256], P(('rows', 'img'))
- new_first_moment: float32 [256, 256, 256], P(('rows', 'img'))
- new_second_moment: float32 [256, 256, 256], P(('rows', 'img'))
- new_master: float32 [256, 256, 256], P(('rows', 'img'))
- new_weights: bfloat16 [256, 256, 256], P(('rows', 'img'))
Inputs may be any that keep to these rules, and one draw needn't show every extreme that they name: `image_counts`: each count is 257 or 1025. `owner_slots`: distinct slots; slot s lies on device s // 8 of rows+img. `master_weights`: float32 values. `first_moment`: float32 values. `second_moment`: positive float32 values.
All inputs are finite; a program needn't handle non-finite values.
Results may differ from a plain program's by a relative error of at most 0.017.
Values may be sent and summed in bfloat16 or wider, within the bound.
A program may use at most 320 MiB of HBM per device.

v0:
```python
import jax
import jax.numpy as jnp
import numpy as np
from jax import lax
from jax.sharding import PartitionSpec as P

D = 1024
HEADS = 16
FF = 4096
DIMG = 768
TOK_DEV = 384
IMG_MAX = 1025
BLOCK = 256
STEP = 5


highest = lax.Precision.HIGHEST
moment_decay = 0.5


def partner(block, axis, apart):
    count = lax.axis_size(axis)
    route = []
    for low in range(count):
        high = low | 1 << apart
        if high != low and high < count:
            route += [(low, high), (high, low)]
    return lax.ppermute(block, axis, route)


def shapes_list():
    return [(D, D), (DIMG, D), (DIMG, D), (D, D), (D, D), (D, D), (D, D), (D, D), (D, FF), (FF, D)]


def weight_scales():
    self_root = (2.0 * TOK_DEV) ** 0.5
    cross_root = (IMG_MAX / 2.0) ** 0.5
    return [
        D ** (-0.5),
        DIMG ** (-0.5),
        DIMG ** (-0.5),
        0.5 * cross_root * D ** (-0.5),
        D ** (-0.5),
        D ** (-0.5),
        D ** (-0.5),
        0.5 * self_root * D ** (-0.5),
        D ** (-0.5),
        2.0 * FF ** (-0.5),
    ]


def block_table(scales):
    pieces = []
    for shape_pair, scale_value in zip(shapes_list(), scales):
        amount = shape_pair[0] * shape_pair[1] // (BLOCK * BLOCK)
        pieces.append(np.full((amount,), scale_value, np.float32))
    return np.concatenate(pieces)


def split_blocks(blocks):
    matrices = []
    begin_at = 0
    for rows_in, cols_out in shapes_list():
        amount = rows_in * cols_out // (BLOCK * BLOCK)
        grid = blocks[begin_at : begin_at + amount].reshape(
            rows_in // BLOCK, cols_out // BLOCK, BLOCK, BLOCK
        )
        matrices.append(grid.transpose(0, 2, 1, 3).reshape(rows_in, cols_out))
        begin_at = begin_at + amount
    return matrices


def join_blocks(matrices):
    pieces = []
    for matrix in matrices:
        rows_in, cols_out = matrix.shape
        grid = matrix.reshape(rows_in // BLOCK, BLOCK, cols_out // BLOCK, BLOCK).transpose(
            0, 2, 1, 3
        )
        pieces.append(grid.reshape(-1, BLOCK, BLOCK))
    return jnp.concatenate(pieces, 0)


def modulated_norm(values, shift, scale):
    centered = values - jnp.mean(values, axis=-1, keepdims=True)
    variance = jnp.mean(centered * centered, axis=-1, keepdims=True)
    return centered * lax.rsqrt(variance + 1e-06) * (1.0 + scale) + shift


def norm_back(values, shift, scale, grad_normed):
    unused_out, pullback = jax.vjp(lambda inner: modulated_norm(inner, shift, scale), values)
    return pullback(grad_normed)[0]


def project(left, right):
    return jnp.dot(left, right, preferred_element_type=jnp.float32)


def heads_view(matrix):
    return matrix.reshape(matrix.shape[0], HEADS, D // HEADS).transpose(1, 0, 2)


def merge_heads(stacked):
    return stacked.transpose(1, 0, 2).reshape(stacked.shape[1], D)


def attend(queries, key_rows, value_rows, key_valid):
    scale_factor = (D // HEADS) ** (-0.5)

    def per_head(operands):
        head_query, head_key, head_value = operands
        scores = project(head_query, head_key.T) * scale_factor
        scores = jnp.where(key_valid[None, :], scores, -1e30)
        row_max = jnp.max(scores, axis=-1, keepdims=True)
        exponent = jnp.exp(scores - row_max)
        row_total = jnp.sum(exponent, axis=-1, keepdims=True)
        weights_low = (exponent / row_total).astype(jnp.bfloat16)
        mixed_out = project(weights_low, head_value)
        return (mixed_out, (row_max + jnp.log(row_total))[:, 0])

    mixed_out, log_total = lax.map(
        per_head, (heads_view(queries), heads_view(key_rows), heads_view(value_rows))
    )
    return (merge_heads(mixed_out).astype(jnp.bfloat16), log_total)


def attend_back(queries, key_rows, value_rows, key_valid, log_total, grad_mixed):
    scale_factor = (D // HEADS) ** (-0.5)

    def per_head(operands):
        head_query, head_key, head_value, head_total, head_grad = operands
        scores = project(head_query, head_key.T) * scale_factor
        scores = jnp.where(key_valid[None, :], scores, -1e30)
        weights_full = jnp.exp(scores - head_total[:, None])
        grad_weights = project(head_grad, head_value.T)
        inner_sum = jnp.sum(weights_full * grad_weights, axis=-1, keepdims=True)
        grad_scores = (weights_full * (grad_weights - inner_sum)).astype(jnp.bfloat16)
        grad_query = project(grad_scores, head_key) * scale_factor
        grad_key = project(grad_scores.T, head_query) * scale_factor
        grad_value = project(weights_full.astype(jnp.bfloat16).T, head_grad)
        return (grad_query, grad_key, grad_value)

    grad_query, grad_key, grad_value = lax.map(
        per_head,
        (
            heads_view(queries),
            heads_view(key_rows),
            heads_view(value_rows),
            log_total,
            heads_view(grad_mixed),
        ),
    )
    return (merge_heads(grad_query), merge_heads(grad_key), merge_heads(grad_value))


def soap_update(
    slot_grads,
    first_moment,
    second_moment,
    left_basis,
    right_basis,
    master_weights,
    slot_rates,
    slot_used,
):
    rotated = jnp.matmul(
        jnp.matmul(jnp.swapaxes(left_basis, 1, 2), slot_grads, precision=highest),
        right_basis,
        precision=highest,
    )
    first_new = moment_decay * first_moment + (1.0 - moment_decay) * rotated
    second_new = moment_decay * second_moment + (1.0 - moment_decay) * rotated * rotated
    correction = 1.0 - moment_decay**STEP
    normalized = first_new / correction / (jnp.sqrt(second_new / correction) + 1e-08)
    rotated_back = jnp.matmul(
        jnp.matmul(left_basis, normalized, precision=highest),
        jnp.swapaxes(right_basis, 1, 2),
        precision=highest,
    )
    fresh_master = master_weights - slot_rates[:, None, None] * (
        rotated_back + 0.01 * master_weights
    )
    keep_mask = slot_used[:, None, None]
    fresh_master = fresh_master * keep_mask
    return (
        slot_grads * keep_mask,
        first_new * keep_mask,
        second_new * keep_mask,
        fresh_master,
        fresh_master.astype(jnp.bfloat16),
    )


def shards(
    triplane,
    cotangent,
    image_tokens,
    modulation,
    image_counts,
    owner_slots,
    master_weights,
    first_moment,
    second_moment,
    left_basis,
    right_basis,
):
    img_size = lax.axis_size("img")
    rows_size = lax.axis_size("rows")
    flat_index = lax.axis_index("rows") * img_size + lax.axis_index("img")
    object_index = flat_index // 2
    pair_index = lax.axis_index("img") // 2
    tok_rows = triplane.shape[0]
    slot_cap = image_tokens.shape[0] // (img_size // 2)
    own_count = master_weights.shape[0]
    gathered_weights = lax.all_gather(
        master_weights.astype(jnp.bfloat16), ("rows", "img"), axis=0, tiled=True
    )
    q_cross, k_cross, v_cross, o_cross, q_self, k_self, v_self, o_self, w_up, w_down = split_blocks(
        gathered_weights[owner_slots]
    )
    shifts = lax.dynamic_index_in_dim(modulation, object_index, 0, keepdims=False)
    count_here = lax.dynamic_index_in_dim(image_counts, object_index, 0, keepdims=False)
    kv_weight = jnp.concatenate([k_cross, v_cross], 1)
    kv_local = project(image_tokens, kv_weight).astype(jnp.bfloat16)
    gathered = lax.all_gather(kv_local, "img", axis=0, tiled=True).reshape(
        img_size, img_size // 2, slot_cap, 2 * D
    )
    kv_object = lax.dynamic_index_in_dim(gathered, pair_index, 1, keepdims=False)
    kv_object = kv_object.reshape(img_size * slot_cap, 2 * D)
    key_slot = jnp.arange(img_size * slot_cap, dtype=jnp.int32)
    token_index = key_slot % slot_cap * img_size + key_slot // slot_cap
    key_valid = token_index < count_here
    residual = triplane.astype(jnp.float32)
    normed_one = modulated_norm(residual, shifts[0], shifts[1]).astype(jnp.bfloat16)
    cross_queries = project(normed_one, q_cross).astype(jnp.bfloat16)
    cross_out, cross_logsum = attend(cross_queries, kv_object[:, :D], kv_object[:, D:], key_valid)
    after_cross = residual + project(cross_out, o_cross)
    normed_two = modulated_norm(after_cross, shifts[2], shifts[3]).astype(jnp.bfloat16)
    qkv_weight = jnp.concatenate([q_self, k_self, v_self], 1)
    self_proj = project(normed_two, qkv_weight).astype(jnp.bfloat16)
    kv_mine = self_proj[:, D:]
    kv_partner = partner(kv_mine, "img", 0)
    kv_all = jnp.concatenate([kv_mine, kv_partner], 0)
    all_valid = jnp.ones((2 * tok_rows,), dtype=jnp.bool_)
    self_out, self_logsum = attend(self_proj[:, :D], kv_all[:, :D], kv_all[:, D:], all_valid)
    after_self = after_cross + project(self_out, o_self)
    normed_three = modulated_norm(after_self, shifts[4], shifts[5]).astype(jnp.bfloat16)
    hidden = project(normed_three, w_up)
    activated = jax.nn.gelu(hidden).astype(jnp.bfloat16)
    result = (after_self + project(activated, w_down)).astype(jnp.bfloat16)
    grad_out = cotangent.astype(jnp.float32)
    grad_low = grad_out.astype(jnp.bfloat16)
    grad_down = project(activated.T, grad_low)
    grad_act = project(grad_low, w_down.T)
    unused_act, gelu_back = jax.vjp(jax.nn.gelu, hidden)
    grad_hidden = gelu_back(grad_act)[0].astype(jnp.bfloat16)
    grad_up = project(normed_three.T, grad_hidden)
    grad_after_self = grad_out + norm_back(
        after_self, shifts[4], shifts[5], project(grad_hidden, w_up.T)
    )
    grad_self_branch = grad_after_self.astype(jnp.bfloat16)
    grad_o_self = project(self_out.T, grad_self_branch)
    grad_self_out = project(grad_self_branch, o_self.T).astype(jnp.bfloat16)
    grad_sq, grad_sk, grad_sv = attend_back(
        self_proj[:, :D], kv_all[:, :D], kv_all[:, D:], all_valid, self_logsum, grad_self_out
    )
    grad_kv_rows = jnp.concatenate([grad_sk, grad_sv], 1)
    grad_kv_mine = grad_kv_rows[:tok_rows] + partner(
        grad_kv_rows[tok_rows:].astype(jnp.bfloat16), "img", 0
    ).astype(jnp.float32)
    grad_qkv = jnp.concatenate([grad_sq, grad_kv_mine], 1).astype(jnp.bfloat16)
    grad_qkv_weight = project(normed_two.T, grad_qkv)
    grad_after_cross = grad_after_self + norm_back(
        after_cross, shifts[2], shifts[3], project(grad_qkv, qkv_weight.T)
    )
    grad_cross_branch = grad_after_cross.astype(jnp.bfloat16)
    grad_o_cross = project(cross_out.T, grad_cross_branch)
    grad_cross_out = project(grad_cross_branch, o_cross.T).astype(jnp.bfloat16)
    grad_cq, grad_ck, grad_cv = attend_back(
        cross_queries, kv_object[:, :D], kv_object[:, D:], key_valid, cross_logsum, grad_cross_out
    )
    grad_object = jnp.concatenate([grad_ck, grad_cv], 1)
    pick_pair = (jnp.arange(img_size // 2, dtype=jnp.int32) == pair_index).astype(jnp.float32)
    spread = grad_object.reshape(img_size, 1, slot_cap, 2 * D) * pick_pair[None, :, None, None]
    grad_kv_local = lax.psum_scatter(
        spread.reshape(img_size * (img_size // 2) * slot_cap, 2 * D).astype(jnp.bfloat16),
        "img",
        scatter_dimension=0,
        tiled=True,
    )
    grad_kv_weight = project(image_tokens.T, grad_kv_local)
    grad_image = project(grad_kv_local, kv_weight.T)
    grad_cq_low = grad_cq.astype(jnp.bfloat16)
    grad_q_cross = project(normed_one.T, grad_cq_low)
    grad_triplane = grad_after_cross + norm_back(
        residual, shifts[0], shifts[1], project(grad_cq_low, q_cross.T)
    )
    weight_list = [
        grad_q_cross,
        grad_kv_weight[:, :D],
        grad_kv_weight[:, D:],
        grad_o_cross,
        grad_qkv_weight[:, :D],
        grad_qkv_weight[:, D : 2 * D],
        grad_qkv_weight[:, 2 * D :],
        grad_o_self,
        grad_up,
        grad_down,
    ]
    slot_total = rows_size * img_size * own_count
    block_grads = join_blocks(weight_list)
    placed = jnp.zeros((slot_total, BLOCK, BLOCK), jnp.float32).at[owner_slots].set(block_grads)
    slot_grads = lax.psum_scatter(placed, ("rows", "img"), scatter_dimension=0, tiled=True)
    my_slots = flat_index * own_count + jnp.arange(own_count, dtype=jnp.int32)
    matched = (owner_slots[:, None] == my_slots[None, :]).astype(jnp.float32)
    slot_used = jnp.sum(matched, axis=0)
    slot_rates = jnp.sum(matched * jnp.asarray(block_table(weight_scales()))[:, None], axis=0)
    updated = soap_update(
        slot_grads,
        first_moment,
        second_moment,
        left_basis,
        right_basis,
        master_weights,
        slot_rates,
        slot_used,
    )
    return (
        result,
        grad_triplane,
        grad_image,
        updated[0],
        updated[1],
        updated[2],
        updated[3],
        updated[4],
    )


def solution(mesh):
    in_specs = (
        P(("rows", "img"), None),
        P(("rows", "img"), None),
        P(("rows", "img"), None),
        P(),
        P(),
        P(),
        P(("rows", "img"), None, None),
        P(("rows", "img"), None, None),
        P(("rows", "img"), None, None),
        P(("rows", "img"), None, None),
        P(("rows", "img"), None, None),
    )
    out_specs = (
        P(("rows", "img"), None),
        P(("rows", "img"), None),
        P(("rows", "img"), None),
        P(("rows", "img"), None, None),
        P(("rows", "img"), None, None),
        P(("rows", "img"), None, None),
        P(("rows", "img"), None, None),
        P(("rows", "img"), None, None),
    )
    return jax.shard_map(shards, mesh=mesh, in_specs=in_specs, out_specs=out_specs, check_vma=False)
```

profile of v0, /device:TPU:0, one launch (start us, length us, event | category | flops | bytes accessed | tf_op | source)
XLA Modules:
  0.0 2713.7 jit_solution(6230967696633828902)
XLA Ops:
  10.7 198.5 %all-gather.3.cloned.1.call-done = bf16[256,256,256]{2,1,0:T(8,128)(2,1)} async-done(((bf16[8,256,256]{2,1,0:T(8,128)(2,1)}), bf16[256,256,256]{2,1,0:T(8,128)(2,1)}) %all-gather.3.cloned.1.call-update) | async-done | bytes 33554448 | tf_op jit(solution)/shard_map/all_gather | solution.py:215
  209.3 22.5 gather_fusion
  245.1 8.2 fusion.169
  274.7 14.8 copy.139
  322.7 71.4 %while.56 = (s32[]{:T(128)}, bf16[16,384,64]{1,2,0:T(8,128)(2,1)}, f32[16,384]{1,0:T(8,128)S(1)}, bf16[16,384,64]{2,1,0:T(8,128)(2,1)}, bf16[16,1040,64]{2,1,0:T...) while((s32[]{:T(128)}, bf16[16,384,64]{1,2,0:T(8,128)(2,1)}, ...), condition=%wide.region_5.6_spmd.clone, body=%wide.region_2.5_spmd.clone.sunk | while | flops 105446256 | bytes 5544077 | solution.py:121
  405.7 11.6 fusion.168
  417.3 11.5 copy.153
  428.9 12.3 copy.205
  441.2 15.1 copy.154
  456.3 12.5 copy.206
  493.3 52.2 %while.54 = (s32[]{:T(128)}, bf16[16,384,64]{1,2,0:T(8,128)(2,1)S(1)}, f32[16,384]{1,0:T(8,128)S(1)}, bf16[16,384,64]{2,1,0:T(8,128)(2,1)}, bf16[16,768,64]{2,1,...) while((s32[]{:T(128)}, bf16[16,384,64]{1,2,0:T(8,128)(2,1)S(1)}, ...), condition=%wide.region_11.12_spmd, body=%wide.region_8.11_spmd.sunk | while | flops 77561472 | bytes 4150369 | solution.py:121
  549.3 9.7 fusion.162
  559.0 8.6 fusion.114
  576.4 125.2 %while.55 = (s32[]{:T(128)}, bf16[16,384,64]{1,2,0:T(8,128)(2,1)S(1)}, f32[16,768,64]{1,2,0:T(8,128)}, f32[16,768,64]{1,2,0:T(8,128)}, bf16[16,384,64]{2,1,0:T(8...) while((s32[]{:T(128)}, ...), condition=%wide.region_18.19_spmd, body=%wide.region_16.18_spmd.sunk | while | flops 191176320 | bytes 10236529 | solution.py:143
  706.8 34.6 %collective-permute-done.1 = bf16[384,2048]{0,1:T(8,128)(2,1)} collective-permute-done((bf16[384,2048]{0,1:T(8,128)(2,1)}, bf16[384,2048]{0,1:T(8,128)(2,1)}, u32[]{:S(2)}, u32[]{:S(2)}) %collective-permute-start.1) | collective-permute-done | bytes 1572896 | tf_op jit(solution)/shard_map/ppermute | solution.py:28
  756.7 145.3 %while.57 = (s32[]{:T(128)}, bf16[16,384,64]{1,2,0:T(8,128)(2,1)S(1)}, f32[16,1040,64]{1,2,0:T(8,128)}, f32[16,1040,64]{1,2,0:T(8,128)}, bf16[16,384,64]{2,1,0:T...) while((s32[]{:T(128)}, ...), condition=%wide.region_23.24_spmd.clone, body=%wide.region_21.23_spmd.clone.sunk | while | flops 259290992 | bytes 13777565 | solution.py:143
  902.0 7.0 fusion.107
  909.0 6.6 copy.193
  917.9 13.7 fusion.163
  931.6 20.7 reshape.427
  952.3 14.2 copy.177
  971.3 10.2 copy.207
  981.5 6.8 bitcast_bitcast_fusion
  988.3 11.9 copy.176
  1014.0 10.4 fusion.140
  1024.4 10.1 fusion.171
  1129.5 8.6 constant_dynamic-update-slice_fusion.6
  1140.3 6.4 constant_dynamic-update-slice_fusion.5
  1146.7 21.2 broadcast_in_dim.128
  1167.9 115.6 %scatter_fusion = f32[256,256,256]{2,1,0:T(8,128)} fusion(f32[256,256,256]{2,1,0:T(8,128)} %broadcast_in_dim.128, s32[248]{0:T(256)S(1)} %copy-done.59, f32[248,256,256]{2,1,0:T(8,128)} %constant_dynamic-update-slice_fusion.5), kind=kCustom, calls=%fused_computation.1 | custom fusion | bytes 195036128 | tf_op jit(solution)/shard_map/scatter | solution.py:312
  1284.4 10.6 add_convert_fusion
  1298.1 1389.2 %reduce-scatter.5.cloned.1.call-done = f32[8,256,256]{2,1,0:T(8,128)} async-done(((f32[256,256,256]{2,1,0:T(8,128)}), f32[8,256,256]{2,1,0:T(8,128)}) %reduce-scatter.5.cloned.1.call-update) | async-done | bytes 2097168 | tf_op jit(solution)/shard_map/reduce_scatter | solution.py:313
  (748 shorter events, 672.9 us)
Async XLA Ops:
  7.2 2686.0 %copy-start = (f32[8,256,256]{2,1,0:T(8,128)S(1)}, f32[8,256,256]{2,1,0:T(8,128)}, u32[]{:S(2)}) copy-start(f32[8,256,256]{2,1,0:T(8,128)} %param.30) | copy-start | bytes 6291460
  7.2 202.1 %all-gather.3.cloned.1.call-start = ((), (), s32[]{:S(2)}) async-start(), calls=%async_computation.2 | async-start | bytes 34603008 | tf_op jit(solution)/shard_map/all_gather | solution.py:215
  10.1 288.1 %all-gather.5.cloned.1.call-start = ((), (), s32[]{:S(2)}) async-start(), calls=%async_computation.3 | async-start | bytes 6389760 | tf_op jit(solution)/shard_map/all_gather | solution.py:225
  242.3 831.4 %reduce-scatter.7.cloned.1.call-start = ((), (), s32[]{:S(2)}) async-start(), calls=%async_computation.5 | async-start | bytes 6389760
  244.5 24.7 copy-start.54
  244.5 24.7 copy-start.56
  244.5 152.9 %copy-start.46 = (f32[1,1,1024]{2,0,1:T(1,128)}, f32[1,1,1024]{2,0,1:T(1,128)S(1)}, u32[]{:S(2)}) copy-start(f32[1,1,1024]{2,0,1:T(1,128)S(1)} %get-tuple-element.432) | copy-start | bytes 12292
  244.7 24.5 copy-start.48
  245.0 24.1 copy-start.50
  405.4 70.4 %collective-permute-start = (bf16[384,2048]{1,0:T(8,128)(2,1)}, bf16[384,2048]{1,0:T(8,128)(2,1)}, u32[]{:S(2)}, u32[]{:S(2)}) collective-permute-start(bf16[384,2048]{1,0:T(8,128)(2,1)} %slice.143), channel_id=1, source_target_pairs={{0,1},{1,0},{2,3},{3,2},{4,5},{5,4},{6,7},{7,6},{8,9},{9,8},{10,11... | collective-permute-start | bytes 4718600 | tf_op jit(solution)/shard_map/ppermute | solution.py:28
  456.3 12.5 copy-start.20
  548.9 22.4 copy-start.5
  548.9 10.0 slice-start.8
  549.2 9.7 slice-start.9
  549.2 9.7 copy-start.34
  549.3 18.3 slice-start.10
  701.6 42.5 %copy-start.28 = (bf16[16,384,64]{1,2,0:T(8,128)(2,1)}, bf16[16,384,64]{1,2,0:T(8,128)(2,1)S(1)}, u32[]{:S(2)}) copy-start(bf16[16,384,64]{1,2,0:T(8,128)(2,1)S(1)} %get-tuple-element.185) | copy-start | bytes 2359300
  705.1 36.3 %collective-permute-start.1 = (bf16[384,2048]{0,1:T(8,128)(2,1)}, bf16[384,2048]{0,1:T(8,128)(2,1)}, u32[]{:S(2)}, u32[]{:S(2)}) collective-permute-start(bf16[384,2048]{0,1:T(8,128)(2,1)} %fusion.121), channel_id=1, source_target_pairs={{0,1},{1,0},{2,3},{3,2},{4,5},{5,4},{6,7},{7,6},{8,9},{9,8},{10,11... | collective-permute-start | bytes 4718600 | tf_op jit(solution)/shard_map/ppermute | solution.py:28
  706.8 37.3 %copy-start.2 = (f32[384,1024]{1,0:T(8,128)S(1)}, f32[384,1024]{1,0:T(8,128)}, u32[]{:S(2)}) copy-start(f32[384,1024]{1,0:T(8,128)} %copy-done.1) | copy-start | bytes 4718596
  915.6 1771.6 %reduce-scatter.5.cloned.1.call-start = ((), (), s32[]{:S(2)}) async-start(), calls=%async_computation.4 | async-start | bytes 69206016 | tf_op jit(solution)/shard_map/reduce_scatter | solution.py:313
  952.3 14.3 copy-start.6
  952.3 14.3 copy-start.30
  988.3 11.9 copy-start.17
  988.3 11.9 copy-start.37
  1111.2 18.2 slice-start.4
  1114.9 14.5 slice-start.5
  1118.9 10.5 slice-start.6
  1126.9 11.2 slice-start
  1129.5 10.8 slice-start.3
  1146.7 21.2 copy-start.59
  1284.4 10.6 copy-start.45
  1284.4 10.6 copy-start.63
  (54 other events, 194.3 us)
Sparse Core Ops, SparseCore 0:
  11.7 197.4 all-gather.2
  242.5 55.6 all-gather.4
  915.7 55.9 reduce-scatter.6
  1283.7 1403.5 reduce-scatter.4
where the time goes:
time: 2730 us; the launch traced here: 2710 us
  waiting for transfers between devices  1620 us (59%)
  local copies, waits for them, and re-layouts  529 us (19%)
  matrix products  477 us (17%)
  other arithmetic  65 us (2%)
    reduce_scatter x1, waiting for transfers between devices, shards(): lax.psum_scatter(placed, ('rows', 'img'), scatter_dimension=0, tiled=True)  1390 us
    dot_general x245, matrix products, project(): return jnp.dot(left, right, preferred_element_type=jnp.float32)  457 us
    all_gather x1, waiting for transfers between devices, shards(): lax.all_gather(master_weights.astype(jnp.bfloat16), ('rows', 'img'), axis...  199 us
    unnamed x185, local copies, waits for them, and re-layouts  132 us
    scatter x1, local copies, waits for them, and re-layouts, shards(): jnp.zeros((slot_total, BLOCK, BLOCK), jnp.float32).at[owner_slots]  116 us
  transfers between devices with their start and end apart: 6, of which 4 were waited for; matrix products, arithmetic and copies ran while one was open for 11% of the time, Pallas kernels for 0%

commit v1 on v0

--- a/solution.py
+++ b/solution.py
@@ -1,7 +1,11 @@
+import functools
+
 import jax
 import jax.numpy as jnp
 import numpy as np
 from jax import lax
+from jax.experimental import pallas as pl
+from jax.experimental.pallas import tpu as pltpu
 from jax.sharding import PartitionSpec as P
 
 D = 1024
@@ -12,6 +16,140 @@
 IMG_MAX = 1025
 BLOCK = 256
 STEP = 5
+
+
+MESH=pl.DeviceIdType.MESH
+VLIM=60*1024*1024
+
+def coords():
+    r = lax.axis_index("rows"); y = lax.axis_index("img")
+    z = lax.div(r, 4); rest = lax.rem(r, 4)
+    return z, lax.div(rest, 2), lax.rem(rest, 2), y
+
+def neighbour(kind):
+    z, x, c, y = coords()
+    if kind == "c": c = 1 - c
+    if kind == "x": x = 1 - x
+    if kind == "y": y = 1 - y
+    if kind == "lo": z = z + 1 - 2 * lax.rem(z, 2)
+    if kind == "hi": z = lax.rem(z + 2, 4)
+    return (z * 4 + x * 2 + c, y)
+
+def place(j):
+    z, x, c, y = coords()
+    lo = lax.rem(z, 2); hi = lax.div(z, 2)
+    if j % 2 == 0: return ((x * 2 + lo) * 2 + y) * 2 + hi
+    return ((y * 2 + lo) * 2 + x) * 2 + hi
+
+WAYS = (("hi", "y", "lo", "x", "c"), ("hi", "x", "lo", "y", "c"))
+
+def greet():
+    bar = pltpu.get_barrier_semaphore()
+    for kind in ("c", "x", "y", "lo", "hi"):
+        pl.semaphore_signal(bar, inc=1, device_id=neighbour(kind), device_id_type=MESH)
+    pl.semaphore_wait(bar, 5)
+
+def gather_kernel(order, master, out, own, f32, lsem, csem, ssem, rsem):
+    z, x, c, y = coords()
+    load = pltpu.make_async_copy(master, f32, lsem)
+    load.start()
+    greet()
+    load.wait()
+    keeps = []
+    copies = {}
+    def start(j, k):
+        base = place(j)
+        if k < 4:
+            n = 2 ** k
+            first = lax.div(base, n) * n
+        else:
+            n, first = 16, 0
+        src = own.at[pl.ds(j, 1)] if k == 0 else out.at[c, j, pl.ds(first, n)]
+        cp = pltpu.make_async_remote_copy(src, out.at[c, j, pl.ds(first, n)], ssem.at[j, k], rsem.at[j, k],
+              device_id=neighbour(WAYS[j % 2][k]), device_id_type=MESH)
+        cp.start()
+        copies[j, k] = cp
+    for j in range(8):
+        own[j] = f32[j].astype(jnp.bfloat16)
+        start(j, 0)
+        keep = pltpu.make_async_copy(own.at[pl.ds(j,1)], out.at[c, j, pl.ds(place(j), 1)], csem.at[j])
+        keep.start(); keeps.append(keep)
+    for keep in keeps: keep.wait()
+    for j, k in order:
+        copies[j, k - 1].wait_recv()
+        start(j, k)
+    for j in range(8): copies[j, 4].wait_recv()
+    for cp in copies.values(): cp.wait_send()
+
+def gather(master, order, cid=11):
+    return pl.pallas_call(functools.partial(gather_kernel, order),
+        out_shape=jax.ShapeDtypeStruct((2, 8, 16, BLOCK, BLOCK), jnp.bfloat16),
+        in_specs=[pl.BlockSpec(memory_space=pl.ANY)], out_specs=pl.BlockSpec(memory_space=pl.ANY),
+        scratch_shapes=[pltpu.VMEM((8, BLOCK, BLOCK), jnp.bfloat16), pltpu.VMEM((8, BLOCK, BLOCK), jnp.float32),
+            pltpu.SemaphoreType.DMA, pltpu.SemaphoreType.DMA((8,)), pltpu.SemaphoreType.DMA((8, 5)), pltpu.SemaphoreType.DMA((8, 5))],
+        compiler_params=pltpu.CompilerParams(collective_id=cid, has_side_effects=True, vmem_limit_bytes=VLIM))(master)
+
+def scatter_kernel(order, grads, out, own, r0, r1, r2, r3, r4, lsem, ssem, rsem):
+    z, x, c, y = coords()
+    got = (r0, r1, r2, r3, r4)
+    loads = []
+    for j in range(8):
+        load = pltpu.make_async_copy(grads.at[c, j], own.at[j], lsem.at[j])
+        load.start(); loads.append(load)
+    greet()
+    copies = {}
+    for j in range(8):
+        cp = pltpu.make_async_remote_copy(grads.at[1 - c, j], r0.at[j], ssem.at[j, 0], rsem.at[j, 0],
+              device_id=neighbour("c"), device_id_type=MESH)
+        cp.start(); copies[j, 0] = cp
+    def add(j, s):
+        n = 16 >> s
+        first = lax.div(place(j), n) * n if s else 0
+        def body(b, carry):
+            own[j, first + b] = (own[j, first + b].astype(jnp.float32) + got[s][j, b].astype(jnp.float32)).astype(jnp.bfloat16)
+            return carry
+        lax.fori_loop(0, n, body, 0)
+    def send(j, s):
+        n = 16 >> s
+        base = place(j)
+        half = lax.div(base, n)
+        other = (half + 1 - 2 * lax.rem(half, 2)) * n
+        cp = pltpu.make_async_remote_copy(own.at[j, pl.ds(other, n)], got[s].at[j], ssem.at[j, s], rsem.at[j, s],
+              device_id=neighbour(WAYS[j % 2][4 - s]), device_id_type=MESH)
+        cp.start(); copies[j, s] = cp
+    for j, s in order:
+        if s == 1: loads[j].wait()
+        copies[j, s - 1].wait_recv()
+        add(j, s - 1)
+        if s < 5: send(j, s)
+        else: out[j] = own[j, place(j)].astype(jnp.float32)
+    for cp in copies.values(): cp.wait_send()
+
+def scatter(grads, order, cid=12):
+    bf = jnp.bfloat16
+    return pl.pallas_call(functools.partial(scatter_kernel, order),
+        out_shape=jax.ShapeDtypeStruct((8, BLOCK, BLOCK), jnp.float32),
+        in_specs=[pl.BlockSpec(memory_space=pl.ANY)], out_specs=pl.BlockSpec(memory_space=pltpu.VMEM),
+        scratch_shapes=[pltpu.VMEM((8, 16, BLOCK, BLOCK), bf), pltpu.VMEM((8, 16, BLOCK, BLOCK), bf), pltpu.VMEM((8, 8, BLOCK, BLOCK), bf),
+            pltpu.VMEM((8, 4, BLOCK, BLOCK), bf), pltpu.VMEM((8, 2, BLOCK, BLOCK), bf), pltpu.VMEM((8, 1, BLOCK, BLOCK), bf),
+            pltpu.SemaphoreType.DMA((8,)), pltpu.SemaphoreType.DMA((8, 5)), pltpu.SemaphoreType.DMA((8, 5))],
+        compiler_params=pltpu.CompilerParams(collective_id=cid, has_side_effects=True, vmem_limit_bytes=VLIM))(grads)
+
+WAVE_OUT = sorted(
+    [(j, k) for k in range(1, 5) for j in range(8)], key=lambda t: (t[0] // 2 + t[1], t[1], t[0])
+)
+WAVE_IN = sorted(
+    [(j, k) for k in range(1, 6) for j in range(8)], key=lambda t: (t[0] // 2 + t[1], t[1], t[0])
+)
+
+
+def positions(slot):
+    owner = slot // 8; j = slot % 8
+    z = owner // 8; x = owner // 4 % 2; c = owner // 2 % 2; y = owner % 2
+    lo = z % 2; hi = z // 2
+    a = ((x * 2 + lo) * 2 + y) * 2 + hi
+    b = ((y * 2 + lo) * 2 + x) * 2 + hi
+    return (c * 8 + j) * 16 + jnp.where(j % 2 == 0, a, b)
 
 
 highest = lax.Precision.HIGHEST
@@ -212,11 +350,17 @@
     tok_rows = triplane.shape[0]
     slot_cap = image_tokens.shape[0] // (img_size // 2)
     own_count = master_weights.shape[0]
-    gathered_weights = lax.all_gather(
-        master_weights.astype(jnp.bfloat16), ("rows", "img"), axis=0, tiled=True
-    )
+    fits = rows_size == 16 and img_size == 2 and own_count == 8
+    if fits:
+        gathered_weights = gather(master_weights, WAVE_OUT).reshape(-1, BLOCK, BLOCK)
+        where = positions(owner_slots)
+    else:
+        gathered_weights = lax.all_gather(
+            master_weights.astype(jnp.bfloat16), ("rows", "img"), axis=0, tiled=True
+        )
+        where = owner_slots
     q_cross, k_cross, v_cross, o_cross, q_self, k_self, v_self, o_self, w_up, w_down = split_blocks(
-        gathered_weights[owner_slots]
+        gathered_weights[where]
     )
     shifts = lax.dynamic_index_in_dim(modulation, object_index, 0, keepdims=False)
     count_here = lax.dynamic_index_in_dim(image_counts, object_index, 0, keepdims=False)
@@ -308,9 +452,14 @@
         grad_down,
     ]
     slot_total = rows_size * img_size * own_count
-    block_grads = join_blocks(weight_list)
-    placed = jnp.zeros((slot_total, BLOCK, BLOCK), jnp.float32).at[owner_slots].set(block_grads)
-    slot_grads = lax.psum_scatter(placed, ("rows", "img"), scatter_dimension=0, tiled=True)
+    block_grads = join_blocks([part.astype(jnp.bfloat16) for part in weight_list])
+    placed = jnp.zeros((slot_total, BLOCK, BLOCK), jnp.bfloat16).at[where].set(block_grads)
+    if fits:
+        slot_grads = scatter(placed.reshape(2, 8, 16, BLOCK, BLOCK), WAVE_IN)
+    else:
+        slot_grads = lax.psum_scatter(
+            placed, ("rows", "img"), scatter_dimension=0, tiled=True
+        ).astype(jnp.float32)
     my_slots = flat_index * own_count + jnp.arange(own_count, dtype=jnp.int32)
     matched = (owner_slots[:, None] == my_slots[None, :]).astype(jnp.float32)
     slot_used = jnp.sum(matched, axis=0)

time: 2730 us -> 1410 us (0.52)
  waiting for transfers between devices: 1620 us -> 50.3 us
  Pallas kernels: 0 us -> 325 us
  local copies, waits for them, and re-layouts: 529 us -> 447 us
    reduce_scatter x1 -> x0, waiting for transfers between devices: 1390 us -> none  [shards(): lax.psum_scatter(placed, ('rows', 'img'), scatter_dimension=0, tiled=True)]
    pallas_call x0 -> x2, Pallas kernels: none -> 325 us  [the longest x1 164 us: gather(): pl.pallas_call(functools.partial(gather_kernel, order), out_shape=jax.Sha...]
    all_gather x1 -> x0, waiting for transfers between devices: 199 us -> none  [shards(): lax.all_gather(master_weights.astype(jnp.bfloat16), ('rows', 'img'), axis...]
    reshape x10 -> x0, local copies, waits for them, and re-layouts: 38.8 us -> none  [split_blocks(): blocks[begin_at:begin_at + amount]]
    transpose x0 -> x10, local copies, waits for them, and re-layouts: none -> 38.5 us  [split_blocks(): matrices.append(grid.transpose(0, 2, 1, 3).reshape(rows_in, cols_out))]
    scatter x1, local copies, waits for them, and re-layouts: 116 us -> 84.7 us  [shards(): jnp.zeros((slot_total, BLOCK, BLOCK), jnp.bfloat16).at[where]]
    unnamed x185 -> x167, local copies, waits for them, and re-layouts: 132 us -> 106 us
  transfers between devices with their start and end apart: 6 -> 4, of which waited for: 4 -> 2; matrix products, arithmetic and copies ran while one was open for 11% -> 19% of each run, Pallas kernels for 0% -> 0%
where the time goes in v1:
time: 1410 us; the launch traced here: 1400 us
  matrix products  494 us (35%)
  local copies, waits for them, and re-layouts  447 us (32%)
  Pallas kernels  325 us (23%)
  other arithmetic  60.5 us (4%)
  waiting for transfers between devices  50.3 us (4%)
  between operations  15.5 us (1%)
    dot_general x245, matrix products, project(): return jnp.dot(left, right, preferred_element_type=jnp.float32)  474 us
    pallas_call x1, Pallas kernels, gather(): pl.pallas_call(functools.partial(gather_kernel, order), out_shape=jax.Sha...  164 us
    pallas_call x1, Pallas kernels, scatter(): pl.pallas_call(functools.partial(scatter_kernel, order), out_shape=jax.Sh...  161 us
    unnamed x167, local copies, waits for them, and re-layouts  106 us
    scatter x1, local copies, waits for them, and re-layouts, shards(): jnp.zeros((slot_total, BLOCK, BLOCK), jnp.bfloat16).at[where]  84.7 us
    transpose x11, local copies, waits for them, and re-layouts, join_blocks(): matrix.reshape(rows_in // BLOCK, BLOCK, cols_out // BLOCK, BLOCK)  50.3 us
    reshape x9, local copies, waits for them, and re-layouts, join_blocks(): matrix.reshape(rows_in // BLOCK, BLOCK, cols_out // BLOCK, BLOCK)  49.8 us
    transpose x10, local copies, waits for them, and re-layouts, split_blocks(): matrices.append(grid.transpose(0, 2, 1, 3).reshape(rows_in, cols_out))  38.5 us
  transfers between devices with their start and end apart: 4, of which 2 were waited for; matrix products, arithmetic and copies ran while one was open for 19% of the time, Pallas kernels for 0%

profile of v1, /device:TPU:0, one launch (start us, length us, event | category | flops | bytes accessed | tf_op | source)
XLA Modules:
  0.0 1396.7 jit_solution(11738585131224530545)
XLA Ops:
  8.6 164.4 %shard_map.179 = bf16[2,8,16,256,256]{4,3,2,1,0:T(8,128)(2,1)} custom-call(f32[8,256,256]{2,1,0:T(8,128)} %master.1), custom_call_target="tpu_custom_call" | custom-call | tf_op jit(solution)/shard_map/pallas_call | solution.py:85
  173.1 22.6 %gather_fusion = bf16[248,256,256]{2,1,0:T(8,128)(2,1)} fusion(bf16[256,256,256]{2,1,0:T(8,128)(2,1)} %bitcast.376, s32[1024]{0:T(1024)S(1)} %pad_clamp_fusion), kind=kCustom, calls=%fused_computation | custom fusion | bytes 65012704 | tf_op jit(solution)/shard_map/gather | solution.py:363
  206.3 6.7 fusion.173
  249.3 15.7 %all-gather.2.cloned.1.call-done = bf16[1040,2048]{1,0:T(8,128)(2,1)} async-done(((bf16[520,2048]{1,0:T(8,128)(2,1)}), bf16[1040,2048]{1,0:T(8,128)(2,1)}) %all-gather.2.cloned.1.call-update) | async-done | bytes 4259856 | tf_op jit(solution)/shard_map/all_gather | solution.py:369
  289.7 70.8 %while.56 = (s32[]{:T(128)}, bf16[16,384,64]{1,2,0:T(8,128)(2,1)}, f32[16,384]{1,0:T(8,128)S(1)}, bf16[16,384,64]{2,1,0:T(8,128)(2,1)}, bf16[16,1040,64]{2,1,0:T...) while((s32[]{:T(128)}, bf16[16,384,64]{1,2,0:T(8,128)(2,1)}, ...), condition=%wide.region_5.6_spmd.clone, body=%wide.region_2.5_spmd.clone.sunk | while | flops 105446256 | bytes 5544077 | solution.py:259
  372.1 11.8 fusion.172
  383.9 11.5 copy.190
  395.4 12.3 copy.236
  407.7 14.9 %copy.191 = bf16[16,256,4,256]{1,0,3,2:T(8,128)(2,1)} copy(bf16[16,256,4,256]{3,1,2,0:T(8,128)(2,1)} %bitcast.383) | data formatting | bytes 16777216 | tf_op jit(solution)/shard_map/transpose | solution.py:206
  422.6 12.4 copy.237
  459.5 52.5 %while.54 = (s32[]{:T(128)}, bf16[16,384,64]{1,2,0:T(8,128)(2,1)S(1)}, f32[16,384]{1,0:T(8,128)S(1)}, bf16[16,384,64]{2,1,0:T(8,128)(2,1)}, bf16[16,768,64]{2,1,...) while((s32[]{:T(128)}, bf16[16,384,64]{1,2,0:T(8,128)(2,1)S(1)}, ...), condition=%wide.region_11.12_spmd, body=%wide.region_8.11_spmd.sunk | while | flops 77561472 | bytes 4150369 | solution.py:259
  515.7 6.8 fusion.167
  522.6 8.1 fusion.114
  544.4 134.5 %while.55 = (s32[]{:T(128)}, bf16[16,384,64]{1,2,0:T(8,128)(2,1)}, f32[16,768,64]{1,2,0:T(8,128)}, f32[16,768,64]{1,2,0:T(8,128)}, bf16[16,384,64]{2,1,0:T(8,128...) while((s32[]{:T(128)}, bf16[16,384,64]{1,2,0:T(8,128)(2,1)}, ...), condition=%wide.region_18.19_spmd, body=%wide.region_16.18_spmd.sunk | while | flops 191176320 | bytes 10236529 | solution.py:281
  683.8 34.6 %collective-permute-done.1 = bf16[384,2048]{0,1:T(8,128)(2,1)} collective-permute-done((bf16[384,2048]{0,1:T(8,128)(2,1)}, bf16[384,2048]{0,1:T(8,128)(2,1)}, u32[]{:S(2)}, u32[]{:S(2)}) %collective-permute-start.1) | collective-permute-done | bytes 1572896 | tf_op jit(solution)/shard_map/ppermute | solution.py:166
  721.2 6.2 multiply_reduce_fusion.2
  736.3 154.2 %while.57 = (s32[]{:T(128)}, bf16[16,384,64]{1,2,0:T(8,128)(2,1)}, f32[16,1040,64]{1,2,0:T(8,128)}, f32[16,1040,64]{1,2,0:T(8,128)}, bf16[16,384,64]{2,1,0:T(8,1...) while((s32[]{:T(128)}, bf16[16,384,64]{1,2,0:T(8,128)(2,1)}, ...), condition=%wide.region_23.24_spmd.clone, body=%wide.region_21.23_spmd.clone.sunk | while | flops 259290992 | bytes 13777565 | solution.py:281
  890.5 6.7 fusion.107
  897.2 6.6 copy.224
  917.0 10.4 convolution_convert_fusion
  927.4 14.7 %reshape.437 = bf16[16,256,4,256]{3,2,1,0:T(4,128)(2,1)} reshape(bf16[4096,1024]{1,0:T(8,128)(2,1)} %convolution_convert_fusion) | data formatting | bytes 16777216 | tf_op jit(solution)/shard_map/reshape | solution.py:215
  942.1 8.5 copy.214
  950.7 9.3 convolution_convert_fusion.1
  960.0 9.7 copy.238
  969.7 7.2 bitcast_bitcast_fusion
  976.9 10.0 copy.213
  986.9 10.2 add_convert_fusion
  1095.0 7.6 constant_dynamic-update-slice_fusion.6
  1102.6 7.6 constant_dynamic-update-slice_fusion.5
  1110.2 10.9 broadcast_in_dim.128
  1121.2 84.7 %scatter_fusion = bf16[256,256,256]{2,1,0:T(8,128)(2,1)} fusion(bf16[256,256,256]{2,1,0:T(8,128)(2,1)} %broadcast_in_dim.128, s32[248]{0:T(256)S(1)} %copy-done.51, bf16[248,256,256]{2,1,0:T(8,128)(2,1)} %constant_dynamic-update-slice_fusion.5), kind=kCustom, calls=%fused_computation.1 | custom fusion | bytes 97518560 | tf_op jit(solution)/shard_map/scatter | solution.py:456
  1205.8 160.6 %shard_map.180 = f32[8,256,256]{2,1,0:T(8,128)} custom-call(bf16[2,8,16,256,256]{4,3,2,1,0:T(8,128)(2,1)} %bitcast.375), custom_call_target="tpu_custom_call" | custom-call | tf_op jit(solution)/shard_map/pallas_call | solution.py:130
  (726 shorter events, 685.9 us)
Async XLA Ops:
  7.2 1365.2 %copy-start = (f32[8,256,256]{2,1,0:T(8,128)S(1)}, f32[8,256,256]{2,1,0:T(8,128)}, u32[]{:S(2)}) copy-start(f32[8,256,256]{2,1,0:T(8,128)} %param.30) | copy-start | bytes 6291460
  7.2 257.8 %all-gather.2.cloned.1.call-start = ((), (), s32[]{:S(2)}) async-start(), calls=%async_computation.1 | async-start | bytes 6389760 | tf_op jit(solution)/shard_map/all_gather | solution.py:369
  206.2 851.1 %reduce-scatter.4.cloned.1.call-start = ((), (), s32[]{:S(2)}) async-start(), calls=%async_computation.2 | async-start | bytes 6389760
  231.6 5.7 copy-start.57
  231.7 132.1 %copy-start.55 = (f32[1,1,1024]{2,0,1:T(1,128)}, f32[1,1,1024]{2,0,1:T(1,128)S(1)}, u32[]{:S(2)}) copy-start(f32[1,1,1024]{2,0,1:T(1,128)S(1)} %get-tuple-element.460) | copy-start | bytes 12292
  363.4 6.4 copy-start.1
  371.8 70.3 %collective-permute-start = (bf16[384,2048]{1,0:T(8,128)(2,1)}, bf16[384,2048]{1,0:T(8,128)(2,1)}, u32[]{:S(2)}, u32[]{:S(2)}) collective-permute-start(bf16[384,2048]{1,0:T(8,128)(2,1)} %slice.148), channel_id=1, source_target_pairs={{0,1},{1,0},{2,3},{3,2},{4,5},{5,4},{6,7},{7,6},{8,9},{9,8},{10,11... | collective-permute-start | bytes 4718600 | tf_op jit(solution)/shard_map/ppermute | solution.py:166
  422.5 12.5 copy-start.16
  515.4 20.9 %copy-start.7 = (f32[384,1024]{1,0:T(8,128)}, f32[384,1024]{1,0:T(8,128)S(1)}, u32[]{:S(2)}) copy-start(f32[384,1024]{1,0:T(8,128)S(1)} %get-tuple-element.469) | copy-start | bytes 4718596
  515.4 7.1 slice-start
  515.7 6.8 slice-start.1
  515.7 6.8 copy-start.28
  515.7 15.0 %slice-start.2 = ((s8[8388608]{0:T(1024)(128)(4,1)}), s8[4194304]{0:T(1024)(128)(4,1)S(1)}, s32[]{:S(2)}) async-start(s8[8388608]{0:T(1024)(128)(4,1)} %bitcast.404), calls=%async_computation.5 | async-start | bytes 8388608
  522.5 8.2 copy-start.65
  522.5 8.1 slice-start.3
  682.1 36.3 %collective-permute-start.1 = (bf16[384,2048]{0,1:T(8,128)(2,1)}, bf16[384,2048]{0,1:T(8,128)(2,1)}, u32[]{:S(2)}, u32[]{:S(2)}) collective-permute-start(bf16[384,2048]{0,1:T(8,128)(2,1)} %fusion.121), channel_id=1, source_target_pairs={{0,1},{1,0},{2,3},{3,2},{4,5},{5,4},{6,7},{7,6},{8,9},{9,8},{10,11... | collective-permute-start | bytes 4718600 | tf_op jit(solution)/shard_map/ppermute | solution.py:166
  683.8 37.4 %copy-start.2 = (f32[384,1024]{1,0:T(8,128)S(1)}, f32[384,1024]{1,0:T(8,128)}, u32[]{:S(2)}) copy-start(f32[384,1024]{1,0:T(8,128)} %copy-done.1) | copy-start | bytes 4718596
  683.8 37.4 %copy-start.41 = (bf16[16,384,64]{1,2,0:T(8,128)(2,1)S(1)}, bf16[16,384,64]{1,2,0:T(8,128)(2,1)}, u32[]{:S(2)}) copy-start(bf16[16,384,64]{1,2,0:T(8,128)(2,1)} %get-tuple-element.185) | copy-start | bytes 2359300
  721.2 6.3 copy-start.35
  942.1 8.5 copy-start.8
  986.9 10.2 copy-start.10
  986.9 10.2 copy-start.26
  1110.2 11.0 copy-start.51
  1366.5 5.9 copy-start.6
  1366.5 5.9 copy-start.33
  1366.5 5.9 copy-start.34
  1366.5 5.9 copy-start.52
  1372.5 5.5 copy-start.31
  1378.0 3.8 copy-start.14
  1378.0 3.8 copy-start.60
  1381.8 4.5 copy-start.38
  1381.8 4.5 copy-start.62
  (43 other events, 94.6 us)
Sparse Core Ops, SparseCore 0:
  206.3 58.6 all-gather.1
  904.0 55.9 reduce-scatter.3

commit v2 on v1

v2 whole, which is shorter than its diff:
```python
import functools

import jax
import jax.numpy as jnp
import numpy as np
from jax import lax
from jax.experimental import pallas as pl
from jax.experimental.pallas import tpu as pltpu
from jax.sharding import PartitionSpec as P

D = 1024
HEADS = 16
FF = 4096
DIMG = 768
TOK_DEV = 384
IMG_MAX = 1025
BLOCK = 256
STEP = 5
HEAD = D // HEADS

MESH=pl.DeviceIdType.MESH
VLIM=60*1024*1024

def coords():
    r = lax.axis_index("rows"); y = lax.axis_index("img")
    z = lax.div(r, 4); rest = lax.rem(r, 4)
    return z, lax.div(rest, 2), lax.rem(rest, 2), y

def neighbour(kind):
    z, x, c, y = coords()
    if kind == "c": c = 1 - c
    if kind == "x": x = 1 - x
    if kind == "y": y = 1 - y
    if kind == "lo": z = z + 1 - 2 * lax.rem(z, 2)
    if kind == "hi": z = lax.rem(z + 2, 4)
    return (z * 4 + x * 2 + c, y)

def place(j):
    z, x, c, y = coords()
    lo = lax.rem(z, 2); hi = lax.div(z, 2)
    if j % 2 == 0: return ((x * 2 + lo) * 2 + y) * 2 + hi
    return ((y * 2 + lo) * 2 + x) * 2 + hi

WAYS = (("hi", "y", "lo", "x", "c"), ("hi", "x", "lo", "y", "c"))

def greet():
    bar = pltpu.get_barrier_semaphore()
    for kind in ("c", "x", "y", "lo", "hi"):
        pl.semaphore_signal(bar, inc=1, device_id=neighbour(kind), device_id_type=MESH)
    pl.semaphore_wait(bar, 5)

def gather_kernel(order, master, out, own, f32, lsem, csem, ssem, rsem):
    z, x, c, y = coords()
    load = pltpu.make_async_copy(master, f32, lsem)
    load.start()
    greet()
    load.wait()
    keeps = []
    copies = {}
    def start(j, k):
        base = place(j)
        if k < 4:
            n = 2 ** k
            first = lax.div(base, n) * n
        else:
            n, first = 16, 0
        src = own.at[pl.ds(j, 1)] if k == 0 else out.at[c, j, pl.ds(first, n)]
        cp = pltpu.make_async_remote_copy(src, out.at[c, j, pl.ds(first, n)], ssem.at[j, k], rsem.at[j, k],
              device_id=neighbour(WAYS[j % 2][k]), device_id_type=MESH)
        cp.start()
        copies[j, k] = cp
    for j in range(8):
        own[j] = f32[j].astype(jnp.bfloat16)
        start(j, 0)
        keep = pltpu.make_async_copy(own.at[pl.ds(j,1)], out.at[c, j, pl.ds(place(j), 1)], csem.at[j])
        keep.start(); keeps.append(keep)
    for keep in keeps: keep.wait()
    for j, k in order:
        copies[j, k - 1].wait_recv()
        start(j, k)
    for j in range(8): copies[j, 4].wait_recv()
    for cp in copies.values(): cp.wait_send()

def gather(master, order, cid=11):
    return pl.pallas_call(functools.partial(gather_kernel, order),
        out_shape=jax.ShapeDtypeStruct((2, 8, 16, BLOCK, BLOCK), jnp.bfloat16),
        in_specs=[pl.BlockSpec(memory_space=pl.ANY)], out_specs=pl.BlockSpec(memory_space=pl.ANY),
        scratch_shapes=[pltpu.VMEM((8, BLOCK, BLOCK), jnp.bfloat16), pltpu.VMEM((8, BLOCK, BLOCK), jnp.float32),
            pltpu.SemaphoreType.DMA, pltpu.SemaphoreType.DMA((8,)), pltpu.SemaphoreType.DMA((8, 5)), pltpu.SemaphoreType.DMA((8, 5))],
        compiler_params=pltpu.CompilerParams(collective_id=cid, has_side_effects=True, vmem_limit_bytes=VLIM))(master)

def scatter_kernel(order, grads, out, own, r0, r1, r2, r3, r4, lsem, ssem, rsem):
    z, x, c, y = coords()
    got = (r0, r1, r2, r3, r4)
    loads = []
    for j in range(8):
        load = pltpu.make_async_copy(grads.at[c, j], own.at[j], lsem.at[j])
        load.start(); loads.append(load)
    greet()
    copies = {}
    for j in range(8):
        cp = pltpu.make_async_remote_copy(grads.at[1 - c, j], r0.at[j], ssem.at[j, 0], rsem.at[j, 0],
              device_id=neighbour("c"), device_id_type=MESH)
        cp.start(); copies[j, 0] = cp
    def add(j, s):
        n = 16 >> s
        first = lax.div(place(j), n) * n if s else 0
        def body(b, carry):
            own[j, first + b] = (own[j, first + b].astype(jnp.float32) + got[s][j, b].astype(jnp.float32)).astype(jnp.bfloat16)
            return carry
        lax.fori_loop(0, n, body, 0)
    def send(j, s):
        n = 16 >> s
        base = place(j)
        half = lax.div(base, n)
        other = (half + 1 - 2 * lax.rem(half, 2)) * n
        cp = pltpu.make_async_remote_copy(own.at[j, pl.ds(other, n)], got[s].at[j], ssem.at[j, s], rsem.at[j, s],
              device_id=neighbour(WAYS[j % 2][4 - s]), device_id_type=MESH)
        cp.start(); copies[j, s] = cp
    for j, s in order:
        if s == 1: loads[j].wait()
        copies[j, s - 1].wait_recv()
        add(j, s - 1)
        if s < 5: send(j, s)
        else: out[j] = own[j, place(j)].astype(jnp.float32)
    for cp in copies.values(): cp.wait_send()

def scatter(grads, order, cid=12):
    bf = jnp.bfloat16
    return pl.pallas_call(functools.partial(scatter_kernel, order),
        out_shape=jax.ShapeDtypeStruct((8, BLOCK, BLOCK), jnp.float32),
        in_specs=[pl.BlockSpec(memory_space=pl.ANY)], out_specs=pl.BlockSpec(memory_space=pltpu.VMEM),
        scratch_shapes=[pltpu.VMEM((8, 16, BLOCK, BLOCK), bf), pltpu.VMEM((8, 16, BLOCK, BLOCK), bf), pltpu.VMEM((8, 8, BLOCK, BLOCK), bf),
            pltpu.VMEM((8, 4, BLOCK, BLOCK), bf), pltpu.VMEM((8, 2, BLOCK, BLOCK), bf), pltpu.VMEM((8, 1, BLOCK, BLOCK), bf),
            pltpu.SemaphoreType.DMA((8,)), pltpu.SemaphoreType.DMA((8, 5)), pltpu.SemaphoreType.DMA((8, 5))],
        compiler_params=pltpu.CompilerParams(collective_id=cid, has_side_effects=True, vmem_limit_bytes=VLIM))(grads)

def positions(slot):
    owner = slot // 8; j = slot % 8
    z = owner // 8; x = owner // 4 % 2; c = owner // 2 % 2; y = owner % 2
    lo = z % 2; hi = z // 2
    a = ((x * 2 + lo) * 2 + y) * 2 + hi
    b = ((y * 2 + lo) * 2 + x) * 2 + hi
    return (c * 8 + j) * 16 + jnp.where(j % 2 == 0, a, b)


highest = lax.Precision.HIGHEST
moment_decay = 0.5
LOW = jnp.bfloat16
WIDE = jnp.float32

WAVE_OUT = sorted(
    [(j, k) for k in range(1, 5) for j in range(8)], key=lambda t: (t[0] // 2 + t[1], t[1], t[0])
)
WAVE_IN = sorted(
    [(j, k) for k in range(1, 6) for j in range(8)], key=lambda t: (t[0] // 2 + t[1], t[1], t[0])
)


def shapes_list():
    return [(D, D), (DIMG, D), (DIMG, D), (D, D), (D, D), (D, D), (D, D), (D, D), (D, FF), (FF, D)]


Q_CROSS, K_CROSS, V_CROSS, O_CROSS, Q_SELF, K_SELF, V_SELF, O_SELF, W_UP, W_DOWN = (
    int(v) for v in np.cumsum([0] + [a * b // BLOCK**2 for a, b in shapes_list()])[:10]
)


def weight_scales():
    self_root = (2.0 * TOK_DEV) ** 0.5
    cross_root = (IMG_MAX / 2.0) ** 0.5
    return [
        D ** (-0.5),
        DIMG ** (-0.5),
        DIMG ** (-0.5),
        0.5 * cross_root * D ** (-0.5),
        D ** (-0.5),
        D ** (-0.5),
        D ** (-0.5),
        0.5 * self_root * D ** (-0.5),
        D ** (-0.5),
        2.0 * FF ** (-0.5),
    ]


def block_table(scales):
    pieces = []
    for shape_pair, scale_value in zip(shapes_list(), scales):
        amount = shape_pair[0] * shape_pair[1] // (BLOCK * BLOCK)
        pieces.append(np.full((amount,), scale_value, np.float32))
    return np.concatenate(pieces)


def low(v):
    return v.astype(LOW)


def dot(a, b):
    return jnp.dot(a, b, preferred_element_type=WIDE)


def dot_nt(a, b):
    return lax.dot_general(a, b, (((1,), (1,)), ((), ())), preferred_element_type=WIDE)


def part(k):
    return slice(k * BLOCK, (k + 1) * BLOCK)


def norm_parts(values):
    centered = values - jnp.mean(values, axis=-1, keepdims=True)
    variance = jnp.mean(centered * centered, axis=-1, keepdims=True)
    return centered, lax.rsqrt(variance + 1e-06)


def modulated_norm(values, shift, scale):
    centered, inverse = norm_parts(values)
    return centered * inverse * (1.0 + scale) + shift


def norm_back(values, scale, grad_normed):
    centered, inverse = norm_parts(values)
    unit = centered * inverse
    grad_unit = grad_normed * (1.0 + scale)
    return inverse * (
        grad_unit
        - jnp.mean(grad_unit, axis=-1, keepdims=True)
        - unit * jnp.mean(grad_unit * unit, axis=-1, keepdims=True)
    )


def halves(pair):
    lane = lax.broadcasted_iota(jnp.int32, pair.shape, 1)
    zero = jnp.zeros_like(pair)
    return jnp.where(lane < HEAD, pair, zero), jnp.where(lane < HEAD, zero, pair)


def masked(scores, valid):
    if valid is None:
        return scores
    wide = jnp.concatenate([valid] * (scores.shape[1] // valid.shape[1]), axis=1)
    return jnp.where(wide > 0.0, scores, -1e30)


def columns(base, tall, wide):
    return [
        pl.BlockSpec((1, BLOCK, BLOCK), lambda n, where, i=i: (where[base + i * wide + n], 0, 0))
        for i in range(tall)
    ]


def rows(base, wide):
    return [
        pl.BlockSpec((1, BLOCK, BLOCK), lambda n, where, k=k: (where[base + n * wide + k], 0, 0))
        for k in range(wide)
    ]


def whole(shape):
    return pl.BlockSpec(shape, lambda n, where: (0,) * len(shape))


def stripe(height):
    return pl.BlockSpec((height, BLOCK), lambda n, where: (0, n))


def by_columns(left, blocks):
    total = dot(left[:, part(0)], blocks[0][0])
    for i in range(1, len(blocks)):
        total = total + dot(left[:, part(i)], blocks[i][0])
    return total


def by_rows(left, blocks):
    total = dot_nt(left[:, part(0)], blocks[0][0])
    for i in range(1, len(blocks)):
        total = total + dot_nt(left[:, part(i)], blocks[i][0])
    return total


def attend(queries, keys, values_turned, weights, valid, count):
    outs, logs = [], []
    for pair in range(2):
        lanes = slice(pair * 2 * HEAD, (pair + 1) * 2 * HEAD)
        key_pair = keys[:count, lanes]
        for which, query in enumerate(halves(queries[:, lanes])):
            head = pair * 2 + which
            scores = masked(dot_nt(key_pair, query), valid)
            top = jnp.max(scores, axis=0, keepdims=True)
            exponent = jnp.exp(scores - top)
            total = jnp.sum(exponent, axis=0, keepdims=True)
            weights[:count] = low(exponent)
            mixed = dot(values_turned[head * HEAD : (head + 1) * HEAD], weights[...])
            outs.append(mixed / total)
            logs.append(top + jnp.log(total))
    turned = jnp.concatenate(outs, axis=0)
    return low(turned.T), jnp.concatenate(logs + logs, axis=0)


def attend_back(queries, keys, values, keys_turned, mixed, grad_mixed, logs, probs, grads, valid, count):
    tokens = queries.shape[0]
    inner = (mixed.astype(WIDE) * grad_mixed.astype(WIDE)).T
    grad_query, grad_key, grad_value = [], [], []
    for pair in range(2):
        lanes = slice(pair * 2 * HEAD, (pair + 1) * 2 * HEAD)
        key_pair, value_pair = keys[:count, lanes], values[:count, lanes]
        query_halves = halves(queries[:, lanes])
        mixed_halves = halves(grad_mixed[:, lanes])
        for which in range(2):
            head = pair * 2 + which
            own = slice(head * HEAD, (head + 1) * HEAD)
            side = slice(which * tokens, (which + 1) * tokens)
            scores = masked(dot_nt(key_pair, query_halves[which]), valid)
            full = jnp.exp(scores - logs[head : head + 1])
            grad_full = dot_nt(value_pair, mixed_halves[which])
            back = low(full * (grad_full - jnp.sum(inner[own], axis=0, keepdims=True)))
            probs[:count, side] = low(full)
            grads[:count, side] = back
            grad_query.append(dot(keys_turned[own], grads[:, side]))
        grad_key.append(dot(grads[:count], jnp.concatenate(query_halves, axis=0)))
        grad_value.append(dot(probs[:count], jnp.concatenate(mixed_halves, axis=0)))
    grad_query = jnp.concatenate(grad_query, axis=0).T * HEAD ** (-0.5)
    return grad_query, jnp.concatenate(grad_key, axis=1), jnp.concatenate(grad_value, axis=1)


def send_blocks(stage, sems, store, where, numbers):
    return [
        pltpu.make_async_copy(stage.at[i], store.at[where[number]], sems.at[i])
        for i, number in enumerate(numbers)
    ]


def cross_forward_kernel(count, where, x, tokens, shifts, valid, *rest):
    q, k, v, o = rest[:4], rest[4:7], rest[7:10], rest[10:14]
    normed_turned, cq, ck, cv, co, logs, x1, n2, normed, total, turned, weights = rest[14:]
    n = pl.program_id(0)

    @pl.when(n == 0)
    def first():
        one = low(modulated_norm(x[...].astype(WIDE), shifts[0:1], shifts[1:2]))
        normed[...] = one
        normed_turned[...] = one.T
        total[...] = x[...].astype(WIDE)
        turned[...] = jnp.zeros_like(turned)
        weights[...] = jnp.zeros_like(weights)

    queries = low(by_columns(normed, q)) * HEAD ** (-0.5)
    cq[...] = queries
    ck[...] = low(by_columns(tokens, k))
    cv[...] = low(by_columns(tokens, v))
    turned[:count] = cv[...]
    mixed, log_total = attend(queries, ck, turned[...].T, weights, valid[...], count)
    co[...] = mixed
    logs[0] = log_total
    for i in range(4):
        total[:, part(i)] += dot(mixed, o[i][0])

    @pl.when(n == 3)
    def last():
        after = total[...]
        x1[...] = after
        n2[...] = low(modulated_norm(after, shifts[2:3], shifts[3:4]))


def self_forward_kernel(x1, mine, other, shifts, *rest):
    q, k, v, o = rest[:4], rest[4:8], rest[8:12], rest[12:16]
    normed_turned, sq, sk, sv, so, logs, x2, n3, total, weights = rest[16:]
    n = pl.program_id(0)
    rows_here = x1.shape[0]

    @pl.when(n == 0)
    def first():
        normed_turned[:, :rows_here] = mine[...].T
        normed_turned[:, rows_here:] = other[...].T
        total[...] = x1[...]

    queries = low(by_columns(mine, q)) * HEAD ** (-0.5)
    sq[...] = queries
    sk[:rows_here] = low(by_columns(mine, k))
    sk[rows_here:] = low(by_columns(other, k))
    sv[:rows_here] = low(by_columns(mine, v))
    sv[rows_here:] = low(by_columns(other, v))
    mixed, log_total = attend(queries, sk, sv[...].T, weights, None, 2 * rows_here)
    so[...] = mixed
    logs[0] = log_total
    for i in range(4):
        total[:, part(i)] += dot(mixed, o[i][0])

    @pl.when(n == 3)
    def last():
        after = total[...]
        x2[...] = after
        n3[...] = low(modulated_norm(after, shifts[4:5], shifts[5:6]))


def feed_kernel(where, x2, n3, cotangent, shifts, *rest):
    up, down = rest[:4], rest[4:8]
    layer_out, g2, store, total, back, turned, stage, sems = rest[8:]
    f = pl.program_id(0)
    steps = FF // BLOCK

    @pl.when(f == 0)
    def first():
        total[...] = x2[...]
        back[...] = jnp.zeros_like(back)
        turned[...] = n3[...].T

    hidden = by_columns(n3, up)
    grad_act = by_rows(cotangent, down)
    square = hidden * hidden
    root = (2.0 / np.pi) ** 0.5
    bent = jnp.tanh(root * (hidden + 0.044715 * (square * hidden)))
    act = low(0.5 * hidden * (1.0 + bent))
    slope = 0.5 * (1.0 + bent) + 0.5 * hidden * (1.0 - bent * bent) * (
        root * (1.0 + 3.0 * 0.044715 * square)
    )
    eh = low(grad_act * slope)
    act_turned = act.T
    for i in range(4):
        total[:, part(i)] += dot(act, down[i][0])
        back[:, part(i)] += dot_nt(eh, up[i][0])

    numbers = [W_UP + i * steps + f for i in range(4)] + [W_DOWN + f * 4 + i for i in range(4)]

    @pl.when(f > 0)
    def drain():
        for copy in send_blocks(stage, sems, store, where, [W_UP] * 8):
            copy.wait()

    for i in range(4):
        stage[i] = low(dot(turned[part(i)], eh))
        stage[4 + i] = low(dot(act_turned, cotangent[:, part(i)]))
    for copy in send_blocks(stage, sems, store, where, numbers):
        copy.start()

    @pl.when(f == steps - 1)
    def last():
        layer_out[...] = low(total[...])
        g2[...] = cotangent[...].astype(WIDE) + norm_back(x2[...], shifts[5:6], back[...])
        for copy in send_blocks(stage, sems, store, where, numbers):
            copy.wait()


def self_backward_kernel(where, g2, normed_turned, sq, sk, sv, so, logs, *rest):
    q, k, v, o = rest[:4], rest[4:8], rest[8:12], rest[12:16]
    own_back, other_back, store, es, probs, grads, own_total, other_total, stage, sems = rest[17:]
    n = pl.program_id(0)
    here = g2.shape[0]
    both = 2 * here

    @pl.when(n == 0)
    def first():
        es[...] = low(g2[...])
        own_total[...] = jnp.zeros_like(own_total)
        other_total[...] = jnp.zeros_like(other_total)

    grad_mixed = low(by_rows(es, o))
    dq, dk, dv = attend_back(
        sq, sk, sv, sk[...].T, so[...], grad_mixed, logs[0], probs, grads, None, both
    )
    dq, dk, dv = low(dq), low(dk), low(dv)
    mixed_turned = so[...].T
    for i in range(4):
        own_total[:, part(i)] += (
            dot_nt(dq, q[i][0]) + dot_nt(dk[:here], k[i][0]) + dot_nt(dv[:here], v[i][0])
        )
        other_total[:, part(i)] += dot_nt(dk[here:], k[i][0]) + dot_nt(dv[here:], v[i][0])

    @pl.when(n > 0)
    def drain():
        for copy in send_blocks(stage, sems, store, where, [Q_SELF] * 16):
            copy.wait()

    for i in range(4):
        stage[i] = low(dot(normed_turned[part(i), :here], dq))
        stage[4 + i] = low(dot(normed_turned[part(i)], dk))
        stage[8 + i] = low(dot(normed_turned[part(i)], dv))
        stage[12 + i] = low(dot(mixed_turned, es[:, part(i)]))
    numbers = [base + i * 4 + n for base in (Q_SELF, K_SELF, V_SELF) for i in range(4)]
    numbers += [O_SELF + n * 4 + i for i in range(4)]
    for copy in send_blocks(stage, sems, store, where, numbers):
        copy.start()

    @pl.when(n == 3)
    def last():
        own_back[...] = own_total[...]
        other_back[...] = low(other_total[...])
        for copy in send_blocks(stage, sems, store, where, numbers):
            copy.wait()


def cross_backward_kernel(
    count, where, x, g2, x1, own_back, got_back, tokens, shifts, valid, normed_turned, cq, ck, cv, co, logs, *rest
):
    q, k, v, o = rest[:4], rest[4:7], rest[7:10], rest[10:14]
    grad_x, grad_tokens, store, ec, g1, probs, grads, x_total, turned, keys_padded, rows_padded, stage, sems = rest[15:]
    n = pl.program_id(0)

    @pl.when(n == 0)
    def first():
        value = g2[...] + norm_back(
            x1[...], shifts[3:4], own_back[...] + got_back[...].astype(WIDE)
        )
        g1[...] = value
        ec[...] = low(value)
        x_total[...] = jnp.zeros_like(x_total)
        grad_tokens[...] = jnp.zeros_like(grad_tokens)
        probs[...] = jnp.zeros_like(probs)
        grads[...] = jnp.zeros_like(grads)
        keys_padded[...] = jnp.zeros_like(keys_padded)
        rows_padded[...] = jnp.zeros_like(rows_padded)
        rows_padded[0, :count] = tokens[:, :BLOCK]
        rows_padded[1, :count] = tokens[:, BLOCK : 2 * BLOCK]
        rows_padded[2, :count] = tokens[:, 2 * BLOCK :]
        for i in range(3):
            turned[part(i)] = rows_padded[i].T

    grad_mixed = low(by_rows(ec, o))
    keys_padded[:count] = ck[...]
    dq, dk, dv = attend_back(
        cq, ck, cv, keys_padded[...].T, co[...], grad_mixed, logs[0], probs, grads, valid[...], count
    )
    dq = low(dq)
    rows_padded[0, :count] = low(dk)
    rows_padded[1, :count] = low(dv)
    mixed_turned = co[...].T
    for i in range(4):
        x_total[:, part(i)] += dot_nt(dq, q[i][0])
    for i in range(3):
        grad_tokens[:, part(i)] += dot_nt(rows_padded[0, :count], k[i][0]) + dot_nt(
            rows_padded[1, :count], v[i][0]
        )

    @pl.when(n > 0)
    def drain():
        for copy in send_blocks(stage, sems, store, where, [Q_CROSS] * 14):
            copy.wait()

    for i in range(4):
        stage[i] = low(dot(normed_turned[part(i)], dq))
        stage[10 + i] = low(dot(mixed_turned, ec[:, part(i)]))
    for i in range(3):
        stage[4 + i] = low(dot(turned[part(i)], rows_padded[0]))
        stage[7 + i] = low(dot(turned[part(i)], rows_padded[1]))
    numbers = [Q_CROSS + i * 4 + n for i in range(4)]
    numbers += [base + i * 4 + n for base in (K_CROSS, V_CROSS) for i in range(3)]
    numbers += [O_CROSS + n * 4 + i for i in range(4)]
    for copy in send_blocks(stage, sems, store, where, numbers):
        copy.start()

    @pl.when(n == 3)
    def last():
        grad_x[...] = g1[...] + norm_back(x[...].astype(WIDE), shifts[1:2], x_total[...])
        for copy in send_blocks(stage, sems, store, where, numbers):
            copy.wait()


def shape(*dims, kind=LOW):
    return jax.ShapeDtypeStruct(dims, kind)


def call(kernel, grid, where, ins, outs, scratch, aliases=None):
    return pl.pallas_call(
        kernel,
        grid_spec=pltpu.PrefetchScalarGridSpec(
            num_scalar_prefetch=1,
            grid=(grid,),
            in_specs=[spec for _, spec in ins],
            out_specs=[spec for _, spec in outs],
            scratch_shapes=scratch,
        ),
        out_shape=[struct for struct, _ in outs],
        input_output_aliases=aliases or {},
        compiler_params=pltpu.CompilerParams(vmem_limit_bytes=VLIM),
    )(where, *[array for array, _ in ins])


def full(array):
    return (array, whole(array.shape))


def made(*dims, kind=LOW):
    return (shape(*dims, kind=kind), whole(dims))


def striped(height):
    return (shape(height, D), stripe(height))


LOG_SPEC = pl.BlockSpec((1, 8, TOK_DEV), lambda n, where: (n, 0, 0))
ANYWHERE = pl.BlockSpec(memory_space=pl.ANY)


def cross_forward(where, store, x, tokens, shifts, valid):
    here, count = x.shape[0], tokens.shape[0]
    padded = -(-count // 128) * 128
    specs = columns(Q_CROSS, 4, 4) + columns(K_CROSS, 3, 4) + columns(V_CROSS, 3, 4) + rows(O_CROSS, 4)
    return call(
        functools.partial(cross_forward_kernel, count),
        4,
        where,
        [full(x), full(tokens), full(shifts), full(valid)] + [(store, spec) for spec in specs],
        [
            made(D, here),
            striped(here),
            striped(count),
            striped(count),
            striped(here),
            (shape(4, 8, here, kind=WIDE), LOG_SPEC),
            made(here, D, kind=WIDE),
            made(here, D),
        ],
        [
            pltpu.VMEM((here, D), LOW),
            pltpu.VMEM((here, D), WIDE),
            pltpu.VMEM((padded, BLOCK), LOW),
            pltpu.VMEM((padded, here), LOW),
        ],
    )


def self_forward(where, store, x1, mine, other, shifts):
    here = x1.shape[0]
    specs = columns(Q_SELF, 4, 4) + columns(K_SELF, 4, 4) + columns(V_SELF, 4, 4) + rows(O_SELF, 4)
    return call(
        lambda where, *refs: self_forward_kernel(*refs),
        4,
        where,
        [full(x1), full(mine), full(other), full(shifts)] + [(store, spec) for spec in specs],
        [
            made(D, 2 * here),
            striped(here),
            striped(2 * here),
            striped(2 * here),
            striped(here),
            (shape(4, 8, here, kind=WIDE), LOG_SPEC),
            made(here, D, kind=WIDE),
            made(here, D),
        ],
        [pltpu.VMEM((here, D), WIDE), pltpu.VMEM((2 * here, here), LOW)],
    )


def feed(where, store, x2, n3, cotangent, shifts, slots):
    here = x2.shape[0]
    specs = columns(W_UP, 4, FF // BLOCK) + rows(W_DOWN, 4)
    return call(
        feed_kernel,
        FF // BLOCK,
        where,
        [full(x2), full(n3), full(cotangent), full(shifts)] + [(store, spec) for spec in specs],
        [made(here, D), made(here, D, kind=WIDE), (shape(slots, BLOCK, BLOCK), ANYWHERE)],
        [
            pltpu.VMEM((here, D), WIDE),
            pltpu.VMEM((here, D), WIDE),
            pltpu.VMEM((D, here), LOW),
            pltpu.VMEM((8, BLOCK, BLOCK), LOW),
            pltpu.SemaphoreType.DMA((8,)),
        ],
    )


def self_backward(where, store, grads, g2, normed_turned, sq, sk, sv, so, logs):
    here = g2.shape[0]
    specs = columns(Q_SELF, 4, 4) + columns(K_SELF, 4, 4) + columns(V_SELF, 4, 4) + rows(O_SELF, 4)
    stripes = [(a, stripe(a.shape[0])) for a in (sq, sk, sv, so)]
    ins = [full(g2), full(normed_turned)] + stripes + [(logs, LOG_SPEC)]
    ins += [(store, spec) for spec in specs] + [(grads, ANYWHERE)]
    return call(
        self_backward_kernel,
        4,
        where,
        ins,
        [made(here, D, kind=WIDE), made(here, D), (shape(*grads.shape), ANYWHERE)],
        [
            pltpu.VMEM((here, D), LOW),
            pltpu.VMEM((2 * here, 2 * here), LOW),
            pltpu.VMEM((2 * here, 2 * here), LOW),
            pltpu.VMEM((here, D), WIDE),
            pltpu.VMEM((here, D), WIDE),
            pltpu.VMEM((16, BLOCK, BLOCK), LOW),
            pltpu.SemaphoreType.DMA((16,)),
        ],
        {len(ins): 2},
    )


def cross_backward(
    where, store, grads, x, g2, x1, own_back, got_back, tokens, shifts, valid, normed_turned, cq, ck, cv, co, logs
):
    here, count = x.shape[0], tokens.shape[0]
    padded = -(-count // 128) * 128
    specs = columns(Q_CROSS, 4, 4) + columns(K_CROSS, 3, 4) + columns(V_CROSS, 3, 4) + rows(O_CROSS, 4)
    ins = [full(a) for a in (x, g2, x1, own_back, got_back, tokens, shifts, valid, normed_turned)]
    ins += [(a, stripe(a.shape[0])) for a in (cq, ck, cv, co)] + [(logs, LOG_SPEC)]
    ins += [(store, spec) for spec in specs] + [(grads, ANYWHERE)]
    return call(
        functools.partial(cross_backward_kernel, count),
        4,
        where,
        ins,
        [made(here, D, kind=WIDE), made(count, DIMG, kind=WIDE), (shape(*grads.shape), ANYWHERE)],
        [
            pltpu.VMEM((here, D), LOW),
            pltpu.VMEM((here, D), WIDE),
            pltpu.VMEM((padded, 2 * here), LOW),
            pltpu.VMEM((padded, 2 * here), LOW),
            pltpu.VMEM((here, D), WIDE),
            pltpu.VMEM((DIMG, padded), LOW),
            pltpu.VMEM((padded, BLOCK), LOW),
            pltpu.VMEM((3, padded, BLOCK), LOW),
            pltpu.VMEM((14, BLOCK, BLOCK), LOW),
            pltpu.SemaphoreType.DMA((14,)),
        ],
        {len(ins): 2},
    )


def partner(block, axis):
    size = lax.axis_size(axis)
    return lax.ppermute(block, axis, [(i, i ^ 1) for i in range(size)])


def soap_update(
    slot_grads,
    first_moment,
    second_moment,
    left_basis,
    right_basis,
    master_weights,
    slot_rates,
    slot_used,
):
    keep_mask = slot_used[:, None, None] > 0.0
    slot_grads = jnp.where(keep_mask, slot_grads, 0.0)
    rotated = jnp.matmul(
        jnp.matmul(jnp.swapaxes(left_basis, 1, 2), slot_grads, precision=highest),
        right_basis,
        precision=highest,
    )
    first_new = moment_decay * first_moment + (1.0 - moment_decay) * rotated
    second_new = moment_decay * second_moment + (1.0 - moment_decay) * rotated * rotated
    correction = 1.0 - moment_decay**STEP
    normalized = first_new / correction / (jnp.sqrt(second_new / correction) + 1e-08)
    rotated_back = jnp.matmul(
        jnp.matmul(left_basis, normalized, precision=highest),
        jnp.swapaxes(right_basis, 1, 2),
        precision=highest,
    )
    fresh_master = master_weights - slot_rates[:, None, None] * (
        rotated_back + 0.01 * master_weights
    )
    fresh_master = jnp.where(keep_mask, fresh_master, 0.0)
    return (
        slot_grads,
        jnp.where(keep_mask, first_new, 0.0),
        jnp.where(keep_mask, second_new, 0.0),
        fresh_master,
        fresh_master.astype(jnp.bfloat16),
    )


def shards(
    triplane,
    cotangent,
    image_tokens,
    modulation,
    image_counts,
    owner_slots,
    master_weights,
    first_moment,
    second_moment,
    left_basis,
    right_basis,
):
    img_size = lax.axis_size("img")
    rows_size = lax.axis_size("rows")
    img_index = lax.axis_index("img")
    flat_index = lax.axis_index("rows") * img_size + img_index
    object_index = flat_index // 2
    pair_index = img_index // 2
    groups = img_size // 2
    slot_cap = image_tokens.shape[0] // groups
    own_count = master_weights.shape[0]
    slot_total = rows_size * img_size * own_count
    fits = rows_size == 16 and img_size == 2 and own_count == 8
    if fits:
        store = gather(master_weights, WAVE_OUT).reshape(-1, BLOCK, BLOCK)
        where = positions(owner_slots)
    else:
        store = lax.all_gather(master_weights.astype(LOW), ("rows", "img"), axis=0, tiled=True)
        where = owner_slots
    where = where.astype(jnp.int32)
    shifts = lax.dynamic_index_in_dim(modulation, object_index, 0, keepdims=False)
    count_here = lax.dynamic_index_in_dim(image_counts, object_index, 0, keepdims=False)
    slot = jnp.arange(slot_cap, dtype=jnp.int32)
    if img_size == 2:
        tokens = jnp.concatenate([image_tokens, partner(image_tokens, "img")], 0)
        sources = jnp.stack([img_index, 1 - img_index])
    else:
        gathered = lax.all_gather(image_tokens, "img", axis=0, tiled=True)
        gathered = gathered.reshape(img_size, groups, slot_cap, DIMG)
        tokens = lax.dynamic_index_in_dim(gathered, pair_index, 1, keepdims=False)
        tokens = tokens.reshape(img_size * slot_cap, DIMG)
        sources = jnp.arange(img_size, dtype=jnp.int32)
    token_index = (slot[None, :] * img_size + sources[:, None]).reshape(-1)
    valid = jnp.broadcast_to((token_index < count_here).astype(WIDE)[:, None], (token_index.shape[0], 128))

    n1_turned, cq, ck, cv, co, cross_logs, x1, n2 = cross_forward(
        where, store, triplane, tokens, shifts, valid
    )
    n2_turned, sq, sk, sv, so, self_logs, x2, n3 = self_forward(
        where, store, x1, n2, partner(n2, "img"), shifts
    )
    layer_out, g2, grads = feed(where, store, x2, n3, cotangent, shifts, slot_total)
    own_back, other_back, grads = self_backward(
        where, store, grads, g2, n2_turned, sq, sk, sv, so, self_logs
    )
    grad_triplane, grad_tokens, grads = cross_backward(
        where,
        store,
        grads,
        triplane,
        g2,
        x1,
        own_back,
        partner(other_back, "img"),
        tokens,
        shifts,
        valid,
        n1_turned,
        cq,
        ck,
        cv,
        co,
        cross_logs,
    )
    if img_size == 2:
        grad_image = grad_tokens[:slot_cap] + partner(grad_tokens[slot_cap:].astype(LOW), "img").astype(WIDE)
    else:
        pick = (jnp.arange(groups, dtype=jnp.int32) == pair_index).astype(WIDE)
        spread = grad_tokens.reshape(img_size, 1, slot_cap, DIMG) * pick[None, :, None, None]
        grad_image = lax.psum_scatter(
            spread.reshape(img_size * groups * slot_cap, DIMG).astype(LOW),
            "img",
            scatter_dimension=0,
            tiled=True,
        ).astype(WIDE)
    if fits:
        slot_grads = scatter(grads.reshape(2, 8, 16, BLOCK, BLOCK), WAVE_IN)
    else:
        used = jnp.zeros((slot_total,), jnp.bool_).at[owner_slots].set(True)
        grads = jnp.where(used[:, None, None], grads, jnp.zeros_like(grads))
        slot_grads = lax.psum_scatter(
            grads, ("rows", "img"), scatter_dimension=0, tiled=True
        ).astype(WIDE)
    my_slots = flat_index * own_count + jnp.arange(own_count, dtype=jnp.int32)
    matched = (owner_slots[:, None] == my_slots[None, :]).astype(WIDE)
    slot_used = jnp.sum(matched, axis=0)
    slot_rates = jnp.sum(matched * jnp.asarray(block_table(weight_scales()))[:, None], axis=0)
    updated = soap_update(
        slot_grads,
        first_moment,
        second_moment,
        left_basis,
        right_basis,
        master_weights,
        slot_rates,
        slot_used,
    )
    return (layer_out, grad_triplane, grad_image) + tuple(updated)


def solution(mesh):
    flat = P(("rows", "img"), None)
    blocks = P(("rows", "img"), None, None)
    in_specs = (flat, flat, flat, P(), P(), P()) + (blocks,) * 5
    out_specs = (flat, flat, flat) + (blocks,) * 5
    return jax.shard_map(shards, mesh=mesh, in_specs=in_specs, out_specs=out_specs, check_vma=False)
```

time: 1410 us -> 581 us (0.41)
  matrix products: 494 us -> 16.3 us
  local copies, waits for them, and re-layouts: 447 us -> 9.31 us
  Pallas kernels: 325 us -> 498 us
  other arithmetic: 60.5 us -> 5.96 us
  between operations: 15.5 us -> 1.03 us
    dot_general x245 -> x0, matrix products: 474 us -> none  [project(): return jnp.dot(left, right, preferred_element_type=jnp.float32)]
    pallas_call x0 -> x5, Pallas kernels: none -> 172 us  [call(): pl.pallas_call(kernel, grid_spec=pltpu.PrefetchScalarGridSpec(num_scalar_...]
    unnamed x167 -> x32, local copies, waits for them, and re-layouts: 106 us -> 3.61 us
    transpose x21 -> x0, local copies, waits for them, and re-layouts: 88.9 us -> none  [the longest x11 50.3 us: join_blocks(): matrix.reshape(rows_in // BLOCK, BLOCK, cols_out // BLOCK, BLOCK)]
    scatter x1 -> x0, local copies, waits for them, and re-layouts: 84.7 us -> none  [shards(): jnp.zeros((slot_total, BLOCK, BLOCK), jnp.bfloat16).at[where]]
    slice x16 -> x1, local copies, waits for them, and re-layouts: 51.3 us -> 1.5 us  [shards(): grad_tokens[slot_cap:].astype(LOW)]
    reshape x9 -> x0, local copies, waits for them, and re-layouts: 49.8 us -> none  [join_blocks(): matrix.reshape(rows_in // BLOCK, BLOCK, cols_out // BLOCK, BLOCK)]
    gather x1 -> x0, local copies, waits for them, and re-layouts: 22.6 us -> none  [shards(): gathered_weights[where]]
  transfers between devices with their start and end apart: 4 -> 4, of which waited for: 2 -> 2; matrix products, arithmetic and copies ran while one was open for 19% -> 4% of each run, Pallas kernels for 0% -> 57%
where the time goes in v2:
time: 581 us; the launch traced here: 572 us
  Pallas kernels  498 us (86%)
  waiting for transfers between devices  37.2 us (6%)
  matrix products  16.3 us (3%)
  local copies, waits for them, and re-layouts  9.31 us (2%)
  other arithmetic  5.96 us (1%)
    pallas_call x5, Pallas kernels, call(): pl.pallas_call(kernel, grid_spec=pltpu.PrefetchScalarGridSpec(num_scalar_...  172 us
    pallas_call x1, Pallas kernels, gather(): pl.pallas_call(functools.partial(gather_kernel, order), out_shape=jax.Sha...  166 us
    pallas_call x1, Pallas kernels, scatter(): pl.pallas_call(functools.partial(scatter_kernel, order), out_shape=jax.Sh...  160 us
    ppermute x4, waiting for transfers between devices, partner(): return lax.ppermute(block, axis, [(i, i ^ 1) for i in range(size)])  37.2 us
  transfers between devices with their start and end apart: 4, of which 2 were waited for; matrix products, arithmetic and copies ran while one was open for 4% of the time, Pallas kernels for 57%

profile of v2, /device:TPU:0, one launch (start us, length us, event | category | flops | bytes accessed | tf_op | source)
XLA Modules:
  0.0 572.3 jit_solution(9538525563540648831)
XLA Ops:
  0.6 3.0 collective-permute-start
  3.7 0.9 constant_dynamic-slice_fusion
  4.6 0.6 copy.34
  5.2 1.2 dynamic_slice.9
  6.6 0.7 compare_convert_fusion.1
  7.4 166.1 %shard_map.179 = bf16[2,8,16,256,256]{4,3,2,1,0:T(8,128)(2,1)} custom-call(f32[8,256,256]{2,1,0:T(8,128)} %master.1), custom_call_target="tpu_custom_call" | custom-call | tf_op jit(solution)/shard_map/pallas_call | solution.py:85
  173.5 0.9 constant_dynamic-update-slice_fusion.1
  174.4 0.6 multiply_add_fusion.2.where
  175.0 0.9 constant_dynamic-update-slice_fusion.tokens
  176.0 1.0 broadcast_in_dim.37.valid
  177.0 28.2 %shard_map.180 = (bf16[1024,384]{1,0:T(8,128)(2,1)}, bf16[384,1024]{1,0:T(8,128)(2,1)}, bf16[1040,1024]{1,0:T(8,128)(2,1)}, bf16[1040,1024]{1,0:T(8,128)(2,1)}, ...) custom-call(s32[248]{0:T(256)} %multiply_add_fusion.2.where, ...), custom_call_target="tpu_custom_call" | custom-call | tf_op jit(solution)/shard_map/pallas_call | solution.py:563
  205.1 0.6 collective-permute-start.1
  205.7 19.6 %collective-permute-done.1.refs_2_ = bf16[384,1024]{1,0:T(8,128)(2,1)S(1)} collective-permute-done((bf16[384,1024]{1,0:T(8,128)(2,1)}, bf16[384,1024]{1,0:T(8,128)(2,1)S(1)}, u32[]{:S(2)}, u32[]{:S(2)}) %collective-permute-start.1) | collective-permute-done | bytes 786464 | tf_op jit(solution)/shard_map/ppermute | solution.py:721
  225.3 0.9 copy-done.9
  226.2 22.9 %shard_map.181 = (bf16[1024,768]{1,0:T(8,128)(2,1)}, bf16[384,1024]{1,0:T(8,128)(2,1)}, bf16[768,1024]{1,0:T(8,128)(2,1)}, bf16[768,1024]{1,0:T(8,128)(2,1)}, bf...) custom-call(s32[248]{0:T(256)} %multiply_add_fusion.2.where, ...), custom_call_target="tpu_custom_call" | custom-call | tf_op jit(solution)/shard_map/pallas_call | solution.py:563
  249.1 40.0 %shard_map.182 = (bf16[384,1024]{1,0:T(8,128)(2,1)}, f32[384,1024]{1,0:T(8,128)}, bf16[256,256,256]{2,1,0:T(8,128)(2,1)}) custom-call(s32[248]{0:T(256)} %multiply_add_fusion.2.where, f32[384,1024]{1,0:T(8,128)} %get-tuple-element.35.x2, bf16[384,1024]{1,0:T(8,128)(2,1)} %get-tuple-element.36.n3, bf16[384,1024]{1,0:T(8,128)(2,1)} %cotangent.1, ...), custom_call_target="tpu_custom_call" | custom-call | tf_op jit(solution)/shard_map/pallas_call | solution.py:563
  289.2 34.0 %shard_map.183 = (f32[384,1024]{1,0:T(8,128)}, bf16[384,1024]{1,0:T(8,128)(2,1)}, bf16[256,256,256]{2,1,0:T(8,128)(2,1)}) custom-call(s32[248]{0:T(256)} %multiply_add_fusion.2.where, f32[384,1024]{1,0:T(8,128)} %get-tuple-element.38.g2, bf16[1024,768]{1,0:T(8,128)(2,1)} %get-tuple-element.39.normed_turned, ...), custom_call_target="tpu_custom_call", output_to_operand_aliasing={{2}: (24, {})} | custom-call | tf_op jit(solution)/shard_map/pallas_call | solution.py:563
  323.2 0.6 collective-permute-start.2
  323.7 0.7 fusion.11
  324.4 0.5 broadcast_compare_fusion
  325.0 17.6 %collective-permute-done.2.got_back = bf16[384,1024]{1,0:T(8,128)(2,1)S(1)} collective-permute-done((bf16[384,1024]{1,0:T(8,128)(2,1)}, bf16[384,1024]{1,0:T(8,128)(2,1)S(1)}, u32[]{:S(2)}, u32[]{:S(2)}) %collective-permute-start.2) | collective-permute-done | bytes 786464 | tf_op jit(solution)/shard_map/ppermute | solution.py:721
  342.6 0.9 copy-done.8
  343.4 46.9 %shard_map.184 = (f32[384,1024]{1,0:T(8,128)}, f32[1040,768]{1,0:T(8,128)}, bf16[256,256,256]{2,1,0:T(8,128)(2,1)}) custom-call(s32[248]{0:T(256)} %multiply_add_fusion.2.where, bf16[384,1024]{1,0:T(8,128)(2,1)} %x.3, f32[384,1024]{1,0:T(8,128)} %get-tuple-element.38.g2, f32[384,1024]{1,0:T(8,128)} %get-tuple-element.33.refs_0_.x1, ...), custom_call_target="tpu_custom_call", output_to_operand_aliasing={{2}: (29, {})} | custom-call | tf_op jit(solution)/shard_map/pallas_call | solution.py:563
  390.3 1.5 slice.12
  391.8 0.5 collective-permute-start.3
  392.4 159.6 %shard_map.185 = f32[8,256,256]{2,1,0:T(8,128)} custom-call(bf16[2,8,16,256,256]{4,3,2,1,0:T(8,128)(2,1)} %bitcast.83), custom_call_target="tpu_custom_call" | custom-call | tf_op jit(solution)/shard_map/pallas_call | solution.py:130
  552.1 2.0 broadcast_select_fusion.2
  554.3 3.6 fusion.21
  558.0 4.7 broadcast_select_fusion
  562.7 3.8 fusion.1
  566.5 4.2 fusion.20
  570.7 1.4 convert_add_fusion
  (34 shorter events, 0.5 us)
Async XLA Ops:
  0.6 557.3 %copy-start = (f32[8,256,256]{2,1,0:T(8,128)S(1)}, f32[8,256,256]{2,1,0:T(8,128)}, u32[]{:S(2)}) copy-start(f32[8,256,256]{2,1,0:T(8,128)} %param.22) | copy-start | bytes 6291460
  0.6 174.4 %collective-permute-start = (bf16[520,768]{1,0:T(8,128)(2,1)}, bf16[520,768]{1,0:T(8,128)(2,1)S(1)}, u32[]{:S(2)}, u32[]{:S(2)}) collective-permute-start(bf16[520,768]{1,0:T(8,128)(2,1)} %param.14), channel_id=1, source_target_pairs={{0,1},{1,0},{2,3},{3,2},{4,5},{5,4},{6,7},{7,6},{8,9},{9,8},{10,11... | collective-permute-start | bytes 2396168 | tf_op jit(solution)/shard_map/ppermute | solution.py:721
  7.4 166.1 %copy-start.7 = (bf16[520,768]{1,0:T(8,128)(2,1)S(1)}, bf16[520,768]{1,0:T(8,128)(2,1)}, u32[]{:S(2)}) copy-start(bf16[520,768]{1,0:T(8,128)(2,1)} %param.14) | copy-start | bytes 2396164
  7.4 167.0 %copy-start.11 = (s32[248]{0:T(256)S(1)}, s32[248]{0:T(256)}, u32[]{:S(2)}) copy-start(s32[248]{0:T(256)} %param.17) | copy-start | bytes 2980
  205.1 20.2 %collective-permute-start.1 = (bf16[384,1024]{1,0:T(8,128)(2,1)}, bf16[384,1024]{1,0:T(8,128)(2,1)S(1)}, u32[]{:S(2)}, u32[]{:S(2)}) collective-permute-start(bf16[384,1024]{1,0:T(8,128)(2,1)} %get-tuple-element.34.refs_1_), channel_id=1, source_target_pairs={{0,1},{1,0},{2,3},{3,2},{4,5},{5,4},{6,7},{7,6},{8,9},{9,8},{10,11... | collective-permute-start | bytes 2359304 | tf_op jit(solution)/shard_map/ppermute | solution.py:721
  225.3 0.9 copy-start.9
  289.1 34.6 %copy-start.12 = (s32[248]{0:T(256)S(1)}, s32[248]{0:T(256)}, u32[]{:S(2)}) copy-start(s32[248]{0:T(256)} %param.17) | copy-start | bytes 2980
  289.2 34.6 %copy-start.14 = (f32[248]{0:T(256)S(1)}, f32[248]{0:T(256)}, u32[]{:S(2)}) copy-start(f32[248]{0:T(256)} %constant.137.clone) | copy-start | bytes 2980
  323.2 19.4 %collective-permute-start.2 = (bf16[384,1024]{1,0:T(8,128)(2,1)}, bf16[384,1024]{1,0:T(8,128)(2,1)S(1)}, u32[]{:S(2)}, u32[]{:S(2)}) collective-permute-start(bf16[384,1024]{1,0:T(8,128)(2,1)} %get-tuple-element.47), channel_id=1, source_target_pairs={{0,1},{1,0},{2,3},{3,2},{4,5},{5,4},{6,7},{7,6},{8,9},{9,8},{10,11... | collective-permute-start | bytes 2359304 | tf_op jit(solution)/shard_map/ppermute | solution.py:721
  342.5 0.9 copy-start.8
  391.8 178.9 %collective-permute-start.3 = (bf16[520,768]{1,0:T(8,128)(2,1)S(1)}, bf16[520,768]{1,0:T(8,128)(2,1)S(1)}, u32[]{:S(2)}, u32[]{:S(2)}) collective-permute-start(bf16[520,768]{1,0:T(8,128)(2,1)S(1)} %slice.12), channel_id=1, source_target_pairs={{0,1},{1,0},{2,3},{3,2},{4,5},{5,4},{6,7},{7,6},{8,9},{9,8},{10,11... | collective-permute-start | bytes 2396168 | tf_op jit(solution)/shard_map/ppermute | solution.py:721
  392.4 159.7 %copy-start.10 = (pred[8]{0:T(512)(128)(4,1)S(1)}, pred[8]{0:T(512)(128)(4,1)}, u32[]{:S(2)}) copy-start(pred[8]{0:T(512)(128)(4,1)} %broadcast_compare_fusion) | copy-start | bytes 28
  552.1 2.2 copy-start.3
  554.3 3.6 copy-start.2
  554.3 3.6 copy-start.4
  554.3 3.7 copy-start.5
  562.7 3.8 copy-start.1
  562.7 3.8 copy-start.13
  566.5 4.2 copy-start.6

commit v3 on v2

v3 whole, which is shorter than its diff:
```python
import functools

import jax
import jax.numpy as jnp
import numpy as np
from jax import lax
from jax.experimental import pallas as pl
from jax.experimental.pallas import tpu as pltpu
from jax.sharding import PartitionSpec as P

D = 1024
HEADS = 16
FF = 4096
DIMG = 768
TOK_DEV = 384
IMG_MAX = 1025
BLOCK = 256
STEP = 5
HEAD = D // HEADS

MESH = pl.DeviceIdType.MESH
VLIM = 60 * 1024 * 1024
WAYS_OUT = (
    ('hi', 'x', 'y', 'lo'),
    ('lo', 'y', 'hi', 'x'),
    ('y', 'hi', 'lo', 'x'),
    ('hi', 'y', 'lo', 'x'),
    ('lo', 'x', 'hi', 'y'),
    ('x', 'hi', 'lo', 'y'),
    ('hi', 'lo', 'x', 'y'),
    ('hi', 'lo', 'y', 'x'),
)
WAYS_IN = (
    ('hi', 'y', 'lo', 'x'),
    ('hi', 'x', 'lo', 'y'),
    ('hi', 'y', 'lo', 'x'),
    ('hi', 'x', 'lo', 'y'),
    ('hi', 'y', 'lo', 'x'),
    ('hi', 'x', 'lo', 'y'),
    ('hi', 'y', 'lo', 'x'),
    ('hi', 'x', 'lo', 'y'),
)
FRONT = 17
ORDER_OUT = (
    (-1, 0), (0, 0), (1, 0), (2, 0), (3, 0), (4, 0), (5, 0), (6, 0),
    (7, 0), (6, 1), (7, 1), (4, 1), (1, 1), (0, 1), (4, 2), (3, 1),
    (6, 2), (7, 2), (7, 3), (6, 3), (3, 2), (5, 1), (2, 1), (0, 2),
    (5, 2), (1, 2), (3, 3), (4, 3), (1, 3), (2, 2), (6, 4), (2, 3),
    (4, 4), (5, 3), (0, 3), (3, 4), (7, 4), (1, 4), (5, 4), (0, 4),
    (2, 4),
)
ORDER_IN = (
    (0, 0), (1, 0), (2, 0), (3, 0), (4, 0), (5, 0), (6, 0), (7, 0),
    (0, 1), (1, 1), (2, 1), (3, 1), (0, 2), (1, 2), (4, 1), (5, 1),
    (2, 2), (3, 2), (0, 3), (1, 3), (6, 1), (7, 1), (4, 2), (5, 2),
    (2, 3), (3, 3), (0, 4), (1, 4), (6, 2), (7, 2), (4, 3), (5, 3),
    (2, 4), (3, 4), (0, 5), (1, 5), (6, 3), (7, 3), (4, 4), (5, 4),
    (2, 5), (3, 5), (6, 4), (7, 4), (4, 5), (5, 5), (6, 5), (7, 5),
)


def coords():
    row = lax.axis_index("rows")
    rest = lax.rem(row, 4)
    return lax.div(row, 4), lax.div(rest, 2), lax.rem(rest, 2), lax.axis_index("img")


def neighbour(kind):
    z, x, c, y = coords()
    if kind == "c":
        c = 1 - c
    if kind == "x":
        x = 1 - x
    if kind == "y":
        y = 1 - y
    if kind == "lo":
        z = z + 1 - 2 * lax.rem(z, 2)
    if kind == "hi":
        z = lax.rem(z + 2, 4)
    return (z * 4 + x * 2 + c, y)


def place(way):
    z, x, c, y = coords()
    bits = {"x": x, "y": y, "lo": lax.rem(z, 2), "hi": lax.div(z, 2)}
    return sum(bits[kind] * 2**k for k, kind in enumerate(way))


def positions(slot, ways):
    owner, j = slot // 8, slot % 8
    z, x, c, y = owner // 8, owner // 4 % 2, owner // 2 % 2, owner % 2
    bits = {"x": x, "y": y, "lo": z % 2, "hi": z // 2}
    total = (c * 8 + j) * 16
    for kind, bit in bits.items():
        total = total + bit * jnp.asarray([2 ** way.index(kind) for way in ways], jnp.int32)[j]
    return total


def greet():
    barrier = pltpu.get_barrier_semaphore()
    for kind in ("c", "x", "y", "lo", "hi"):
        pl.semaphore_signal(barrier, inc=1, device_id=neighbour(kind), device_id_type=MESH)
    pl.semaphore_wait(barrier, 5)


def gather_kernel(
    master, tokens, triplane, modulation, out, both, turned, n1, n1_turned,
    own, wide, mine, x, shifts, others, spread, upright, lsem, csem, ssem, rsem, tsem,
):
    c = coords()[2]
    early = [
        pltpu.make_async_copy(source, target, lsem.at[i])
        for i, (source, target) in enumerate(
            ((master, wide), (tokens, mine), (triplane, x), (modulation, shifts))
        )
    ]
    for copy in early:
        copy.start()
    greet()
    cross = pltpu.make_async_remote_copy(
        tokens, others, tsem.at[0], tsem.at[1], device_id=neighbour("y"), device_id_type=MESH
    )
    early[0].wait()
    copies, keeps = {}, {}

    def start(j, k):
        base = place(WAYS_OUT[j])
        count = 2**k
        first = lax.div(base, count) * count if k < 4 else 0
        here = pl.ds(first, count)
        source = own.at[pl.ds(j, 1)] if k == 0 else out.at[c, j, here]
        copy = pltpu.make_async_remote_copy(
            source,
            out.at[c, j, here],
            ssem.at[j, k],
            rsem.at[j, k],
            device_id=neighbour((WAYS_OUT[j] + ("c",))[k]),
            device_id_type=MESH,
        )
        copy.start()
        copies[j, k] = copy

    for j, k in ORDER_OUT:
        if j < 0:
            cross.start()
        elif k == 0:
            own[j] = wide[j].astype(jnp.bfloat16)
            start(j, 0)
            keep = pltpu.make_async_copy(
                own.at[pl.ds(j, 1)], out.at[c, j, pl.ds(place(WAYS_OUT[j]), 1)], csem.at[j]
            )
            keep.start()
            keeps[j] = keep
        else:
            if k == 1:
                keeps[j].wait()
            copies[j, k - 1].wait_recv()
            start(j, k)
        if (j, k) == ORDER_OUT[FRONT]:
            row = pl.ds(lax.axis_index("rows"), 1)
            early[2].wait()
            early[3].wait()
            one = modulated_norm(
                x[...].astype(jnp.float32), shifts[0, row], shifts[1, row]
            )
            n1[...] = one.astype(jnp.bfloat16)
            n1_turned[...] = one.astype(jnp.bfloat16).T
        if (j, k) == ORDER_OUT[FRONT + 6]:
            half = tokens.shape[0]
            cross.wait()
            early[1].wait()
            spread[:half] = mine[...].astype(jnp.float32)
            spread[half:] = others[...].astype(jnp.float32)
            both[...] = spread[...].astype(jnp.bfloat16)
            upright[2 * half :] = jnp.zeros_like(upright[2 * half :])
            for i in range(tokens.shape[1] // BLOCK):
                lanes = slice(i * BLOCK, (i + 1) * BLOCK)
                upright[: 2 * half] = both[:, lanes]
                turned[lanes] = upright[...].T
    for j in range(8):
        copies[j, 4].wait_recv()
    for copy in copies.values():
        copy.wait_send()


def gather(master, tokens, x, modulation):
    anywhere, inside = pl.BlockSpec(memory_space=pl.ANY), pl.BlockSpec(memory_space=pltpu.VMEM)
    half, width = tokens.shape
    padded = -(-2 * half // 128) * 128
    bf = jnp.bfloat16
    return pl.pallas_call(
        gather_kernel,
        out_shape=[
            jax.ShapeDtypeStruct((2, 8, 16, BLOCK, BLOCK), bf),
            jax.ShapeDtypeStruct((2 * half, width), bf),
            jax.ShapeDtypeStruct((width, padded), bf),
            jax.ShapeDtypeStruct(x.shape, bf),
            jax.ShapeDtypeStruct(x.shape[::-1], bf),
        ],
        in_specs=[anywhere] * 4,
        out_specs=[anywhere] + [inside] * 4,
        scratch_shapes=[
            pltpu.VMEM((8, BLOCK, BLOCK), bf),
            pltpu.VMEM((8, BLOCK, BLOCK), jnp.float32),
            pltpu.VMEM((half, width), bf),
            pltpu.VMEM(x.shape, bf),
            pltpu.VMEM(modulation.shape, jnp.float32),
            pltpu.VMEM((half, width), bf),
            pltpu.VMEM((2 * half, width), jnp.float32),
            pltpu.VMEM((padded, BLOCK), bf),
            pltpu.SemaphoreType.DMA((4,)),
            pltpu.SemaphoreType.DMA((8,)),
            pltpu.SemaphoreType.DMA((8, 5)),
            pltpu.SemaphoreType.DMA((8, 5)),
            pltpu.SemaphoreType.DMA((2,)),
        ],
        compiler_params=pltpu.CompilerParams(
            collective_id=11, has_side_effects=True, vmem_limit_bytes=VLIM
        ),
    )(master, tokens, x, modulation)


def times(a, b, left, right):
    return lax.dot_general(
        a,
        b,
        (((left,), (right,)), ((), ())),
        precision=lax.Precision.HIGHEST,
        preferred_element_type=jnp.float32,
    )


def scatter_kernel(grads, first, second, left, right, master, rates, *rest):
    outs = rest[:5]
    own, r0, r1, r2, r3, r4, held, made, made_low, lsem, ssem, rsem, hsem, osem = rest[5:]
    c = coords()[2]
    got = (r0, r1, r2, r3, r4)
    loads, copies, fetches, puts = [], {}, {}, {}
    for j in range(8):
        load = pltpu.make_async_copy(grads.at[c, j], own.at[j], lsem.at[j])
        load.start()
        loads.append(load)
    greet()

    def exchange(j, s, source, kind):
        copy = pltpu.make_async_remote_copy(
            source,
            got[s].at[j],
            ssem.at[j, s],
            rsem.at[j, s],
            device_id=neighbour(kind),
            device_id_type=MESH,
        )
        copy.start()
        copies[j, s] = copy

    def add(j, s):
        count = 16 >> s
        start = lax.div(place(WAYS_IN[j]), count) * count if s else 0

        def body(b, carry):
            own[j, start + b] = (
                own[j, start + b].astype(jnp.float32) + got[s][j, b].astype(jnp.float32)
            ).astype(jnp.bfloat16)
            return carry

        lax.fori_loop(0, count, body, 0)

    def send(j, s):
        count = 16 >> s
        half = lax.div(place(WAYS_IN[j]), count)
        other = (half + 1 - 2 * lax.rem(half, 2)) * count
        exchange(j, s, own.at[j, pl.ds(other, count)], WAYS_IN[j][4 - s])

    def fetch(turn, j):
        side = turn % 2
        fetches[turn] = [
            pltpu.make_async_copy(array.at[j], held.at[side, i], hsem.at[side, i])
            for i, array in enumerate((first, second, left, right, master))
        ]
        for copy in fetches[turn]:
            copy.start()

    def finish(turn, j):
        side = turn % 2
        for copy in fetches[turn]:
            copy.wait()
        if turn >= 2:
            for copy in puts[turn - 2]:
                copy.wait()
        base = place(WAYS_IN[j])
        used = rates[j, 1:2] > 0.0
        total = own[j, base].astype(jnp.float32) + r4[j, 0].astype(jnp.float32)
        total = jnp.where(used, total, 0.0)
        rotated = times(times(held[side, 2], total, 0, 0), held[side, 3], 1, 0)
        new_first = 0.5 * held[side, 0] + 0.5 * rotated
        new_second = 0.5 * held[side, 1] + 0.5 * rotated * rotated
        fix = 1.0 - 0.5**STEP
        unit = (new_first / fix) / (jnp.sqrt(new_second / fix) + 1e-08)
        update = times(times(held[side, 2], unit, 1, 0), held[side, 3], 1, 1)
        old = held[side, 4]
        new = jnp.where(used, old - rates[j, 0:1] * (update + 0.01 * old), 0.0)
        made[side, 0] = total
        made[side, 1] = jnp.where(used, new_first, 0.0)
        made[side, 2] = jnp.where(used, new_second, 0.0)
        made[side, 3] = new
        made_low[side] = new.astype(jnp.bfloat16)
        puts[turn] = [
            pltpu.make_async_copy(made.at[side, i], outs[i].at[j], osem.at[side, i])
            for i in range(4)
        ] + [pltpu.make_async_copy(made_low.at[side], outs[4].at[j], osem.at[side, 4])]
        for copy in puts[turn]:
            copy.start()

    ends = [j for j, s in ORDER_IN if s == 5]
    for turn in range(2):
        fetch(turn, ends[turn])
    turn = 0
    for j, s in ORDER_IN:
        if s == 0:
            exchange(j, 0, grads.at[1 - c, j], "c")
            continue
        if s == 1:
            loads[j].wait()
        copies[j, s - 1].wait_recv()
        if s < 5:
            add(j, s - 1)
            send(j, s)
        else:
            finish(turn, j)
            if turn < 6:
                fetch(turn + 2, ends[turn + 2])
            turn += 1
    for copy in puts[6] + puts[7]:
        copy.wait()
    for copy in copies.values():
        copy.wait_send()


def scatter(grads, first, second, left, right, master, rates):
    bf, wide, block = jnp.bfloat16, jnp.float32, (BLOCK, BLOCK)
    anywhere = pl.BlockSpec(memory_space=pl.ANY)
    return pl.pallas_call(
        scatter_kernel,
        out_shape=[jax.ShapeDtypeStruct((8,) + block, kind) for kind in (wide,) * 4 + (bf,)],
        in_specs=[anywhere] * 6 + [pl.BlockSpec(memory_space=pltpu.VMEM)],
        out_specs=[anywhere] * 5,
        scratch_shapes=[pltpu.VMEM((8, count) + block, bf) for count in (16, 16, 8, 4, 2, 1)]
        + [
            pltpu.VMEM((2, 5) + block, wide),
            pltpu.VMEM((2, 4) + block, wide),
            pltpu.VMEM((2,) + block, bf),
            pltpu.SemaphoreType.DMA((8,)),
            pltpu.SemaphoreType.DMA((8, 5)),
            pltpu.SemaphoreType.DMA((8, 5)),
            pltpu.SemaphoreType.DMA((2, 5)),
            pltpu.SemaphoreType.DMA((2, 5)),
        ],
        compiler_params=pltpu.CompilerParams(
            collective_id=12, has_side_effects=True, vmem_limit_bytes=VLIM
        ),
    )(grads, first, second, left, right, master, rates)


highest = lax.Precision.HIGHEST
moment_decay = 0.5
LOW = jnp.bfloat16
ROOM = 32 * 1024 * 1024
WIDE = jnp.float32

def shapes_list():
    return [(D, D), (DIMG, D), (DIMG, D), (D, D), (D, D), (D, D), (D, D), (D, D), (D, FF), (FF, D)]


Q_CROSS, K_CROSS, V_CROSS, O_CROSS, Q_SELF, K_SELF, V_SELF, O_SELF, W_UP, W_DOWN = (
    int(v) for v in np.cumsum([0] + [a * b // BLOCK**2 for a, b in shapes_list()])[:10]
)


NBLK = W_DOWN + FF * D // BLOCK**2


def weight_scales():
    self_root = (2.0 * TOK_DEV) ** 0.5
    cross_root = (IMG_MAX / 2.0) ** 0.5
    return [
        D ** (-0.5),
        DIMG ** (-0.5),
        DIMG ** (-0.5),
        0.5 * cross_root * D ** (-0.5),
        D ** (-0.5),
        D ** (-0.5),
        D ** (-0.5),
        0.5 * self_root * D ** (-0.5),
        D ** (-0.5),
        2.0 * FF ** (-0.5),
    ]


def block_table(scales):
    pieces = []
    for shape_pair, scale_value in zip(shapes_list(), scales):
        amount = shape_pair[0] * shape_pair[1] // (BLOCK * BLOCK)
        pieces.append(np.full((amount,), scale_value, np.float32))
    return np.concatenate(pieces)


def low(v):
    return v.astype(LOW)


def dot(a, b):
    return jnp.dot(a, b, preferred_element_type=WIDE)


def dot_nt(a, b):
    return lax.dot_general(a, b, (((1,), (1,)), ((), ())), preferred_element_type=WIDE)


def part(k):
    return slice(k * BLOCK, (k + 1) * BLOCK)


def norm_parts(values):
    centered = values - jnp.mean(values, axis=-1, keepdims=True)
    variance = jnp.mean(centered * centered, axis=-1, keepdims=True)
    return centered, lax.rsqrt(variance + 1e-06)


def modulated_norm(values, shift, scale):
    centered, inverse = norm_parts(values)
    return centered * inverse * (1.0 + scale) + shift


def norm_back(values, scale, grad_normed):
    centered, inverse = norm_parts(values)
    unit = centered * inverse
    grad_unit = grad_normed * (1.0 + scale)
    return inverse * (
        grad_unit
        - jnp.mean(grad_unit, axis=-1, keepdims=True)
        - unit * jnp.mean(grad_unit * unit, axis=-1, keepdims=True)
    )


def halves(pair):
    lane = lax.broadcasted_iota(jnp.int32, pair.shape, 1)
    zero = jnp.zeros_like(pair)
    return jnp.where(lane < HEAD, pair, zero), jnp.where(lane < HEAD, zero, pair)


def fill_valid(valid, where, parts):
    cap = valid.shape[0] // parts
    slot = lax.broadcasted_iota(jnp.int32, (cap, 128), 0)
    for i in range(parts):
        number = slot * parts + where[2 * NBLK + 2 + i]
        valid[i * cap : (i + 1) * cap] = (number < where[2 * NBLK + 1]).astype(WIDE)


def of_row(shifts, where, k):
    return shifts[k, pl.ds(where[2 * NBLK], 1)]


def masked(scores, valid):
    if valid is None:
        return scores
    wide = jnp.concatenate([valid] * (scores.shape[1] // valid.shape[1]), axis=1)
    return jnp.where(wide > 0.0, scores, -1e30)


def columns(base, tall, wide):
    return [
        pl.BlockSpec((1, BLOCK, BLOCK), lambda n, where, i=i: (where[base + i * wide + n], 0, 0))
        for i in range(tall)
    ]


def rows(base, wide):
    return [
        pl.BlockSpec((1, BLOCK, BLOCK), lambda n, where, k=k: (where[base + n * wide + k], 0, 0))
        for k in range(wide)
    ]


def whole(shape, mode=None):
    return pl.BlockSpec(shape, lambda n, where: (0,) * len(shape), pipeline_mode=mode)


def stripe(height):
    return pl.BlockSpec((height, BLOCK), lambda n, where: (0, n))


def stacked(blocks, axis):
    return jnp.concatenate([block[0] for block in blocks], axis=axis)


def by_columns(left, blocks):
    return dot(left[...], stacked(blocks, 0))


def by_rows(left, blocks):
    return dot_nt(left[...], stacked(blocks, 1))


def attend_part(queries, keys, values_turned, weights, valid, count):
    outs, tops, totals, scores = [], [], [], []
    for pair in range(2):
        lanes = slice(pair * 2 * HEAD, (pair + 1) * 2 * HEAD)
        key_pair = keys[:count, lanes]
        for query in halves(queries[:, lanes]):
            scores.append(masked(dot_nt(key_pair, query), valid))
    for head in range(4):
        top = jnp.max(scores[head], axis=0, keepdims=True)
        exponent = jnp.exp(scores[head] - top)
        weights[head, :count] = low(exponent)
        tops.append(top)
        totals.append(jnp.sum(exponent, axis=0, keepdims=True))
    for head in range(4):
        outs.append(dot(values_turned[head * HEAD : (head + 1) * HEAD], weights[head]))
    return outs, tops, totals


def attend_end(outs, tops, totals):
    turned = jnp.concatenate([out / total for out, total in zip(outs, totals)], axis=0)
    logs = [top + jnp.log(total) for top, total in zip(tops, totals)]
    return low(turned.T), jnp.concatenate(logs + logs, axis=0)


def attend_back(queries, keys, values, keys_turned, mixed, grad_mixed, logs, probs, grads, valid, count):
    tokens = queries.shape[0]
    inner = (mixed.astype(WIDE) * grad_mixed.astype(WIDE)).T
    grad_query, grad_key, grad_value = [], [], []
    for pair in range(2):
        lanes = slice(pair * 2 * HEAD, (pair + 1) * 2 * HEAD)
        key_pair, value_pair = keys[:count, lanes], values[:count, lanes]
        query_halves = halves(queries[:, lanes])
        mixed_halves = halves(grad_mixed[:, lanes])
        scores = [masked(dot_nt(key_pair, query), valid) for query in query_halves]
        grad_full = [dot_nt(value_pair, mix) for mix in mixed_halves]
        for which in range(2):
            head = pair * 2 + which
            own = slice(head * HEAD, (head + 1) * HEAD)
            side = slice(which * tokens, (which + 1) * tokens)
            full = jnp.exp(scores[which] - logs[head : head + 1])
            back = low(full * (grad_full[which] - jnp.sum(inner[own], axis=0, keepdims=True)))
            probs[pair, :count, side] = low(full)
            grads[pair, :count, side] = back
        for which in range(2):
            head = pair * 2 + which
            own = slice(head * HEAD, (head + 1) * HEAD)
            side = slice(which * tokens, (which + 1) * tokens)
            grad_query.append(dot(keys_turned[own], grads[pair, :, side]))
        grad_key.append(dot(grads[pair, :count], jnp.concatenate(query_halves, axis=0)))
        grad_value.append(dot(probs[pair, :count], jnp.concatenate(mixed_halves, axis=0)))
    grad_query = jnp.concatenate(grad_query, axis=0).T * HEAD ** (-0.5)
    return grad_query, jnp.concatenate(grad_key, axis=1), jnp.concatenate(grad_value, axis=1)


def send_blocks(stage, sems, side, store, where, numbers):
    return [
        pltpu.make_async_copy(stage.at[side, i], store.at[where[NBLK + number]], sems.at[side, i])
        for i, number in enumerate(numbers)
    ]


def keep_blocks(products, stage, sems, store, where, numbers):
    step, steps = pl.program_id(0), pl.num_programs(0)
    side = lax.rem(step, 2)

    @pl.when(step >= 2)
    def reuse():
        for copy in send_blocks(stage, sems, side, store, where, numbers):
            copy.wait()

    for i, product in enumerate(products()):
        stage[side, i] = product
    for copy in send_blocks(stage, sems, side, store, where, numbers):
        copy.start()

    @pl.when(step == steps - 1)
    def drain():
        for copy in send_blocks(stage, sems, 1 - side, store, where, numbers):
            copy.wait()
        for copy in send_blocks(stage, sems, side, store, where, numbers):
            copy.wait()


def cross_forward_kernel(parts, where, x, n1, tokens, shifts, *rest):
    q, k, v, o = rest[:4], rest[4:7], rest[7:10], rest[10:14]
    cq, ck, cv, co, logs, x1, n2, total, turned, weights, valid = rest[14:]
    n = pl.program_id(0)
    count = tokens.shape[0]

    @pl.when(n == 0)
    def first():
        total[...] = x[...].astype(WIDE)
        turned[count:] = jnp.zeros_like(turned[count:])
        for head in range(4):
            weights[head, count:] = jnp.zeros_like(weights[head, count:])
        fill_valid(valid, where, parts)

    queries = low(by_columns(n1, q)) * HEAD ** (-0.5)
    cq[...] = queries
    pair = low(dot(tokens[...], jnp.concatenate([stacked(k, 0), stacked(v, 0)], axis=1)))
    ck[...] = pair[:, :BLOCK]
    cv[...] = pair[:, BLOCK:]
    turned[:count] = pair[:, BLOCK:]
    mixed, log_total = attend_end(
        *attend_part(queries, ck, turned[...].T, weights, valid[...], count)
    )
    co[...] = mixed
    logs[0] = log_total
    total[...] += dot(mixed, stacked(o, 1))

    @pl.when(n == 3)
    def last():
        after = total[...]
        x1[...] = after
        n2[...] = low(modulated_norm(after, of_row(shifts, where, 2), of_row(shifts, where, 3)))


def self_own_kernel(where, mine, *rest):
    q, k, v = rest[:4], rest[4:8], rest[8:12]
    turned, sq, sk, sv, mix, stats, weights = rest[12:]
    n = pl.program_id(0)

    @pl.when(n == 0)
    def first():
        turned[...] = mine[...].T

    all_three = low(
        dot(mine[...], jnp.concatenate([stacked(q, 0), stacked(k, 0), stacked(v, 0)], axis=1))
    )
    queries = all_three[:, :BLOCK] * HEAD ** (-0.5)
    sq[...] = queries
    sk[...] = all_three[:, BLOCK : 2 * BLOCK]
    sv[...] = all_three[:, 2 * BLOCK :]
    outs, tops, totals = attend_part(queries, sk, sv[...].T, weights, None, mine.shape[0])
    mix[...] = jnp.concatenate(outs, axis=0)
    stats[0] = jnp.concatenate(tops + totals, axis=0)


def self_other_kernel(where, x1, other, shifts, sq, mix, stats, *rest):
    k, v, o = rest[:4], rest[4:8], rest[8:12]
    turned, sk, sv, so, logs, x2, n3, total, weights = rest[12:]
    n = pl.program_id(0)

    @pl.when(n == 0)
    def first():
        turned[...] = other[...].T
        total[...] = x1[...]

    pair = low(dot(other[...], jnp.concatenate([stacked(k, 0), stacked(v, 0)], axis=1)))
    sk[...] = pair[:, :BLOCK]
    sv[...] = pair[:, BLOCK:]
    parts = attend_part(sq[...], sk, sv[...].T, weights, None, other.shape[0])
    outs, tops, totals = [], [], []
    for head, (out, top, amount) in enumerate(zip(*parts)):
        old_top, old_amount = stats[0, head : head + 1], stats[0, 4 + head : 5 + head]
        new_top = jnp.maximum(top, old_top)
        grow, keep = jnp.exp(top - new_top), jnp.exp(old_top - new_top)
        outs.append(out * grow + mix[head * HEAD : (head + 1) * HEAD] * keep)
        tops.append(new_top)
        totals.append(amount * grow + old_amount * keep)
    mixed, logs[0] = attend_end(outs, tops, totals)
    so[...] = mixed
    total[...] += dot(mixed, stacked(o, 1))

    @pl.when(n == 3)
    def last():
        after = total[...]
        x2[...] = after
        n3[...] = low(modulated_norm(after, of_row(shifts, where, 4), of_row(shifts, where, 5)))


def grid_of(blocks, across):
    return jnp.concatenate(
        [stacked(blocks[i : i + across], 1) for i in range(0, len(blocks), across)], axis=0
    )


def feed_early_kernel(where, cotangent, *rest):
    down, grad_act = rest[:16], rest[16]
    grad_act[...] = dot_nt(cotangent[...], grid_of(down, 4))


def feed_kernel(where, x2, n3, cotangent, shifts, grad_act, *rest):
    up, down = rest[:8], rest[8:16]
    layer_out, g2, act, eh, total, back = rest[16:]
    f = pl.program_id(0)

    @pl.when(f == 0)
    def first():
        total[...] = x2[...]
        back[...] = jnp.zeros_like(back)

    up = grid_of(up, 2)
    hidden = dot(n3[...], up)
    square = hidden * hidden
    root = (2.0 / np.pi) ** 0.5
    bent = jnp.tanh(root * (hidden + 0.044715 * (square * hidden)))
    act[...] = low(0.5 * hidden * (1.0 + bent))
    slope = 0.5 * (1.0 + bent) + 0.5 * hidden * (1.0 - bent * bent) * (
        root * (1.0 + 3.0 * 0.044715 * square)
    )
    eh[...] = low(grad_act[...] * slope)
    total[...] += dot(act[...], grid_of(down, 4))
    back[...] += dot_nt(eh[...], up)

    @pl.when(f == FF // BLOCK // 2 - 1)
    def last():
        layer_out[...] = low(total[...])
        g2[...] = cotangent[...].astype(WIDE) + norm_back(x2[...], of_row(shifts, where, 5), back[...])


def feed_late_kernel(where, n3, cotangent, act, eh, store, turned, stage, sems):
    f = pl.program_id(0)
    wide = FF // BLOCK

    @pl.when(f == 0)
    def first():
        turned[...] = n3[...].T

    def products():
        up = low(dot(turned[...], eh[...]))
        down = low(dot(act[...].T, cotangent[...]))
        return [up[part(i), part(j)] for j in range(2) for i in range(4)] + [
            down[part(j), part(i)] for j in range(2) for i in range(4)
        ]

    numbers = [W_UP + i * wide + f * 2 + j for j in range(2) for i in range(4)]
    numbers += [W_DOWN + (f * 2 + j) * 4 + i for j in range(2) for i in range(4)]
    keep_blocks(products, stage, sems, store, where, numbers)


def self_backward_kernel(where, g2, sq, k_own, k_other, v_own, v_other, so, logs, *rest):
    q, k, v, o = rest[:4], rest[4:8], rest[8:12], rest[12:16]
    own_back, other_back, dq, dk, dv, es, probs, grads, sk, sv, own_total, other_total = rest[16:]
    n = pl.program_id(0)
    here = g2.shape[0]
    both = 2 * here

    @pl.when(n == 0)
    def first():
        es[...] = low(g2[...])
        own_total[...] = jnp.zeros_like(own_total)
        other_total[...] = jnp.zeros_like(other_total)

    grad_mixed = low(by_rows(es, o))
    sk[:here] = k_own[...]
    sk[here:] = k_other[...]
    sv[:here] = v_own[...]
    sv[here:] = v_other[...]
    wide_dq, wide_dk, wide_dv = attend_back(
        sq, sk, sv, sk[...].T, so[...], grad_mixed, logs[0], probs, grads, None, both
    )
    dq[...] = low(wide_dq)
    dk[...] = low(wide_dk)
    dv[...] = low(wide_dv)
    key_values = jnp.concatenate([stacked(k, 0), stacked(v, 0)], axis=1)
    both_grads = jnp.concatenate([dk[...], dv[...]], axis=1)
    own_total[...] += dot_nt(
        jnp.concatenate([dq[...], both_grads[:here]], axis=1),
        jnp.concatenate([stacked(q, 0), key_values], axis=1),
    )
    other_total[...] += dot_nt(both_grads[here:], key_values)

    @pl.when(n == 3)
    def last():
        own_back[...] = own_total[...]
        other_back[...] = low(other_total[...])


def self_late_kernel(where, g2, own_turned, other_turned, dq, dk, dv, so, old, store, es, turned, stage, sems):
    n = pl.program_id(0)
    here = g2.shape[0]

    @pl.when(n == 0)
    def first():
        es[...] = low(g2[...])
        turned[:, :here] = own_turned[...]
        turned[:, here:] = other_turned[...]

    def products():
        tall = [low(dot(own_turned[...], dq[...]))]
        tall += [low(dot(turned[...], grad[...])) for grad in (dk, dv)]
        flat = low(dot(so[...].T, es[...]))
        return [matrix[part(i)] for matrix in tall for i in range(4)] + [
            flat[:, part(i)] for i in range(4)
        ]

    numbers = [base + i * 4 + n for base in (Q_SELF, K_SELF, V_SELF) for i in range(4)]
    numbers += [O_SELF + n * 4 + i for i in range(4)]
    keep_blocks(products, stage, sems, store, where, numbers)


def cross_backward_kernel(
    parts, where, x, g2, x1, own_back, got_back, turned, shifts, normed_turned, cq, ck, cv, co, logs, *rest
):
    q, k, v, o = rest[:4], rest[4:7], rest[7:10], rest[10:14]
    grad_x, grad_tokens, store, ec, g1, probs, grads, x_total, keys_padded, rows_padded, valid, stage, sems = rest[15:]
    n = pl.program_id(0)
    count = ck.shape[0]

    @pl.when(n == 0)
    def first():
        value = g2[...] + norm_back(
            x1[...], of_row(shifts, where, 3), own_back[...] + got_back[...].astype(WIDE)
        )
        g1[...] = value
        ec[...] = low(value)
        x_total[...] = jnp.zeros_like(x_total)
        grad_tokens[...] = jnp.zeros_like(grad_tokens)
        keys_padded[count:] = jnp.zeros_like(keys_padded[count:])
        for i in range(2):
            grads[i, count:] = jnp.zeros_like(grads[i, count:])
            rows_padded[i, count:] = jnp.zeros_like(rows_padded[i, count:])
        fill_valid(valid, where, parts)

    grad_mixed = low(by_rows(ec, o))
    keys_padded[:count] = ck[...]
    dq, dk, dv = attend_back(
        cq, ck, cv, keys_padded[...].T, co[...], grad_mixed, logs[0], probs, grads, valid[...], count
    )
    dq = low(dq)
    rows_padded[0, :count] = low(dk)
    rows_padded[1, :count] = low(dv)
    x_total[...] += dot_nt(dq, stacked(q, 0))
    grad_tokens[...] += dot_nt(
        jnp.concatenate([rows_padded[0, :count], rows_padded[1, :count]], axis=1),
        jnp.concatenate([stacked(k, 0), stacked(v, 0)], axis=1),
    )

    def products():
        tall = [low(dot(normed_turned[...], dq))]
        tall += [low(dot(turned[...], rows_padded[side])) for side in range(2)]
        flat = low(dot(co[...].T, ec[...]))
        return [matrix[part(i)] for matrix in tall for i in range(matrix.shape[0] // BLOCK)] + [
            flat[:, part(i)] for i in range(4)
        ]

    numbers = [Q_CROSS + i * 4 + n for i in range(4)]
    numbers += [base + i * 4 + n for base in (K_CROSS, V_CROSS) for i in range(3)]
    numbers += [O_CROSS + n * 4 + i for i in range(4)]
    keep_blocks(products, stage, sems, store, where, numbers)

    @pl.when(n == 3)
    def last():
        grad_x[...] = g1[...] + norm_back(x[...].astype(WIDE), of_row(shifts, where, 1), x_total[...])


def shape(*dims, kind=LOW):
    return jax.ShapeDtypeStruct(dims, kind)


def call(kernel, grid, where, ins, outs, scratch, products, aliases=None, room=ROOM):
    moved = BLOCK * BLOCK * 2 * grid * 16
    return pl.pallas_call(
        kernel,
        grid_spec=pltpu.PrefetchScalarGridSpec(
            num_scalar_prefetch=1,
            grid=(grid,),
            in_specs=[spec for _, spec in ins],
            out_specs=[spec for _, spec in outs],
            scratch_shapes=scratch,
        ),
        out_shape=[struct for struct, _ in outs],
        input_output_aliases=aliases or {},
        compiler_params=pltpu.CompilerParams(vmem_limit_bytes=room),
        cost_estimate=pl.CostEstimate(
            flops=int(2 * products), bytes_accessed=moved, transcendentals=0
        ),
    )(where, *[array for array, _ in ins])


def full(array):
    return (array, whole(array.shape, pl.Buffered(1)))


def of_object(modulation):
    return full(modulation)


def made(*dims, kind=LOW):
    return (shape(*dims, kind=kind), whole(dims))


def striped(height):
    return (shape(height, D), stripe(height))


LOG_SPEC = pl.BlockSpec((1, 8, TOK_DEV), lambda n, where: (n, 0, 0))
ANYWHERE = pl.BlockSpec(memory_space=pl.ANY)


def padded_to(count):
    return -(-count // 128) * 128


def cross_forward(where, store, x, n1, tokens, shifts, parts):
    here, count = x.shape[0], tokens.shape[0]
    padded = padded_to(count)
    specs = columns(Q_CROSS, 4, 4) + columns(K_CROSS, 3, 4) + columns(V_CROSS, 3, 4) + rows(O_CROSS, 4)
    return call(
        functools.partial(cross_forward_kernel, parts),
        4,
        where,
        [full(x), full(n1), full(tokens), of_object(shifts)] + [(store, spec) for spec in specs],
        [
            striped(here),
            striped(count),
            striped(count),
            striped(here),
            (shape(4, 8, here, kind=WIDE), LOG_SPEC),
            made(here, D, kind=WIDE),
            made(here, D),
        ],
        [
            pltpu.VMEM((here, D), WIDE),
            pltpu.VMEM((padded, BLOCK), LOW),
            pltpu.VMEM((4, padded, here), LOW),
            pltpu.VMEM((count, 128), WIDE),
        ],
        here * D * D * 12,
    )


def tall(here):
    return pl.BlockSpec((BLOCK, here), lambda n, where: (n, 0))


def self_own(where, store, mine):
    here = mine.shape[0]
    specs = columns(Q_SELF, 4, 4) + columns(K_SELF, 4, 4) + columns(V_SELF, 4, 4)
    return call(
        self_own_kernel,
        4,
        where,
        [full(mine)] + [(store, spec) for spec in specs],
        [
            made(D, here),
            striped(here),
            striped(here),
            striped(here),
            (shape(D, here, kind=WIDE), tall(here)),
            (shape(4, 8, here, kind=WIDE), LOG_SPEC),
        ],
        [pltpu.VMEM((4, here, here), LOW)],
        here * D * D * 6,
    )


def self_other(where, store, x1, other, shifts, sq, mix, stats):
    here = x1.shape[0]
    specs = columns(K_SELF, 4, 4) + columns(V_SELF, 4, 4) + rows(O_SELF, 4)
    return call(
        self_other_kernel,
        4,
        where,
        [full(x1), full(other), of_object(shifts), (sq, stripe(here)), (mix, tall(here)), (stats, LOG_SPEC)]
        + [(store, spec) for spec in specs],
        [
            made(D, here),
            striped(here),
            striped(here),
            striped(here),
            (shape(4, 8, here, kind=WIDE), LOG_SPEC),
            made(here, D, kind=WIDE),
            made(here, D),
        ],
        [pltpu.VMEM((here, D), WIDE), pltpu.VMEM((4, here, here), LOW)],
        here * D * D * 6,
    )


def feed_specs(height):
    wide = FF // BLOCK
    up = [
        pl.BlockSpec(
            (1, BLOCK, BLOCK),
            lambda n, where, i=i, j=j: (where[W_UP + i * wide + n * height + j], 0, 0),
        )
        for i in range(4)
        for j in range(height)
    ]
    down = [
        pl.BlockSpec(
            (1, BLOCK, BLOCK), lambda n, where, i=i: (where[W_DOWN + n * height * 4 + i], 0, 0)
        )
        for i in range(4 * height)
    ]
    return up, down


def broad(here, height):
    return pl.BlockSpec((here, height * BLOCK), lambda n, where: (0, n))


def feed_early(where, store, cotangent):
    here = cotangent.shape[0]
    return call(
        feed_early_kernel,
        FF // BLOCK // 4,
        where,
        [full(cotangent)] + [(store, spec) for spec in feed_specs(4)[1]],
        [(shape(here, FF, kind=WIDE), broad(here, 4))],
        [],
        here * D * FF,
    )[0]


def feed(where, store, x2, n3, cotangent, shifts, grad_act):
    here = x2.shape[0]
    up, down = feed_specs(2)
    return call(
        feed_kernel,
        FF // BLOCK // 2,
        where,
        [full(x2), full(n3), full(cotangent), of_object(shifts), (grad_act, broad(here, 2))]
        + [(store, spec) for spec in up + down],
        [
            made(here, D),
            made(here, D, kind=WIDE),
            (shape(here, FF), broad(here, 2)),
            (shape(here, FF), broad(here, 2)),
        ],
        [pltpu.VMEM((here, D), WIDE), pltpu.VMEM((here, D), WIDE)],
        here * D * FF * 3,
    )


def feed_late(where, n3, cotangent, act, eh, slots):
    here = n3.shape[0]
    return call(
        feed_late_kernel,
        FF // BLOCK // 2,
        where,
        [full(n3), full(cotangent), (act, broad(here, 2)), (eh, broad(here, 2))],
        [(shape(slots, BLOCK, BLOCK), ANYWHERE)],
        [
            pltpu.VMEM((D, here), LOW),
            pltpu.VMEM((2, 16, BLOCK, BLOCK), LOW),
            pltpu.SemaphoreType.DMA((2, 16)),
        ],
        here * D * FF * 2,
    )[0]


def self_backward(where, store, g2, sq, k_own, k_other, v_own, v_other, so, logs):
    here = g2.shape[0]
    specs = columns(Q_SELF, 4, 4) + columns(K_SELF, 4, 4) + columns(V_SELF, 4, 4) + rows(O_SELF, 4)
    ins = [full(g2)] + [(a, stripe(here)) for a in (sq, k_own, k_other, v_own, v_other, so)]
    ins += [(logs, LOG_SPEC)] + [(store, spec) for spec in specs]
    return call(
        self_backward_kernel,
        4,
        where,
        ins,
        [made(here, D, kind=WIDE), made(here, D), striped(here), striped(2 * here), striped(2 * here)],
        [
            pltpu.VMEM((here, D), LOW),
            pltpu.VMEM((2, 2 * here, 2 * here), LOW),
            pltpu.VMEM((2, 2 * here, 2 * here), LOW),
            pltpu.VMEM((2 * here, BLOCK), LOW),
            pltpu.VMEM((2 * here, BLOCK), LOW),
            pltpu.VMEM((here, D), WIDE),
            pltpu.VMEM((here, D), WIDE),
        ],
        here * D * D * 16,
    )


def self_late(where, grads, g2, own_turned, other_turned, dq, dk, dv, so):
    here = g2.shape[0]
    ins = [full(a) for a in (g2, own_turned, other_turned)]
    ins += [(a, stripe(a.shape[0])) for a in (dq, dk, dv, so)] + [(grads, ANYWHERE)]
    return call(
        self_late_kernel,
        4,
        where,
        ins,
        [(shape(*grads.shape), ANYWHERE)],
        [
            pltpu.VMEM((here, D), LOW),
            pltpu.VMEM((D, 2 * here), LOW),
            pltpu.VMEM((2, 16, BLOCK, BLOCK), LOW),
            pltpu.SemaphoreType.DMA((2, 16)),
        ],
        here * D * D * 6,
        {len(ins): 0},
    )[0]


def cross_backward(
    where, store, grads, x, g2, x1, own_back, got_back, turned, shifts, normed_turned, cq, ck, cv, co, logs, parts
):
    here, count = x.shape[0], ck.shape[0]
    padded = padded_to(count)
    specs = columns(Q_CROSS, 4, 4) + columns(K_CROSS, 3, 4) + columns(V_CROSS, 3, 4) + rows(O_CROSS, 4)
    ins = [full(a) for a in (x, g2, x1, own_back, got_back, turned)]
    ins += [of_object(shifts), full(normed_turned)]
    ins += [(a, stripe(a.shape[0])) for a in (cq, ck, cv, co)] + [(logs, LOG_SPEC)]
    ins += [(store, spec) for spec in specs] + [(grads, ANYWHERE)]
    return call(
        functools.partial(cross_backward_kernel, parts),
        4,
        where,
        ins,
        [made(here, D, kind=WIDE), made(count, DIMG, kind=WIDE), (shape(*grads.shape), ANYWHERE)],
        [
            pltpu.VMEM((here, D), LOW),
            pltpu.VMEM((here, D), WIDE),
            pltpu.VMEM((2, padded, 2 * here), LOW),
            pltpu.VMEM((2, padded, 2 * here), LOW),
            pltpu.VMEM((here, D), WIDE),
            pltpu.VMEM((padded, BLOCK), LOW),
            pltpu.VMEM((2, padded, BLOCK), LOW),
            pltpu.VMEM((count, 128), WIDE),
            pltpu.VMEM((2, 14, BLOCK, BLOCK), LOW),
            pltpu.SemaphoreType.DMA((2, 14)),
        ],
        here * D * D * 24,
        {len(ins): 2},
        room=40 * 1024 * 1024,
    )


def partner(block, axis):
    size = lax.axis_size(axis)
    return lax.ppermute(block, axis, [(i, i ^ 1) for i in range(size)])


def soap_update(
    slot_grads,
    first_moment,
    second_moment,
    left_basis,
    right_basis,
    master_weights,
    slot_rates,
    slot_used,
):
    keep_mask = slot_used[:, None, None] > 0.0
    slot_grads = jnp.where(keep_mask, slot_grads, 0.0)
    rotated = jnp.matmul(
        jnp.matmul(jnp.swapaxes(left_basis, 1, 2), slot_grads, precision=highest),
        right_basis,
        precision=highest,
    )
    first_new = moment_decay * first_moment + (1.0 - moment_decay) * rotated
    second_new = moment_decay * second_moment + (1.0 - moment_decay) * rotated * rotated
    correction = 1.0 - moment_decay**STEP
    normalized = first_new / correction / (jnp.sqrt(second_new / correction) + 1e-08)
    rotated_back = jnp.matmul(
        jnp.matmul(left_basis, normalized, precision=highest),
        jnp.swapaxes(right_basis, 1, 2),
        precision=highest,
    )
    fresh_master = master_weights - slot_rates[:, None, None] * (
        rotated_back + 0.01 * master_weights
    )
    fresh_master = jnp.where(keep_mask, fresh_master, 0.0)
    return (
        slot_grads,
        jnp.where(keep_mask, first_new, 0.0),
        jnp.where(keep_mask, second_new, 0.0),
        fresh_master,
        fresh_master.astype(jnp.bfloat16),
    )


def shards(
    triplane,
    cotangent,
    image_tokens,
    modulation,
    image_counts,
    owner_slots,
    master_weights,
    first_moment,
    second_moment,
    left_basis,
    right_basis,
):
    img_size = lax.axis_size("img")
    rows_size = lax.axis_size("rows")
    img_index = lax.axis_index("img")
    flat_index = lax.axis_index("rows") * img_size + img_index
    object_index = flat_index // 2
    pair_index = img_index // 2
    groups = img_size // 2
    slot_cap = image_tokens.shape[0] // groups
    own_count = master_weights.shape[0]
    slot_total = rows_size * img_size * own_count
    fits = rows_size == 16 and img_size == 2 and own_count == 8
    modulation = jnp.swapaxes(modulation, 0, 1)
    info = [object_index[None], image_counts[object_index][None]]
    if img_size == 2:
        info += [img_index[None], 1 - img_index[None]]
    else:
        info += [jnp.arange(img_size, dtype=jnp.int32)]
    if fits:
        store, tokens, tokens_turned, n1, n1_turned = gather(
            master_weights, image_tokens, triplane, modulation
        )
        store = store.reshape(-1, BLOCK, BLOCK)
        where = [positions(owner_slots, WAYS_OUT), positions(owner_slots, WAYS_IN)]
    else:
        store = lax.all_gather(master_weights.astype(LOW), ("rows", "img"), axis=0, tiled=True)
        where = [owner_slots, owner_slots]
        if img_size == 2:
            tokens = jnp.concatenate([image_tokens, partner(image_tokens, "img")], 0)
        else:
            tokens = lax.all_gather(image_tokens, "img", axis=0, tiled=True)
            tokens = tokens.reshape(img_size, groups, slot_cap, DIMG)
            tokens = lax.dynamic_index_in_dim(tokens, pair_index, 1, keepdims=False)
            tokens = tokens.reshape(img_size * slot_cap, DIMG)
        count = tokens.shape[0]
        tokens_turned = jnp.pad(tokens.T, ((0, 0), (0, padded_to(count) - count)))
        shifts = lax.dynamic_index_in_dim(modulation, object_index, 1, keepdims=False)
        n1 = low(modulated_norm(triplane.astype(WIDE), shifts[0], shifts[1]))
        n1_turned = n1.T
    where = jnp.concatenate([piece.astype(jnp.int32) for piece in where + info])

    cq, ck, cv, co, cross_logs, x1, n2 = cross_forward(
        where, store, triplane, n1, tokens, modulation, img_size
    )
    n2_other = partner(n2, "img")
    own_turned, sq, k_own, v_own, mix, stats = self_own(where, store, n2)
    grad_act = feed_early(where, store, cotangent)
    other_turned, k_other, v_other, so, self_logs, x2, n3 = self_other(
        where, store, x1, n2_other, modulation, sq, mix, stats
    )
    layer_out, g2, act, eh = feed(where, store, x2, n3, cotangent, modulation, grad_act)
    own_back, other_back, dq, dk, dv = self_backward(
        where, store, g2, sq, k_own, k_other, v_own, v_other, so, self_logs
    )
    got_back = partner(other_back, "img")
    grads = feed_late(where, n3, cotangent, act, eh, slot_total)
    grads = self_late(where, grads, g2, own_turned, other_turned, dq, dk, dv, so)
    grad_triplane, grad_tokens, grads = cross_backward(
        where,
        store,
        grads,
        triplane,
        g2,
        x1,
        own_back,
        got_back,
        tokens_turned,
        modulation,
        n1_turned,
        cq,
        ck,
        cv,
        co,
        cross_logs,
        img_size,
    )
    if img_size == 2:
        grad_image = grad_tokens[:slot_cap] + partner(grad_tokens[slot_cap:].astype(LOW), "img").astype(WIDE)
    else:
        pick = (jnp.arange(groups, dtype=jnp.int32) == pair_index).astype(WIDE)
        spread = grad_tokens.reshape(img_size, 1, slot_cap, DIMG) * pick[None, :, None, None]
        grad_image = lax.psum_scatter(
            spread.reshape(img_size * groups * slot_cap, DIMG).astype(LOW),
            "img",
            scatter_dimension=0,
            tiled=True,
        ).astype(WIDE)
    my_slots = flat_index * own_count + jnp.arange(own_count, dtype=jnp.int32)
    matched = (owner_slots[:, None] == my_slots[None, :]).astype(WIDE)
    slot_used = jnp.sum(matched, axis=0)
    slot_rates = jnp.sum(matched * jnp.asarray(block_table(weight_scales()))[:, None], axis=0)
    state = (first_moment, second_moment, left_basis, right_basis, master_weights)
    if fits:
        rates = jnp.broadcast_to(
            jnp.stack([slot_rates, slot_used], 1)[:, :, None], (own_count, 2, BLOCK)
        )
        updated = scatter(grads.reshape(2, 8, 16, BLOCK, BLOCK), *state, rates)
    else:
        used = jnp.zeros((slot_total,), jnp.bool_).at[owner_slots].set(True)
        grads = jnp.where(used[:, None, None], grads, jnp.zeros_like(grads))
        slot_grads = lax.psum_scatter(
            grads, ("rows", "img"), scatter_dimension=0, tiled=True
        ).astype(WIDE)
        updated = soap_update(slot_grads, *state, slot_rates, slot_used)
    return (layer_out, grad_triplane, grad_image) + tuple(updated)


def solution(mesh):
    flat = P(("rows", "img"), None)
    blocks = P(("rows", "img"), None, None)
    in_specs = (flat, flat, flat, P(), P(), P()) + (blocks,) * 5
    out_specs = (flat, flat, flat) + (blocks,) * 5
    return jax.shard_map(shards, mesh=mesh, in_specs=in_specs, out_specs=out_specs, check_vma=False)
```

time: 581 us -> 532 us (0.916)
  waiting for transfers between devices: 37.2 us -> 0.91 us
  local copies, waits for them, and re-layouts: 9.31 us -> 28.3 us
  matrix products: 16.3 us -> 0 us
  Pallas kernels: 498 us -> 486 us
    ppermute x4 -> x3, waiting for transfers between devices: 37.2 us -> 0.91 us  [partner(): return lax.ppermute(block, axis, [(i, i ^ 1) for i in range(size)])]
    unnamed x32 -> x67, local copies, waits for them, and re-layouts: 3.61 us -> 23.2 us
    dot_general x4 -> x0, matrix products: 16.3 us -> none  [the longest x1 4.74 us: soap_update(): jnp.matmul(jnp.matmul(jnp.swapaxes(left_basis, 1, 2), slot_grads, precisi...]
    pallas_call x5 -> x9, Pallas kernels: 172 us -> 165 us  [call(): pl.pallas_call(kernel, grid_spec=pltpu.PrefetchScalarGridSpec(num_scalar_...]
  transfers between devices with their start and end apart: 4 -> 3, of which waited for: 2 -> 1; matrix products, arithmetic and copies ran while one was open for 4% -> 0% of each run, Pallas kernels for 57% -> 39%
where the time goes in v3:
time: 532 us; the launch traced here: 522 us
  Pallas kernels  486 us (91%)
  local copies, waits for them, and re-layouts  28.3 us (5%)
    pallas_call x9, Pallas kernels, call(): pl.pallas_call(kernel, grid_spec=pltpu.PrefetchScalarGridSpec(num_scalar_...  165 us
    pallas_call x1, Pallas kernels, scatter(): pl.pallas_call(scatter_kernel, out_shape=[jax.ShapeDtypeStruct((8,) + blo...  163 us
    pallas_call x1, Pallas kernels, gather(): pl.pallas_call(gather_kernel, out_shape=[jax.ShapeDtypeStruct((2, 8, 16,...  157 us
    unnamed x67, local copies, waits for them, and re-layouts  23.2 us
  transfers between devices with their start and end apart: 3, of which 1 were waited for; matrix products, arithmetic and copies ran while one was open for 0% of the time, Pallas kernels for 39%

profile of v3, /device:TPU:0, one launch (start us, length us, event | category | flops | bytes accessed | tf_op | source)
XLA Modules:
  0.0 521.8 jit_solution(6298518609179559559)
XLA Ops:
  1.5 1.2 dynamic_slice.3
  3.4 157.1 %shard_map.251 = (bf16[2,8,16,256,256]{4,3,2,1,0:T(8,128)(2,1)}, bf16[1040,768]{1,0:T(8,128)(2,1)}, bf16[768,1152]{1,0:T(8,128)(2,1)}, bf16[384,1024]{1,0:T(8,128)(2,1)}, bf16[1024,384]{1,0:T(8,128)(2,1)}) custom-call(f32[8,256,256]{2,1,0:T(8,128)} %master.3, bf16[520,768]{1,0:T(8,128)(2,1)} %tokens.1, bf16[384,1024]{1,0:T(8,128)(2,1)} %x.3, ...), custom_call_target="tpu_custom_call" | custom-call | tf_op jit(solution)/shard_map/pallas_call | solution.py:191
  161.3 1.4 copy-done.12
  162.7 1.1 copy-done.22
  163.8 23.0 %shard_map.252 = (bf16[384,1024]{1,0:T(8,128)(2,1)S(1)}, bf16[1040,1024]{1,0:T(8,128)(2,1)S(1)}, bf16[1040,1024]{1,0:T(8,128)(2,1)S(1)}, bf16[384,1024]{1,0:T(8,...) custom-call(s32[500]{0:T(512)S(1)} %concatenate.3.where, ...), custom_call_target="tpu_custom_call" | custom-call | flops 9663676416 | bytes 8388608 | tf_op jit(solution)/shard_map/pallas_call | solution.py:858
  186.8 1.3 copy-done.10
  188.7 7.8 %shard_map.255.grad_act = f32[384,4096]{1,0:T(8,128)S(1)} custom-call(s32[500]{0:T(512)S(1)} %concatenate.3.where, bf16[384,1024]{1,0:T(8,128)(2,1)S(1)} %copy-done.2, bf16[256,256,256]{2,1,0:T(8,128)(2,1)} %bitcast.32, bf16[256,256,256]{2,1,0:T(8,128)(2,1)} %bitcast.41, bf16[256,256,256]{2,1,0:T(8,128)(2,1)} %bitcast.28, bf16[256,256,256]{2,1,0:T(8,128)(2,1)} %bitcast.29, ...), custom_call_target="tpu_custom_call" | custom-call | flops 3221225472 | bytes 8388608 | tf_op jit(solution)/shard_map/pallas_call | solution.py:858
  196.5 10.1 %shard_map.253 = (bf16[1024,384]{1,0:T(8,128)(2,1)S(1)}, bf16[384,1024]{1,0:T(8,128)(2,1)S(1)}, bf16[384,1024]{1,0:T(8,128)(2,1)S(1)}, bf16[384,1024]{1,0:T(8,12...) custom-call(s32[500]{0:T(512)S(1)} %concatenate.3.where, bf16[384,1024]{1,0:T(8,128)(2,1)} %get-tuple-element.54.mine, ...), custom_call_target="tpu_custom_call" | custom-call | flops 4831838208 | bytes 8388608 | tf_op jit(solution)/shard_map/pallas_call | solution.py:858
  207.4 0.9 collective-permute-done.other
  208.4 12.3 %shard_map.254 = (bf16[1024,384]{1,0:T(8,128)(2,1)S(1)}, bf16[384,1024]{1,0:T(8,128)(2,1)S(1)}, bf16[384,1024]{1,0:T(8,128)(2,1)S(1)}, bf16[384,1024]{1,0:T(8,12...) custom-call(s32[500]{0:T(512)S(1)} %concatenate.3.where, ...), custom_call_target="tpu_custom_call" | custom-call | flops 4831838208 | bytes 8388608 | tf_op jit(solution)/shard_map/pallas_call | solution.py:858
  221.6 0.9 copy-done.18
  222.5 22.7 %shard_map.256 = (bf16[384,1024]{1,0:T(8,128)(2,1)}, f32[384,1024]{1,0:T(8,128)S(1)}, bf16[384,4096]{1,0:T(8,128)(2,1)S(1)}, bf16[384,4096]{1,0:T(8,128)(2,1)S(1)}) custom-call(s32[500]{0:T(512)S(1)} %concatenate.3.where, f32[384,1024]{1,0:T(8,128)S(1)} %get-tuple-element.58.x2, bf16[384,1024]{1,0:T(8,128)(2,1)S(1)} %get-tuple-element.59.n3, ...), custom_call_target="tpu_custom_call" | custom-call | flops 9663676416 | bytes 16777216 | tf_op jit(solution)/shard_map/pallas_call | solution.py:858
  245.2 1.7 copy-done.8
  246.9 1.1 copy-done.19
  248.0 1.1 copy-done.21
  249.1 22.5 %shard_map.257 = (f32[384,1024]{1,0:T(8,128)S(1)}, bf16[384,1024]{1,0:T(8,128)(2,1)S(1)}, bf16[384,1024]{1,0:T(8,128)(2,1)S(1)}, bf16[768,1024]{1,0:T(8,128)(2,1)S(1)}, bf16[768,1024]{1,0:T(8,128)(2,1)S(1)}) custom-call(s32[500]{0:T(512)S(1)} %concatenate.3.where, f32[384,1024]{1,0:T(8,128)S(1)} %get-tuple-element.61.g2, bf16[384,1024]{1,0:T(8,128)(2,1)S(1)} %copy-done.7, ...), custom_call_target="tpu_custom_call" | custom-call | flops 12884901888 | bytes 8388608 | tf_op jit(solution)/shard_map/pallas_call | solution.py:858
  272.3 1.9 copy-done.9
  274.2 13.6 %shard_map.258.old = bf16[256,256,256]{2,1,0:T(8,128)(2,1)} custom-call(s32[500]{0:T(512)S(1)} %concatenate.3.where, bf16[384,1024]{1,0:T(8,128)(2,1)S(1)} %get-tuple-element.59.n3, bf16[384,1024]{1,0:T(8,128)(2,1)S(1)} %copy-done.3, bf16[384,4096]{1,0:T(8,128)(2,1)S(1)} %copy-done.9, bf16[384,4096]{1,0:T(8,128)(2,1)S(1)} %get-tuple-element.83.eh), custom_call_target="tpu_custom_call" | custom-call | flops 6442450944 | bytes 16777216 | tf_op jit(solution)/shard_map/pallas_call | solution.py:858
  287.9 9.6 %shard_map.259.rest_14_ = bf16[256,256,256]{2,1,0:T(8,128)(2,1)} custom-call(s32[500]{0:T(512)S(1)} %concatenate.3.where, f32[384,1024]{1,0:T(8,128)S(1)} %get-tuple-element.61.g2, bf16[1024,384]{1,0:T(8,128)(2,1)S(1)} %get-tuple-element.77.own_turned, bf16[1024,384]{1,0:T(8,128)(2,1)S(1)} %copy-done.15, ...), custom_call_target="tpu_custom_call", output_to_operand_aliasing={{}: (8, {})} | custom-call | flops 4831838208 | bytes 8388608 | tf_op jit(solution)/shard_map/pallas_call | solution.py:858
  297.6 43.5 %shard_map.260 = (f32[384,1024]{1,0:T(8,128)}, f32[1040,768]{1,0:T(8,128)}, bf16[256,256,256]{2,1,0:T(8,128)(2,1)}) custom-call(s32[500]{0:T(512)S(1)} %concatenate.3.where, bf16[384,1024]{1,0:T(8,128)(2,1)S(1)} %copy-done.1, f32[384,1024]{1,0:T(8,128)S(1)} %get-tuple-element.61.g2, f32[384,1024]{1,0:T(8,128)S(1)} %copy-done.5, ...), custom_call_target="tpu_custom_call", output_to_operand_aliasing={{2}: (28, {})} | custom-call | flops 19327352832 | bytes 8388608 | tf_op jit(solution)/shard_map/pallas_call | solution.py:858
  341.1 2.4 slice.84
  343.5 1.4 collective-permute-start.2
  345.8 163.4 %shard_map.261 = (f32[8,256,256]{2,1,0:T(8,128)}, f32[8,256,256]{2,1,0:T(8,128)}, f32[8,256,256]{2,1,0:T(8,128)}, f32[8,256,256]{2,1,0:T(8,128)}, bf16[8,256,256]{2,1,0:T(8,128)(2,1)}) custom-call(bf16[2,8,16,256,256]{4,3,2,1,0:T(8,128)(2,1)} %bitcast.112, f32[8,256,256]{2,1,0:T(8,128)} %first.1, f32[8,256,256]{2,1,0:T(8,128)} %second.1, ...), custom_call_target="tpu_custom_call" | custom-call | tf_op jit(solution)/shard_map/pallas_call | solution.py:343
  509.3 1.3 convert_add_fusion
  511.4 1.3 copy.39
  512.7 1.0 copy-done.25
  513.7 1.3 copy.40
  515.1 1.0 copy-done.24
  516.1 1.3 copy.41
  517.4 1.0 copy-done.23
  518.4 1.3 copy.42
  520.4 1.0 copy.43
  (63 shorter events, 7.7 us)
Async XLA Ops:
  0.6 160.6 %copy-start.1 = (bf16[384,1024]{1,0:T(8,128)(2,1)S(1)}, bf16[384,1024]{1,0:T(8,128)(2,1)}, u32[]{:S(2)}) copy-start(bf16[384,1024]{1,0:T(8,128)(2,1)} %x.3) | copy-start | bytes 2359300
  0.6 160.6 %copy-start = (f32[16,6,1024]{2,0,1:T(8,128)S(1)}, f32[16,6,1024]{2,0,1:T(8,128)}, u32[]{:S(2)}) copy-start(f32[16,6,1024]{2,0,1:T(8,128)} %param.23) | copy-start | bytes 1179652
  161.2 1.4 copy-start.12
  162.7 1.1 copy-start.22
  163.8 24.9 %copy-start.2 = (bf16[384,1024]{1,0:T(8,128)(2,1)S(1)}, bf16[384,1024]{1,0:T(8,128)(2,1)}, u32[]{:S(2)}) copy-start(bf16[384,1024]{1,0:T(8,128)(2,1)} %cotangent.5) | copy-start | bytes 2359300
  186.8 1.4 copy-start.10
  188.1 20.2 %copy-start.4 = (f32[384,1024]{1,0:T(8,128)}, f32[384,1024]{1,0:T(8,128)S(1)}, u32[]{:S(2)}) copy-start(f32[384,1024]{1,0:T(8,128)S(1)} %get-tuple-element.53.x1) | copy-start | bytes 4718596
  188.1 20.2 %collective-permute-start = (bf16[384,1024]{1,0:T(8,128)(2,1)}, bf16[384,1024]{1,0:T(8,128)(2,1)}, u32[]{:S(2)}, u32[]{:S(2)}) collective-permute-start(bf16[384,1024]{1,0:T(8,128)(2,1)} %get-tuple-element.54.mine), channel_id=1, source_target_pairs={{0,1},{1,0},{2,3},{3,2},{4,5},{5,4},{6,7},{7,6},{8,9},{9,8},{10,11... | collective-permute-start | bytes 2359304 | tf_op jit(solution)/shard_map/ppermute | solution.py:1130
  206.6 0.9 copy-start.16
  207.4 13.3 %copy-start.6 = (bf16[384,1024]{1,0:T(8,128)(2,1)}, bf16[384,1024]{1,0:T(8,128)(2,1)S(1)}, u32[]{:S(2)}) copy-start(bf16[384,1024]{1,0:T(8,128)(2,1)S(1)} %get-tuple-element.55.sq) | copy-start | bytes 2359300
  208.4 14.1 %copy-start.3 = (bf16[384,1024]{1,0:T(8,128)(2,1)S(1)}, bf16[384,1024]{1,0:T(8,128)(2,1)}, u32[]{:S(2)}) copy-start(bf16[384,1024]{1,0:T(8,128)(2,1)} %cotangent.5) | copy-start | bytes 2359300
  222.5 22.7 %copy-start.20 = (bf16[384,1024]{1,0:T(8,128)(2,1)}, bf16[384,1024]{1,0:T(8,128)(2,1)S(1)}, u32[]{:S(2)}) copy-start(bf16[384,1024]{1,0:T(8,128)(2,1)S(1)} %get-tuple-element.65.v_other) | copy-start | bytes 2359300
  222.5 24.4 %copy-start.7 = (bf16[384,1024]{1,0:T(8,128)(2,1)S(1)}, bf16[384,1024]{1,0:T(8,128)(2,1)}, u32[]{:S(2)}) copy-start(bf16[384,1024]{1,0:T(8,128)(2,1)} %copy-done.6) | copy-start | bytes 2359300
  222.5 24.4 %copy-start.17 = (bf16[384,1024]{1,0:T(8,128)(2,1)S(1)}, bf16[384,1024]{1,0:T(8,128)(2,1)}, u32[]{:S(2)}) copy-start(bf16[384,1024]{1,0:T(8,128)(2,1)} %copy-done.16) | copy-start | bytes 2359300
  245.2 1.7 copy-start.8
  246.9 1.1 copy-start.19
  248.0 1.1 copy-start.21
  271.6 25.9 %collective-permute-start.1 = (bf16[384,1024]{1,0:T(8,128)(2,1)S(1)}, bf16[384,1024]{1,0:T(8,128)(2,1)S(1)}, u32[]{:S(2)}, u32[]{:S(2)}) collective-permute-start(bf16[384,1024]{1,0:T(8,128)(2,1)S(1)} %get-tuple-element.69), channel_id=1, source_target_pairs={{0,1},{1,0},{2,3},{3,2},{4,5},{5,4},{6,7},{7,6},{8,9},{9,8},{10,11... | collective-permute-start | bytes 2359304 | tf_op jit(solution)/shard_map/ppermute | solution.py:1130
  272.3 1.9 copy-start.9
  274.2 13.6 %copy-start.15 = (bf16[1024,384]{1,0:T(8,128)(2,1)S(1)}, bf16[1024,384]{1,0:T(8,128)(2,1)}, u32[]{:S(2)}) copy-start(bf16[1024,384]{1,0:T(8,128)(2,1)} %copy-done.14) | copy-start | bytes 2359300
  287.9 9.6 %copy-start.5 = (f32[384,1024]{1,0:T(8,128)S(1)}, f32[384,1024]{1,0:T(8,128)}, u32[]{:S(2)}) copy-start(f32[384,1024]{1,0:T(8,128)} %copy-done.4) | copy-start | bytes 4718596
  287.9 9.6 %copy-start.11 = (bf16[768,1152]{1,0:T(8,128)(2,1)S(1)}, bf16[768,1152]{1,0:T(8,128)(2,1)}, u32[]{:S(2)}) copy-start(bf16[768,1152]{1,0:T(8,128)(2,1)} %get-tuple-element.70.turned) | copy-start | bytes 5308420
  287.9 9.6 %copy-start.13 = (bf16[1024,384]{1,0:T(8,128)(2,1)S(1)}, bf16[1024,384]{1,0:T(8,128)(2,1)}, u32[]{:S(2)}) copy-start(bf16[1024,384]{1,0:T(8,128)(2,1)} %get-tuple-element.71.normed_turned) | copy-start | bytes 2359300
  297.5 47.3 %copy-start.29 = (s32[248]{0:T(256)S(1)}, s32[248]{0:T(256)}, u32[]{:S(2)}) copy-start(s32[248]{0:T(256)} %param.25) | copy-start | bytes 2980
  297.6 47.3 %copy-start.30 = (f32[248]{0:T(256)S(1)}, f32[248]{0:T(256)}, u32[]{:S(2)}) copy-start(f32[248]{0:T(256)} %constant.163.clone) | copy-start | bytes 2980
  343.5 165.8 %collective-permute-start.2 = (bf16[520,768]{1,0:T(8,128)(2,1)}, bf16[520,768]{1,0:T(8,128)(2,1)S(1)}, u32[]{:S(2)}, u32[]{:S(2)}) collective-permute-start(bf16[520,768]{1,0:T(8,128)(2,1)} %slice.84), channel_id=1, source_target_pairs={{0,1},{1,0},{2,3},{3,2},{4,5},{5,4},{6,7},{7,6},{8,9},{9,8},{10,11... | collective-permute-start | bytes 2396168 | tf_op jit(solution)/shard_map/ppermute | solution.py:1130
  345.8 163.4 %copy-start.27 = (f32[1040,768]{1,0:T(8,128)S(1)}, f32[1040,768]{1,0:T(8,128)}, u32[]{:S(2)}) copy-start(f32[1040,768]{1,0:T(8,128)} %get-tuple-element.85) | copy-start | bytes 9584644
  509.2 2.2 copy-start.26
  511.4 2.3 copy-start.25
  513.7 2.3 copy-start.24
  516.1 2.3 copy-start.23
  518.4 2.0 copy-start.28
  (2 other events, 1.8 us)

commit v4 on v3

--- a/solution.py
+++ b/solution.py
@@ -31,14 +31,14 @@
     ('hi', 'lo', 'y', 'x'),
 )
 WAYS_IN = (
-    ('hi', 'y', 'lo', 'x'),
+    ('lo', 'y', 'hi', 'x'),
+    ('hi', 'x', 'y', 'lo'),
+    ('hi', 'y', 'x', 'lo'),
+    ('hi', 'lo', 'x', 'y'),
     ('hi', 'x', 'lo', 'y'),
     ('hi', 'y', 'lo', 'x'),
-    ('hi', 'x', 'lo', 'y'),
-    ('hi', 'y', 'lo', 'x'),
-    ('hi', 'x', 'lo', 'y'),
-    ('hi', 'y', 'lo', 'x'),
-    ('hi', 'x', 'lo', 'y'),
+    ('hi', 'lo', 'x', 'y'),
+    ('lo', 'hi', 'y', 'x'),
 )
 FRONT = 17
 ORDER_OUT = (
@@ -51,11 +51,11 @@
 )
 ORDER_IN = (
     (0, 0), (1, 0), (2, 0), (3, 0), (4, 0), (5, 0), (6, 0), (7, 0),
-    (0, 1), (1, 1), (2, 1), (3, 1), (0, 2), (1, 2), (4, 1), (5, 1),
-    (2, 2), (3, 2), (0, 3), (1, 3), (6, 1), (7, 1), (4, 2), (5, 2),
-    (2, 3), (3, 3), (0, 4), (1, 4), (6, 2), (7, 2), (4, 3), (5, 3),
-    (2, 4), (3, 4), (0, 5), (1, 5), (6, 3), (7, 3), (4, 4), (5, 4),
-    (2, 5), (3, 5), (6, 4), (7, 4), (4, 5), (5, 5), (6, 5), (7, 5),
+    (1, 1), (0, 1), (4, 1), (0, 2), (7, 1), (4, 2), (6, 1), (2, 1),
+    (7, 2), (5, 1), (5, 2), (6, 2), (1, 2), (0, 3), (7, 3), (6, 3),
+    (1, 3), (3, 1), (1, 4), (4, 3), (7, 4), (2, 2), (4, 4), (2, 3),
+    (6, 4), (3, 2), (0, 4), (5, 3), (4, 5), (6, 5), (2, 4), (7, 5),
+    (3, 3), (2, 5), (5, 4), (1, 5), (0, 5), (5, 5), (3, 4), (3, 5),
 )
 
 
@@ -259,9 +259,7 @@
         start = lax.div(place(WAYS_IN[j]), count) * count if s else 0
 
         def body(b, carry):
-            own[j, start + b] = (
-                own[j, start + b].astype(jnp.float32) + got[s][j, b].astype(jnp.float32)
-            ).astype(jnp.bfloat16)
+            own[j, start + b] = own[j, start + b] + got[s][j, b]
             return carry
 
         lax.fori_loop(0, count, body, 0)
@@ -357,7 +355,7 @@
             pltpu.SemaphoreType.DMA((2, 5)),
         ],
         compiler_params=pltpu.CompilerParams(
-            collective_id=12, has_side_effects=True, vmem_limit_bytes=VLIM
+            collective_id=12, has_side_effects=True, vmem_limit_bytes=54 * 1024 * 1024
         ),
     )(grads, first, second, left, right, master, rates)
 
@@ -685,8 +683,8 @@
 
 
 def feed_kernel(where, x2, n3, cotangent, shifts, grad_act, *rest):
-    up, down = rest[:8], rest[8:16]
-    layer_out, g2, act, eh, total, back = rest[16:]
+    up, down = rest[:16], rest[16:32]
+    layer_out, g2, act, eh, total, back = rest[32:]
     f = pl.program_id(0)
 
     @pl.when(f == 0)
@@ -694,20 +692,21 @@
         total[...] = x2[...]
         back[...] = jnp.zeros_like(back)
 
-    up = grid_of(up, 2)
-    hidden = dot(n3[...], up)
-    square = hidden * hidden
     root = (2.0 / np.pi) ** 0.5
-    bent = jnp.tanh(root * (hidden + 0.044715 * (square * hidden)))
-    act[...] = low(0.5 * hidden * (1.0 + bent))
-    slope = 0.5 * (1.0 + bent) + 0.5 * hidden * (1.0 - bent * bent) * (
-        root * (1.0 + 3.0 * 0.044715 * square)
-    )
-    eh[...] = low(grad_act[...] * slope)
+    ups = [stacked(up[j::4], 0) for j in range(4)]
+    hiddens = [dot(n3[...], ups[j]) for j in range(4)]
+    for j, hidden in enumerate(hiddens):
+        square = hidden * hidden
+        bent = jnp.tanh(hidden * (root + (0.044715 * root) * square))
+        gate = 0.5 * bent + 0.5
+        value = hidden * gate
+        act[:, part(j)] = low(value)
+        slope = gate + value * (1.0 - gate) * (2.0 * root + (6.0 * 0.044715 * root) * square)
+        eh[:, part(j)] = low(grad_act[:, part(j)] * slope)
     total[...] += dot(act[...], grid_of(down, 4))
-    back[...] += dot_nt(eh[...], up)
-
-    @pl.when(f == FF // BLOCK // 2 - 1)
+    back[...] += dot_nt(eh[...], jnp.concatenate(ups, axis=1))
+
+    @pl.when(f == FF // BLOCK // 4 - 1)
     def last():
         layer_out[...] = low(total[...])
         g2[...] = cotangent[...].astype(WIDE) + norm_back(x2[...], of_row(shifts, where, 5), back[...])
@@ -782,12 +781,12 @@
         turned[:, here:] = other_turned[...]
 
     def products():
-        tall = [low(dot(own_turned[...], dq[...]))]
-        tall += [low(dot(turned[...], grad[...])) for grad in (dk, dv)]
+        query = low(dot(own_turned[...], dq[...]))
+        pair = low(dot(turned[...], jnp.concatenate([dk[...], dv[...]], axis=1)))
         flat = low(dot(so[...].T, es[...]))
-        return [matrix[part(i)] for matrix in tall for i in range(4)] + [
-            flat[:, part(i)] for i in range(4)
-        ]
+        blocks = [query[part(i)] for i in range(4)]
+        blocks += [pair[part(i), part(j)] for j in range(2) for i in range(4)]
+        return blocks + [flat[:, part(i)] for i in range(4)]
 
     numbers = [base + i * 4 + n for base in (Q_SELF, K_SELF, V_SELF) for i in range(4)]
     numbers += [O_SELF + n * 4 + i for i in range(4)]
@@ -798,7 +797,7 @@
     parts, where, x, g2, x1, own_back, got_back, turned, shifts, normed_turned, cq, ck, cv, co, logs, *rest
 ):
     q, k, v, o = rest[:4], rest[4:7], rest[7:10], rest[10:14]
-    grad_x, grad_tokens, store, ec, g1, probs, grads, x_total, keys_padded, rows_padded, valid, stage, sems = rest[15:]
+    grad_x, grad_own, grad_others, store, grad_tokens, ec, g1, probs, grads, x_total, keys_padded, rows_padded, valid, stage, sems = rest[15:]
     n = pl.program_id(0)
     count = ck.shape[0]
 
@@ -814,7 +813,7 @@
         keys_padded[count:] = jnp.zeros_like(keys_padded[count:])
         for i in range(2):
             grads[i, count:] = jnp.zeros_like(grads[i, count:])
-            rows_padded[i, count:] = jnp.zeros_like(rows_padded[i, count:])
+        rows_padded[count:] = jnp.zeros_like(rows_padded[count:])
         fill_valid(valid, where, parts)
 
     grad_mixed = low(by_rows(ec, o))
@@ -823,21 +822,21 @@
         cq, ck, cv, keys_padded[...].T, co[...], grad_mixed, logs[0], probs, grads, valid[...], count
     )
     dq = low(dq)
-    rows_padded[0, :count] = low(dk)
-    rows_padded[1, :count] = low(dv)
+    rows_padded[:count, :BLOCK] = low(dk)
+    rows_padded[:count, BLOCK:] = low(dv)
     x_total[...] += dot_nt(dq, stacked(q, 0))
     grad_tokens[...] += dot_nt(
-        jnp.concatenate([rows_padded[0, :count], rows_padded[1, :count]], axis=1),
+        rows_padded[:count],
         jnp.concatenate([stacked(k, 0), stacked(v, 0)], axis=1),
     )
 
     def products():
-        tall = [low(dot(normed_turned[...], dq))]
-        tall += [low(dot(turned[...], rows_padded[side])) for side in range(2)]
+        query = low(dot(normed_turned[...], dq))
+        pair = low(dot(turned[...], rows_padded[...]))
         flat = low(dot(co[...].T, ec[...]))
-        return [matrix[part(i)] for matrix in tall for i in range(matrix.shape[0] // BLOCK)] + [
-            flat[:, part(i)] for i in range(4)
-        ]
+        blocks = [query[part(i)] for i in range(4)]
+        blocks += [pair[part(i), part(j)] for j in range(2) for i in range(3)]
+        return blocks + [flat[:, part(i)] for i in range(4)]
 
     numbers = [Q_CROSS + i * 4 + n for i in range(4)]
     numbers += [base + i * 4 + n for base in (K_CROSS, V_CROSS) for i in range(3)]
@@ -846,6 +845,9 @@
 
     @pl.when(n == 3)
     def last():
+        half = grad_own.shape[0]
+        grad_own[...] = grad_tokens[:half]
+        grad_others[...] = low(grad_tokens[half:])
         grad_x[...] = g1[...] + norm_back(x[...].astype(WIDE), of_row(shifts, where, 1), x_total[...])
 
 
@@ -1011,18 +1013,18 @@
 
 def feed(where, store, x2, n3, cotangent, shifts, grad_act):
     here = x2.shape[0]
-    up, down = feed_specs(2)
+    up, down = feed_specs(4)
     return call(
         feed_kernel,
-        FF // BLOCK // 2,
+        FF // BLOCK // 4,
         where,
-        [full(x2), full(n3), full(cotangent), of_object(shifts), (grad_act, broad(here, 2))]
+        [full(x2), full(n3), full(cotangent), of_object(shifts), (grad_act, broad(here, 4))]
         + [(store, spec) for spec in up + down],
         [
             made(here, D),
             made(here, D, kind=WIDE),
-            (shape(here, FF), broad(here, 2)),
-            (shape(here, FF), broad(here, 2)),
+            (shape(here, FF), broad(here, 4)),
+            (shape(here, FF), broad(here, 4)),
         ],
         [pltpu.VMEM((here, D), WIDE), pltpu.VMEM((here, D), WIDE)],
         here * D * FF * 3,
@@ -1106,23 +1108,49 @@
         4,
         where,
         ins,
-        [made(here, D, kind=WIDE), made(count, DIMG, kind=WIDE), (shape(*grads.shape), ANYWHERE)],
         [
+            made(here, D, kind=WIDE),
+            made(count // parts, DIMG, kind=WIDE),
+            made(count - count // parts, DIMG),
+            (shape(*grads.shape), ANYWHERE),
+        ],
+        [
+            pltpu.VMEM((count, DIMG), WIDE),
             pltpu.VMEM((here, D), LOW),
             pltpu.VMEM((here, D), WIDE),
             pltpu.VMEM((2, padded, 2 * here), LOW),
             pltpu.VMEM((2, padded, 2 * here), LOW),
             pltpu.VMEM((here, D), WIDE),
             pltpu.VMEM((padded, BLOCK), LOW),
-            pltpu.VMEM((2, padded, BLOCK), LOW),
+            pltpu.VMEM((padded, 2 * BLOCK), LOW),
             pltpu.VMEM((count, 128), WIDE),
             pltpu.VMEM((2, 14, BLOCK, BLOCK), LOW),
             pltpu.SemaphoreType.DMA((2, 14)),
         ],
         here * D * D * 24,
-        {len(ins): 2},
+        {len(ins): 3},
         room=40 * 1024 * 1024,
     )
+
+
+def hand_on_kernel(*refs):
+    count = len(refs) // 2
+    for source, target in zip(refs[:count], refs[count:]):
+        target[...] = source[...]
+
+
+def hand_on(arrays):
+    specs = [
+        pl.BlockSpec((a.shape[0] // 4,) + a.shape[1:], lambda i: (i, 0, 0)) for a in arrays
+    ]
+    return pl.pallas_call(
+        hand_on_kernel,
+        grid=(4,),
+        out_shape=[jax.ShapeDtypeStruct(a.shape, a.dtype) for a in arrays],
+        in_specs=specs,
+        out_specs=specs,
+        compiler_params=pltpu.CompilerParams(vmem_limit_bytes=VLIM),
+    )(*arrays)
 
 
 def partner(block, axis):
@@ -1238,7 +1266,7 @@
     got_back = partner(other_back, "img")
     grads = feed_late(where, n3, cotangent, act, eh, slot_total)
     grads = self_late(where, grads, g2, own_turned, other_turned, dq, dk, dv, so)
-    grad_triplane, grad_tokens, grads = cross_backward(
+    grad_triplane, grad_own, grad_others, grads = cross_backward(
         where,
         store,
         grads,
@@ -1258,9 +1286,10 @@
         img_size,
     )
     if img_size == 2:
-        grad_image = grad_tokens[:slot_cap] + partner(grad_tokens[slot_cap:].astype(LOW), "img").astype(WIDE)
+        grad_image = grad_own + partner(grad_others, "img").astype(WIDE)
     else:
         pick = (jnp.arange(groups, dtype=jnp.int32) == pair_index).astype(WIDE)
+        grad_tokens = jnp.concatenate([grad_own, grad_others.astype(WIDE)], 0)
         spread = grad_tokens.reshape(img_size, 1, slot_cap, DIMG) * pick[None, :, None, None]
         grad_image = lax.psum_scatter(
             spread.reshape(img_size * groups * slot_cap, DIMG).astype(LOW),
@@ -1277,7 +1306,7 @@
         rates = jnp.broadcast_to(
             jnp.stack([slot_rates, slot_used], 1)[:, :, None], (own_count, 2, BLOCK)
         )
-        updated = scatter(grads.reshape(2, 8, 16, BLOCK, BLOCK), *state, rates)
+        updated = hand_on(scatter(grads.reshape(2, 8, 16, BLOCK, BLOCK), *state, rates))
     else:
         used = jnp.zeros((slot_total,), jnp.bool_).at[owner_slots].set(True)
         grads = jnp.where(used[:, None, None], grads, jnp.zeros_like(grads))

time: 532 us -> 514 us (0.966)
  local copies, waits for them, and re-layouts: 28.3 us -> 12 us
    unnamed x67 -> x44, local copies, waits for them, and re-layouts: 23.2 us -> 9.28 us
    pallas_call x0 -> x1, Pallas kernels: none -> 7.5 us  [hand_on(): pl.pallas_call(hand_on_kernel, grid=(4,), out_shape=[jax.ShapeDtypeStruct...]
    pallas_call x1, Pallas kernels: 163 us -> 157 us  [scatter(): pl.pallas_call(scatter_kernel, out_shape=[jax.ShapeDtypeStruct((8,) + blo...]
  transfers between devices with their start and end apart: 3 -> 3, of which waited for: 1 -> 1; matrix products, arithmetic and copies ran while one was open for 0% -> 0% of each run, Pallas kernels for 39% -> 41%
where the time goes in v4:
time: 514 us; the launch traced here: 504 us
  Pallas kernels  484 us (94%)
  local copies, waits for them, and re-layouts  12 us (2%)
    pallas_call x9, Pallas kernels, call(): pl.pallas_call(kernel, grid_spec=pltpu.PrefetchScalarGridSpec(num_scalar_...  162 us
    pallas_call x1, Pallas kernels, gather(): pl.pallas_call(gather_kernel, out_shape=[jax.ShapeDtypeStruct((2, 8, 16,...  157 us
    pallas_call x1, Pallas kernels, scatter(): pl.pallas_call(scatter_kernel, out_shape=[jax.ShapeDtypeStruct((8,) + blo...  157 us
  transfers between devices with their start and end apart: 3, of which 1 were waited for; matrix products, arithmetic and copies ran while one was open for 0% of the time, Pallas kernels for 41%

profile of v4, /device:TPU:0, one launch (start us, length us, event | category | flops | bytes accessed | tf_op | source)
XLA Modules:
  0.0 504.4 jit_solution(6140152285628805723)
XLA Ops:
  0.7 0.8 fusion.6
  1.5 1.2 dynamic_slice.3
  2.7 0.7 fusion.10
  3.4 157.0 %shard_map.251 = (bf16[2,8,16,256,256]{4,3,2,1,0:T(8,128)(2,1)}, bf16[1040,768]{1,0:T(8,128)(2,1)}, bf16[768,1152]{1,0:T(8,128)(2,1)}, bf16[384,1024]{1,0:T(8,128)(2,1)}, bf16[1024,384]{1,0:T(8,128)(2,1)}) custom-call(f32[8,256,256]{2,1,0:T(8,128)} %master.3, bf16[520,768]{1,0:T(8,128)(2,1)} %tokens.1, bf16[384,1024]{1,0:T(8,128)(2,1)} %x.3, ...), custom_call_target="tpu_custom_call" | custom-call | tf_op jit(solution)/shard_map/pallas_call | solution.py:191
  160.5 0.7 concatenate.3.where
  161.2 1.4 copy-done.13
  162.6 1.1 copy-done.19
  163.8 23.0 %shard_map.252 = (bf16[384,1024]{1,0:T(8,128)(2,1)S(1)}, bf16[1040,1024]{1,0:T(8,128)(2,1)S(1)}, bf16[1040,1024]{1,0:T(8,128)(2,1)S(1)}, bf16[384,1024]{1,0:T(8,...) custom-call(s32[500]{0:T(512)S(1)} %concatenate.3.where, ...), custom_call_target="tpu_custom_call" | custom-call | flops 9663676416 | bytes 8388608 | tf_op jit(solution)/shard_map/pallas_call | solution.py:860
  186.8 1.4 copy-done.10
  188.1 0.5 collective-permute-start
  188.6 7.8 %shard_map.255.grad_act = f32[384,4096]{1,0:T(8,128)S(1)} custom-call(s32[500]{0:T(512)S(1)} %concatenate.3.where, bf16[384,1024]{1,0:T(8,128)(2,1)S(1)} %copy-done.2, bf16[256,256,256]{2,1,0:T(8,128)(2,1)} %bitcast.38, bf16[256,256,256]{2,1,0:T(8,128)(2,1)} %bitcast.27, bf16[256,256,256]{2,1,0:T(8,128)(2,1)} %bitcast.28, bf16[256,256,256]{2,1,0:T(8,128)(2,1)} %bitcast.29, ...), custom_call_target="tpu_custom_call" | custom-call | flops 3221225472 | bytes 8388608 | tf_op jit(solution)/shard_map/pallas_call | solution.py:860
  196.5 10.1 %shard_map.253 = (bf16[1024,384]{1,0:T(8,128)(2,1)S(1)}, bf16[384,1024]{1,0:T(8,128)(2,1)S(1)}, bf16[384,1024]{1,0:T(8,128)(2,1)S(1)}, bf16[384,1024]{1,0:T(8,12...) custom-call(s32[500]{0:T(512)S(1)} %concatenate.3.where, bf16[384,1024]{1,0:T(8,128)(2,1)} %get-tuple-element.60.mine, ...), custom_call_target="tpu_custom_call" | custom-call | flops 4831838208 | bytes 8388608 | tf_op jit(solution)/shard_map/pallas_call | solution.py:860
  206.6 1.8 collective-permute-done.other
  208.4 12.3 %shard_map.254 = (bf16[1024,384]{1,0:T(8,128)(2,1)S(1)}, bf16[384,1024]{1,0:T(8,128)(2,1)S(1)}, bf16[384,1024]{1,0:T(8,128)(2,1)S(1)}, bf16[384,1024]{1,0:T(8,12...) custom-call(s32[500]{0:T(512)S(1)} %concatenate.3.where, ...), custom_call_target="tpu_custom_call" | custom-call | flops 4831838208 | bytes 8388608 | tf_op jit(solution)/shard_map/pallas_call | solution.py:860
  220.7 0.9 copy-done.15
  221.6 0.9 copy-done.17
  222.5 20.5 %shard_map.256 = (bf16[384,1024]{1,0:T(8,128)(2,1)}, f32[384,1024]{1,0:T(8,128)S(1)}, bf16[384,4096]{1,0:T(8,128)(2,1)S(1)}, bf16[384,4096]{1,0:T(8,128)(2,1)S(1)}) custom-call(s32[500]{0:T(512)S(1)} %concatenate.3.where, f32[384,1024]{1,0:T(8,128)S(1)} %get-tuple-element.64.x2, bf16[384,1024]{1,0:T(8,128)(2,1)S(1)} %get-tuple-element.65.n3, ...), custom_call_target="tpu_custom_call" | custom-call | flops 9663676416 | bytes 8388608 | tf_op jit(solution)/shard_map/pallas_call | solution.py:860
  243.0 1.6 copy-done.8
  244.7 22.5 %shard_map.257 = (f32[384,1024]{1,0:T(8,128)S(1)}, bf16[384,1024]{1,0:T(8,128)(2,1)S(1)}, bf16[384,1024]{1,0:T(8,128)(2,1)S(1)}, bf16[768,1024]{1,0:T(8,128)(2,1)S(1)}, bf16[768,1024]{1,0:T(8,128)(2,1)S(1)}) custom-call(s32[500]{0:T(512)S(1)} %concatenate.3.where, f32[384,1024]{1,0:T(8,128)S(1)} %get-tuple-element.67.g2, bf16[384,1024]{1,0:T(8,128)(2,1)S(1)} %copy-done.7, ...), custom_call_target="tpu_custom_call" | custom-call | flops 12884901888 | bytes 8388608 | tf_op jit(solution)/shard_map/pallas_call | solution.py:860
  267.2 0.6 collective-permute-start.1
  267.8 1.9 copy-done.9
  269.7 13.7 %shard_map.258.old = bf16[256,256,256]{2,1,0:T(8,128)(2,1)} custom-call(s32[500]{0:T(512)S(1)} %concatenate.3.where, bf16[384,1024]{1,0:T(8,128)(2,1)S(1)} %get-tuple-element.65.n3, bf16[384,1024]{1,0:T(8,128)(2,1)S(1)} %copy-done.3, bf16[384,4096]{1,0:T(8,128)(2,1)S(1)} %copy-done.9, bf16[384,4096]{1,0:T(8,128)(2,1)S(1)} %get-tuple-element.89.eh), custom_call_target="tpu_custom_call" | custom-call | flops 6442450944 | bytes 16777216 | tf_op jit(solution)/shard_map/pallas_call | solution.py:860
  283.4 9.6 %shard_map.259.rest_14_ = bf16[256,256,256]{2,1,0:T(8,128)(2,1)} custom-call(s32[500]{0:T(512)S(1)} %concatenate.3.where, f32[384,1024]{1,0:T(8,128)S(1)} %get-tuple-element.67.g2, bf16[1024,384]{1,0:T(8,128)(2,1)S(1)} %get-tuple-element.83.own_turned, bf16[1024,384]{1,0:T(8,128)(2,1)S(1)} %get-tuple-element.84.other_turned, ...), custom_call_target="tpu_custom_call", output_to_operand_aliasing={{}: (8, {})} | custom-call | flops 4831838208 | bytes 8388608 | tf_op jit(solution)/shard_map/pallas_call | solution.py:860
  293.1 0.0 copy-start.21
  293.1 42.9 %shard_map.260 = (f32[384,1024]{1,0:T(8,128)}, f32[520,768]{1,0:T(8,128)S(1)}, bf16[520,768]{1,0:T(8,128)(2,1)}, bf16[256,256,256]{2,1,0:T(8,128)(2,1)}) custom-call(s32[500]{0:T(512)S(1)} %concatenate.3.where, bf16[384,1024]{1,0:T(8,128)(2,1)S(1)} %copy-done.1, f32[384,1024]{1,0:T(8,128)S(1)} %get-tuple-element.67.g2, ...), custom_call_target="tpu_custom_call", output_to_operand_aliasing={{3}: (28, {})} | custom-call | flops 19327352832 | bytes 8388608 | tf_op jit(solution)/shard_map/pallas_call | solution.py:860
  336.0 1.6 collective-permute-start.2
  337.6 0.2 fusion
  337.8 0.1 copy.31
  337.8 0.7 broadcast_in_dim.11.rates
  338.5 156.7 %shard_map.261 = (f32[8,256,256]{2,1,0:T(8,128)}, f32[8,256,256]{2,1,0:T(8,128)}, f32[8,256,256]{2,1,0:T(8,128)}, f32[8,256,256]{2,1,0:T(8,128)}, bf16[8,256,256]{2,1,0:T(8,128)(2,1)}) custom-call(bf16[2,8,16,256,256]{4,3,2,1,0:T(8,128)(2,1)} %bitcast.128, f32[8,256,256]{2,1,0:T(8,128)} %first.1, f32[8,256,256]{2,1,0:T(8,128)} %second.1, ...), custom_call_target="tpu_custom_call" | custom-call | tf_op jit(solution)/shard_map/pallas_call | solution.py:341
  495.2 7.5 %shard_map.262 = (f32[8,256,256]{2,1,0:T(8,128)}, f32[8,256,256]{2,1,0:T(8,128)}, f32[8,256,256]{2,1,0:T(8,128)}, f32[8,256,256]{2,1,0:T(8,128)}, bf16[8,256,256]{2,1,0:T(8,128)(2,1)}) custom-call(f32[8,256,256]{2,1,0:T(8,128)} %get-tuple-element.94.refs_0_, f32[8,256,256]{2,1,0:T(8,128)} %get-tuple-element.95.refs_1_, ...), custom_call_target="tpu_custom_call" | custom-call | tf_op jit(solution)/shard_map/pallas_call | solution.py:1146
  502.7 1.3 convert_add_fusion
  (40 shorter events, 0.1 us)
Async XLA Ops:
  0.6 160.6 %copy-start.1 = (bf16[384,1024]{1,0:T(8,128)(2,1)S(1)}, bf16[384,1024]{1,0:T(8,128)(2,1)}, u32[]{:S(2)}) copy-start(bf16[384,1024]{1,0:T(8,128)(2,1)} %x.3) | copy-start | bytes 2359300
  0.6 160.6 %copy-start = (f32[16,6,1024]{2,0,1:T(8,128)S(1)}, f32[16,6,1024]{2,0,1:T(8,128)}, u32[]{:S(2)}) copy-start(f32[16,6,1024]{2,0,1:T(8,128)} %param.23) | copy-start | bytes 1179652
  161.2 1.4 copy-start.13
  162.6 1.1 copy-start.19
  163.8 24.9 %copy-start.2 = (bf16[384,1024]{1,0:T(8,128)(2,1)S(1)}, bf16[384,1024]{1,0:T(8,128)(2,1)}, u32[]{:S(2)}) copy-start(bf16[384,1024]{1,0:T(8,128)(2,1)} %cotangent.5) | copy-start | bytes 2359300
  186.8 1.4 copy-start.10
  188.1 8.3 %copy-start.11 = (bf16[1040,1024]{1,0:T(8,128)(2,1)}, bf16[1040,1024]{1,0:T(8,128)(2,1)S(1)}, u32[]{:S(2)}) copy-start(bf16[1040,1024]{1,0:T(8,128)(2,1)S(1)} %get-tuple-element.80.cv) | copy-start | bytes 6389764
  188.1 20.2 %copy-start.4 = (f32[384,1024]{1,0:T(8,128)}, f32[384,1024]{1,0:T(8,128)S(1)}, u32[]{:S(2)}) copy-start(f32[384,1024]{1,0:T(8,128)S(1)} %get-tuple-element.59.x1) | copy-start | bytes 4718596
  188.1 20.2 %collective-permute-start = (bf16[384,1024]{1,0:T(8,128)(2,1)}, bf16[384,1024]{1,0:T(8,128)(2,1)}, u32[]{:S(2)}, u32[]{:S(2)}) collective-permute-start(bf16[384,1024]{1,0:T(8,128)(2,1)} %get-tuple-element.60.mine), channel_id=1, source_target_pairs={{0,1},{1,0},{2,3},{3,2},{4,5},{5,4},{6,7},{7,6},{8,9},{9,8},{10,11... | collective-permute-start | bytes 2359304 | tf_op jit(solution)/shard_map/ppermute | solution.py:1158
  206.6 14.2 %copy-start.6 = (bf16[384,1024]{1,0:T(8,128)(2,1)}, bf16[384,1024]{1,0:T(8,128)(2,1)S(1)}, u32[]{:S(2)}) copy-start(bf16[384,1024]{1,0:T(8,128)(2,1)S(1)} %get-tuple-element.61.sq) | copy-start | bytes 2359300
  208.4 14.1 %copy-start.3 = (bf16[384,1024]{1,0:T(8,128)(2,1)S(1)}, bf16[384,1024]{1,0:T(8,128)(2,1)}, u32[]{:S(2)}) copy-start(bf16[384,1024]{1,0:T(8,128)(2,1)} %cotangent.5) | copy-start | bytes 2359300
  220.7 0.9 copy-start.15
  221.6 0.9 copy-start.17
  222.5 22.2 %copy-start.7 = (bf16[384,1024]{1,0:T(8,128)(2,1)S(1)}, bf16[384,1024]{1,0:T(8,128)(2,1)}, u32[]{:S(2)}) copy-start(bf16[384,1024]{1,0:T(8,128)(2,1)} %copy-done.6) | copy-start | bytes 2359300
  222.5 22.2 %copy-start.16 = (bf16[384,1024]{1,0:T(8,128)(2,1)S(1)}, bf16[384,1024]{1,0:T(8,128)(2,1)}, u32[]{:S(2)}) copy-start(bf16[384,1024]{1,0:T(8,128)(2,1)} %copy-done.15) | copy-start | bytes 2359300
  222.5 22.2 %copy-start.18 = (bf16[384,1024]{1,0:T(8,128)(2,1)S(1)}, bf16[384,1024]{1,0:T(8,128)(2,1)}, u32[]{:S(2)}) copy-start(bf16[384,1024]{1,0:T(8,128)(2,1)} %copy-done.17) | copy-start | bytes 2359300
  243.0 1.7 copy-start.8
  267.2 25.8 %collective-permute-start.1 = (bf16[384,1024]{1,0:T(8,128)(2,1)S(1)}, bf16[384,1024]{1,0:T(8,128)(2,1)S(1)}, u32[]{:S(2)}, u32[]{:S(2)}) collective-permute-start(bf16[384,1024]{1,0:T(8,128)(2,1)S(1)} %get-tuple-element.75), channel_id=1, source_target_pairs={{0,1},{1,0},{2,3},{3,2},{4,5},{5,4},{6,7},{7,6},{8,9},{9,8},{10,11... | collective-permute-start | bytes 2359304 | tf_op jit(solution)/shard_map/ppermute | solution.py:1158
  267.8 1.9 copy-start.9
  283.4 9.6 %copy-start.5 = (f32[384,1024]{1,0:T(8,128)S(1)}, f32[384,1024]{1,0:T(8,128)}, u32[]{:S(2)}) copy-start(f32[384,1024]{1,0:T(8,128)} %copy-done.4) | copy-start | bytes 4718596
  283.4 9.6 %copy-start.12 = (bf16[768,1152]{1,0:T(8,128)(2,1)S(1)}, bf16[768,1152]{1,0:T(8,128)(2,1)}, u32[]{:S(2)}) copy-start(bf16[768,1152]{1,0:T(8,128)(2,1)} %get-tuple-element.76.turned) | copy-start | bytes 5308420
  283.4 9.6 %copy-start.14 = (bf16[1024,384]{1,0:T(8,128)(2,1)S(1)}, bf16[1024,384]{1,0:T(8,128)(2,1)}, u32[]{:S(2)}) copy-start(bf16[1024,384]{1,0:T(8,128)(2,1)} %get-tuple-element.77.normed_turned) | copy-start | bytes 2359300
  293.1 44.5 %copy-start.20 = (s32[248]{0:T(256)S(1)}, s32[248]{0:T(256)}, u32[]{:S(2)}) copy-start(s32[248]{0:T(256)} %param.25) | copy-start | bytes 2980
  293.1 44.5 %copy-start.21 = (f32[248]{0:T(256)S(1)}, f32[248]{0:T(256)}, u32[]{:S(2)}) copy-start(f32[248]{0:T(256)} %constant.163.clone) | copy-start | bytes 2980
  336.0 166.7 %collective-permute-start.2 = (bf16[520,768]{1,0:T(8,128)(2,1)}, bf16[520,768]{1,0:T(8,128)(2,1)S(1)}, u32[]{:S(2)}, u32[]{:S(2)}) collective-permute-start(bf16[520,768]{1,0:T(8,128)(2,1)} %get-tuple-element.92), channel_id=1, source_target_pairs={{0,1},{1,0},{2,3},{3,2},{4,5},{5,4},{6,7},{7,6},{8,9},{9,8},{10,11... | collective-permute-start | bytes 2396168 | tf_op jit(solution)/shard_map/ppermute | solution.py:1158

commit v5 on v4

--- a/solution.py
+++ b/solution.py
@@ -21,14 +21,14 @@
 MESH = pl.DeviceIdType.MESH
 VLIM = 60 * 1024 * 1024
 WAYS_OUT = (
+    ('lo', 'hi', 'y', 'x'),
+    ('hi', 'lo', 'x', 'y'),
+    ('y', 'x', 'hi', 'lo'),
+    ('hi', 'lo', 'x', 'y'),
+    ('hi', 'x', 'lo', 'y'),
+    ('lo', 'y', 'hi', 'x'),
+    ('hi', 'y', 'lo', 'x'),
     ('hi', 'x', 'y', 'lo'),
-    ('lo', 'y', 'hi', 'x'),
-    ('y', 'hi', 'lo', 'x'),
-    ('hi', 'y', 'lo', 'x'),
-    ('lo', 'x', 'hi', 'y'),
-    ('x', 'hi', 'lo', 'y'),
-    ('hi', 'lo', 'x', 'y'),
-    ('hi', 'lo', 'y', 'x'),
 )
 WAYS_IN = (
     ('lo', 'y', 'hi', 'x'),
@@ -42,11 +42,11 @@
 )
 FRONT = 17
 ORDER_OUT = (
-    (-1, 0), (0, 0), (1, 0), (2, 0), (3, 0), (4, 0), (5, 0), (6, 0),
-    (7, 0), (6, 1), (7, 1), (4, 1), (1, 1), (0, 1), (4, 2), (3, 1),
-    (6, 2), (7, 2), (7, 3), (6, 3), (3, 2), (5, 1), (2, 1), (0, 2),
-    (5, 2), (1, 2), (3, 3), (4, 3), (1, 3), (2, 2), (6, 4), (2, 3),
-    (4, 4), (5, 3), (0, 3), (3, 4), (7, 4), (1, 4), (5, 4), (0, 4),
+    (6, 0), (2, 0), (2, 1), (0, 0), (5, 0), (3, 0), (6, 1), (-1, 0),
+    (3, 1), (1, 0), (5, 1), (4, 0), (1, 1), (3, 2), (4, 1), (0, 1),
+    (0, 2), (6, 2), (7, 0), (7, 1), (4, 2), (3, 3), (5, 2), (0, 3),
+    (7, 2), (3, 4), (1, 2), (7, 3), (6, 3), (5, 3), (2, 2), (4, 3),
+    (0, 4), (7, 4), (2, 3), (4, 4), (1, 3), (6, 4), (1, 4), (5, 4),
     (2, 4),
 )
 ORDER_IN = (
@@ -165,7 +165,7 @@
             )
             n1[...] = one.astype(jnp.bfloat16)
             n1_turned[...] = one.astype(jnp.bfloat16).T
-        if (j, k) == ORDER_OUT[FRONT + 6]:
+        if (j, k) == ORDER_OUT[min(max(FRONT + 6, ORDER_OUT.index((-1, 0)) + 9), len(ORDER_OUT) - 1)]:
             half = tokens.shape[0]
             cross.wait()
             early[1].wait()
@@ -363,7 +363,6 @@
 highest = lax.Precision.HIGHEST
 moment_decay = 0.5
 LOW = jnp.bfloat16
-ROOM = 32 * 1024 * 1024
 WIDE = jnp.float32
 
 def shapes_list():
@@ -451,8 +450,13 @@
     cap = valid.shape[0] // parts
     slot = lax.broadcasted_iota(jnp.int32, (cap, 128), 0)
     for i in range(parts):
-        number = slot * parts + where[2 * NBLK + 2 + i]
-        valid[i * cap : (i + 1) * cap] = (number < where[2 * NBLK + 1]).astype(WIDE)
+        number = slot * parts + where[2 * NBLK + 1 + i]
+        limit = where[2 * NBLK + 1 + parts + where[2 * NBLK]]
+        valid[i * cap : (i + 1) * cap] = (number < limit).astype(WIDE)
+
+
+def group(n, width):
+    return pl.ds(pl.multiple_of(n * width, width), width)
 
 
 def of_row(shifts, where, k):
@@ -501,20 +505,24 @@
 
 
 def attend_part(queries, keys, values_turned, weights, valid, count):
-    outs, tops, totals, scores = [], [], [], []
+    outs, tops, totals = [], [], []
+    tokens = queries.shape[0]
+    scores = []
     for pair in range(2):
         lanes = slice(pair * 2 * HEAD, (pair + 1) * 2 * HEAD)
-        key_pair = keys[:count, lanes]
-        for query in halves(queries[:, lanes]):
-            scores.append(masked(dot_nt(key_pair, query), valid))
-    for head in range(4):
-        top = jnp.max(scores[head], axis=0, keepdims=True)
-        exponent = jnp.exp(scores[head] - top)
-        weights[head, :count] = low(exponent)
-        tops.append(top)
-        totals.append(jnp.sum(exponent, axis=0, keepdims=True))
-    for head in range(4):
-        outs.append(dot(values_turned[head * HEAD : (head + 1) * HEAD], weights[head]))
+        both = jnp.concatenate(halves(queries[:, lanes]), axis=0)
+        scores.append(masked(dot_nt(keys[:count, lanes], both), valid))
+    for pair in range(2):
+        top = jnp.max(scores[pair], axis=0, keepdims=True)
+        exponent = jnp.exp(scores[pair] - top)
+        total = jnp.sum(exponent, axis=0, keepdims=True)
+        weights[pair, :count] = low(exponent)
+        tops += [top[:, :tokens], top[:, tokens:]]
+        totals += [total[:, :tokens], total[:, tokens:]]
+    for pair in range(2):
+        lanes = slice(pair * 2 * HEAD, (pair + 1) * 2 * HEAD)
+        mixed = dot(values_turned[lanes], weights[pair])
+        outs += [mixed[:HEAD, :tokens], mixed[HEAD:, tokens:]]
     return outs, tops, totals
 
 
@@ -527,29 +535,27 @@
 def attend_back(queries, keys, values, keys_turned, mixed, grad_mixed, logs, probs, grads, valid, count):
     tokens = queries.shape[0]
     inner = (mixed.astype(WIDE) * grad_mixed.astype(WIDE)).T
+    inner = jnp.concatenate(
+        [jnp.sum(inner[head * HEAD : (head + 1) * HEAD], axis=0, keepdims=True) for head in range(4)],
+        axis=1,
+    )
+    logs = jnp.concatenate([logs[head : head + 1] for head in range(4)], axis=1)
     grad_query, grad_key, grad_value = [], [], []
     for pair in range(2):
+        kept = pair % grads.shape[0]
         lanes = slice(pair * 2 * HEAD, (pair + 1) * 2 * HEAD)
-        key_pair, value_pair = keys[:count, lanes], values[:count, lanes]
-        query_halves = halves(queries[:, lanes])
-        mixed_halves = halves(grad_mixed[:, lanes])
-        scores = [masked(dot_nt(key_pair, query), valid) for query in query_halves]
-        grad_full = [dot_nt(value_pair, mix) for mix in mixed_halves]
-        for which in range(2):
-            head = pair * 2 + which
-            own = slice(head * HEAD, (head + 1) * HEAD)
-            side = slice(which * tokens, (which + 1) * tokens)
-            full = jnp.exp(scores[which] - logs[head : head + 1])
-            back = low(full * (grad_full[which] - jnp.sum(inner[own], axis=0, keepdims=True)))
-            probs[pair, :count, side] = low(full)
-            grads[pair, :count, side] = back
-        for which in range(2):
-            head = pair * 2 + which
-            own = slice(head * HEAD, (head + 1) * HEAD)
-            side = slice(which * tokens, (which + 1) * tokens)
-            grad_query.append(dot(keys_turned[own], grads[pair, :, side]))
-        grad_key.append(dot(grads[pair, :count], jnp.concatenate(query_halves, axis=0)))
-        grad_value.append(dot(probs[pair, :count], jnp.concatenate(mixed_halves, axis=0)))
+        side = slice(pair * 2 * tokens, (pair + 1) * 2 * tokens)
+        both_queries = jnp.concatenate(halves(queries[:, lanes]), axis=0)
+        both_mixed = jnp.concatenate(halves(grad_mixed[:, lanes]), axis=0)
+        scores = masked(dot_nt(keys[:count, lanes], both_queries), valid)
+        grad_full = dot_nt(values[:count, lanes], both_mixed)
+        full = jnp.exp(scores - logs[:, side])
+        grads[kept, :count] = low(full * (grad_full - inner[:, side]))
+        probs[kept, :count] = low(full)
+        turned = dot(keys_turned[lanes], grads[kept])
+        grad_query += [turned[:HEAD, :tokens], turned[HEAD:, tokens:]]
+        grad_key.append(dot(grads[kept, :count], both_queries))
+        grad_value.append(dot(probs[kept, :count], both_mixed))
     grad_query = jnp.concatenate(grad_query, axis=0).T * HEAD ** (-0.5)
     return grad_query, jnp.concatenate(grad_key, axis=1), jnp.concatenate(grad_value, axis=1)
 
@@ -585,16 +591,15 @@
 
 def cross_forward_kernel(parts, where, x, n1, tokens, shifts, *rest):
     q, k, v, o = rest[:4], rest[4:7], rest[7:10], rest[10:14]
-    cq, ck, cv, co, logs, x1, n2, total, turned, weights, valid = rest[14:]
+    cq, ck, cv, co, logs, x1, n2, all_mixed, all_out, turned, weights, valid = rest[14:]
     n = pl.program_id(0)
     count = tokens.shape[0]
 
     @pl.when(n == 0)
     def first():
-        total[...] = x[...].astype(WIDE)
         turned[count:] = jnp.zeros_like(turned[count:])
-        for head in range(4):
-            weights[head, count:] = jnp.zeros_like(weights[head, count:])
+        for pair in range(2):
+            weights[pair, count:] = jnp.zeros_like(weights[pair, count:])
         fill_valid(valid, where, parts)
 
     queries = low(by_columns(n1, q)) * HEAD ** (-0.5)
@@ -608,11 +613,12 @@
     )
     co[...] = mixed
     logs[0] = log_total
-    total[...] += dot(mixed, stacked(o, 1))
+    all_mixed[:, group(n, BLOCK)] = mixed
+    all_out[group(n, BLOCK)] = stacked(o, 1)
 
     @pl.when(n == 3)
     def last():
-        after = total[...]
+        after = x[...].astype(WIDE) + dot(all_mixed[...], all_out[...])
         x1[...] = after
         n2[...] = low(modulated_norm(after, of_row(shifts, where, 2), of_row(shifts, where, 3)))
 
@@ -640,13 +646,12 @@
 
 def self_other_kernel(where, x1, other, shifts, sq, mix, stats, *rest):
     k, v, o = rest[:4], rest[4:8], rest[8:12]
-    turned, sk, sv, so, logs, x2, n3, total, weights = rest[12:]
+    turned, sk, sv, so, logs, x2, n3, all_mixed, all_out, weights = rest[12:]
     n = pl.program_id(0)
 
     @pl.when(n == 0)
     def first():
         turned[...] = other[...].T
-        total[...] = x1[...]
 
     pair = low(dot(other[...], jnp.concatenate([stacked(k, 0), stacked(v, 0)], axis=1)))
     sk[...] = pair[:, :BLOCK]
@@ -662,11 +667,12 @@
         totals.append(amount * grow + old_amount * keep)
     mixed, logs[0] = attend_end(outs, tops, totals)
     so[...] = mixed
-    total[...] += dot(mixed, stacked(o, 1))
+    all_mixed[:, group(n, BLOCK)] = mixed
+    all_out[group(n, BLOCK)] = stacked(o, 1)
 
     @pl.when(n == 3)
     def last():
-        after = total[...]
+        after = x1[...] + dot(all_mixed[...], all_out[...])
         x2[...] = after
         n3[...] = low(modulated_norm(after, of_row(shifts, where, 4), of_row(shifts, where, 5)))
 
@@ -855,7 +861,7 @@
     return jax.ShapeDtypeStruct(dims, kind)
 
 
-def call(kernel, grid, where, ins, outs, scratch, products, aliases=None, room=ROOM):
+def call(kernel, grid, where, ins, outs, scratch, products, aliases=None, room=32):
     moved = BLOCK * BLOCK * 2 * grid * 16
     return pl.pallas_call(
         kernel,
@@ -868,7 +874,7 @@
         ),
         out_shape=[struct for struct, _ in outs],
         input_output_aliases=aliases or {},
-        compiler_params=pltpu.CompilerParams(vmem_limit_bytes=room),
+        compiler_params=pltpu.CompilerParams(vmem_limit_bytes=room * 1024 * 1024),
         cost_estimate=pl.CostEstimate(
             flops=int(2 * products), bytes_accessed=moved, transcendentals=0
         ),
@@ -918,12 +924,14 @@
             made(here, D),
         ],
         [
-            pltpu.VMEM((here, D), WIDE),
+            pltpu.VMEM((here, D), LOW),
+            pltpu.VMEM((D, D), LOW),
             pltpu.VMEM((padded, BLOCK), LOW),
-            pltpu.VMEM((4, padded, here), LOW),
+            pltpu.VMEM((2, padded, 2 * here), LOW),
             pltpu.VMEM((count, 128), WIDE),
         ],
         here * D * D * 12,
+        room=34,
     )
 
 
@@ -947,7 +955,7 @@
             (shape(D, here, kind=WIDE), tall(here)),
             (shape(4, 8, here, kind=WIDE), LOG_SPEC),
         ],
-        [pltpu.VMEM((4, here, here), LOW)],
+        [pltpu.VMEM((2, here, 2 * here), LOW)],
         here * D * D * 6,
     )
 
@@ -970,7 +978,7 @@
             made(here, D, kind=WIDE),
             made(here, D),
         ],
-        [pltpu.VMEM((here, D), WIDE), pltpu.VMEM((4, here, here), LOW)],
+        [pltpu.VMEM((here, D), LOW), pltpu.VMEM((D, D), LOW), pltpu.VMEM((2, here, 2 * here), LOW)],
         here * D * D * 6,
     )
 
@@ -1028,6 +1036,7 @@
         ],
         [pltpu.VMEM((here, D), WIDE), pltpu.VMEM((here, D), WIDE)],
         here * D * FF * 3,
+        room=32,
     )
 
 
@@ -1045,6 +1054,7 @@
             pltpu.SemaphoreType.DMA((2, 16)),
         ],
         here * D * FF * 2,
+        room=26,
     )[0]
 
 
@@ -1061,14 +1071,15 @@
         [made(here, D, kind=WIDE), made(here, D), striped(here), striped(2 * here), striped(2 * here)],
         [
             pltpu.VMEM((here, D), LOW),
-            pltpu.VMEM((2, 2 * here, 2 * here), LOW),
-            pltpu.VMEM((2, 2 * here, 2 * here), LOW),
+            pltpu.VMEM((1, 2 * here, 2 * here), LOW),
+            pltpu.VMEM((1, 2 * here, 2 * here), LOW),
             pltpu.VMEM((2 * here, BLOCK), LOW),
             pltpu.VMEM((2 * here, BLOCK), LOW),
             pltpu.VMEM((here, D), WIDE),
             pltpu.VMEM((here, D), WIDE),
         ],
         here * D * D * 16,
+        room=28,
     )
 
 
@@ -1090,6 +1101,7 @@
         ],
         here * D * D * 6,
         {len(ins): 0},
+        room=30,
     )[0]
 
 
@@ -1129,7 +1141,7 @@
         ],
         here * D * D * 24,
         {len(ins): 3},
-        room=40 * 1024 * 1024,
+        room=40,
     )
 
 
@@ -1222,11 +1234,12 @@
     slot_total = rows_size * img_size * own_count
     fits = rows_size == 16 and img_size == 2 and own_count == 8
     modulation = jnp.swapaxes(modulation, 0, 1)
-    info = [object_index[None], image_counts[object_index][None]]
+    info = [object_index[None]]
     if img_size == 2:
         info += [img_index[None], 1 - img_index[None]]
     else:
         info += [jnp.arange(img_size, dtype=jnp.int32)]
+    info += [image_counts]
     if fits:
         store, tokens, tokens_turned, n1, n1_turned = gather(
             master_weights, image_tokens, triplane, modulation

time: 514 us -> 506 us (0.984)
  local copies, waits for them, and re-layouts: 12 us -> 5.5 us
    pallas_call x1, Pallas kernels: 157 us -> 163 us  [scatter(): pl.pallas_call(scatter_kernel, out_shape=[jax.ShapeDtypeStruct((8,) + blo...]
  transfers between devices with their start and end apart: 3 -> 3, of which waited for: 1 -> 1; matrix products, arithmetic and copies ran while one was open for 0% -> 0% of each run, Pallas kernels for 41% -> 43%
where the time goes in v5:
time: 506 us; the launch traced here: 496 us
  Pallas kernels  483 us (95%)
  local copies, waits for them, and re-layouts  5.5 us (1%)
    pallas_call x1, Pallas kernels, scatter(): pl.pallas_call(scatter_kernel, out_shape=[jax.ShapeDtypeStruct((8,) + blo...  163 us
    pallas_call x9, Pallas kernels, call(): pl.pallas_call(kernel, grid_spec=pltpu.PrefetchScalarGridSpec(num_scalar_...  160 us
    pallas_call x1, Pallas kernels, gather(): pl.pallas_call(gather_kernel, out_shape=[jax.ShapeDtypeStruct((2, 8, 16,...  153 us
  transfers between devices with their start and end apart: 3, of which 1 were waited for; matrix products, arithmetic and copies ran while one was open for 0% of the time, Pallas kernels for 43%

profile of v5, /device:TPU:0, one launch (start us, length us, event | category | flops | bytes accessed | tf_op | source)
XLA Modules:
  0.0 496.0 jit_solution(1316264520242200115)
XLA Ops:
  0.6 0.0 copy-start.1
  0.7 0.8 fusion.6
  1.5 0.7 fusion.10
  2.2 152.9 %shard_map.251 = (bf16[2,8,16,256,256]{4,3,2,1,0:T(8,128)(2,1)}, bf16[1040,768]{1,0:T(8,128)(2,1)}, bf16[768,1152]{1,0:T(8,128)(2,1)}, bf16[384,1024]{1,0:T(8,128)(2,1)}, bf16[1024,384]{1,0:T(8,128)(2,1)}) custom-call(f32[8,256,256]{2,1,0:T(8,128)} %master.3, bf16[520,768]{1,0:T(8,128)(2,1)} %tokens.1, bf16[384,1024]{1,0:T(8,128)(2,1)} %x.3, ...), custom_call_target="tpu_custom_call" | custom-call | tf_op jit(solution)/shard_map/pallas_call | solution.py:191
  155.2 0.1 concatenate.3.where
  155.3 1.4 copy-done.13
  156.7 1.1 copy-done.19
  157.8 21.6 %shard_map.252 = (bf16[384,1024]{1,0:T(8,128)(2,1)S(1)}, bf16[1040,1024]{1,0:T(8,128)(2,1)S(1)}, bf16[1040,1024]{1,0:T(8,128)(2,1)S(1)}, bf16[384,1024]{1,0:T(8,...) custom-call(s32[515]{0:T(1024)S(1)} %concatenate.3.where, ...), custom_call_target="tpu_custom_call" | custom-call | flops 9663676416 | bytes 8388608 | tf_op jit(solution)/shard_map/pallas_call | solution.py:866
  179.4 0.1 collective-permute-start
  179.5 9.2 %shard_map.255.grad_act = f32[384,4096]{1,0:T(8,128)S(1)} custom-call(s32[515]{0:T(1024)S(1)} %concatenate.3.where, bf16[384,1024]{1,0:T(8,128)(2,1)S(1)} %copy-done.2, bf16[256,256,256]{2,1,0:T(8,128)(2,1)} %bitcast.38, bf16[256,256,256]{2,1,0:T(8,128)(2,1)} %bitcast.27, bf16[256,256,256]{2,1,0:T(8,128)(2,1)} %bitcast.28, bf16[256,256,256]{2,1,0:T(8,128)(2,1)} %bitcast.29, ...), custom_call_target="tpu_custom_call" | custom-call | flops 3221225472 | bytes 8388608 | tf_op jit(solution)/shard_map/pallas_call | solution.py:866
  188.7 10.2 %shard_map.253 = (bf16[1024,384]{1,0:T(8,128)(2,1)S(1)}, bf16[384,1024]{1,0:T(8,128)(2,1)S(1)}, bf16[384,1024]{1,0:T(8,128)(2,1)S(1)}, bf16[384,1024]{1,0:T(8,12...) custom-call(s32[515]{0:T(1024)S(1)} %concatenate.3.where, bf16[384,1024]{1,0:T(8,128)(2,1)} %get-tuple-element.60.mine, ...), custom_call_target="tpu_custom_call" | custom-call | flops 4831838208 | bytes 8388608 | tf_op jit(solution)/shard_map/pallas_call | solution.py:866
  199.0 0.0 copy-start.6
  199.0 0.7 collective-permute-done.other
  199.7 12.0 %shard_map.254 = (bf16[1024,384]{1,0:T(8,128)(2,1)S(1)}, bf16[384,1024]{1,0:T(8,128)(2,1)S(1)}, bf16[384,1024]{1,0:T(8,128)(2,1)S(1)}, bf16[384,1024]{1,0:T(8,12...) custom-call(s32[515]{0:T(1024)S(1)} %concatenate.3.where, ...), custom_call_target="tpu_custom_call" | custom-call | flops 4831838208 | bytes 8388608 | tf_op jit(solution)/shard_map/pallas_call | solution.py:866
  211.8 0.0 copy-start.8
  211.8 20.5 %shard_map.256 = (bf16[384,1024]{1,0:T(8,128)(2,1)}, f32[384,1024]{1,0:T(8,128)S(1)}, bf16[384,4096]{1,0:T(8,128)(2,1)S(1)}, bf16[384,4096]{1,0:T(8,128)(2,1)S(1)}) custom-call(s32[515]{0:T(1024)S(1)} %concatenate.3.where, f32[384,1024]{1,0:T(8,128)S(1)} %get-tuple-element.64.x2, bf16[384,1024]{1,0:T(8,128)(2,1)S(1)} %get-tuple-element.65.n3, ...), custom_call_target="tpu_custom_call" | custom-call | flops 9663676416 | bytes 8388608 | tf_op jit(solution)/shard_map/pallas_call | solution.py:866
  232.4 22.1 %shard_map.257 = (f32[384,1024]{1,0:T(8,128)S(1)}, bf16[384,1024]{1,0:T(8,128)(2,1)S(1)}, bf16[384,1024]{1,0:T(8,128)(2,1)S(1)}, bf16[768,1024]{1,0:T(8,128)(2,1)S(1)}, bf16[768,1024]{1,0:T(8,128)(2,1)S(1)}) custom-call(s32[515]{0:T(1024)S(1)} %concatenate.3.where, f32[384,1024]{1,0:T(8,128)S(1)} %get-tuple-element.67.g2, bf16[384,1024]{1,0:T(8,128)(2,1)S(1)} %copy-done.7, ...), custom_call_target="tpu_custom_call" | custom-call | flops 12884901888 | bytes 8388608 | tf_op jit(solution)/shard_map/pallas_call | solution.py:866
  254.5 0.4 collective-permute-start.1
  254.8 13.7 %shard_map.258.old = bf16[256,256,256]{2,1,0:T(8,128)(2,1)} custom-call(s32[515]{0:T(1024)S(1)} %concatenate.3.where, bf16[384,1024]{1,0:T(8,128)(2,1)S(1)} %copy-done.9, bf16[384,1024]{1,0:T(8,128)(2,1)S(1)} %copy-done.3, bf16[384,4096]{1,0:T(8,128)(2,1)S(1)} %get-tuple-element.88.act, bf16[384,4096]{1,0:T(8,128)(2,1)S(1)} %get-tuple-element.89.eh), custom_call_target="tpu_custom_call" | custom-call | flops 6442450944 | bytes 16777216 | tf_op jit(solution)/shard_map/pallas_call | solution.py:866
  268.5 0.0 copy-start.5
  268.6 9.9 %shard_map.259.rest_14_ = bf16[256,256,256]{2,1,0:T(8,128)(2,1)} custom-call(s32[515]{0:T(1024)S(1)} %concatenate.3.where, f32[384,1024]{1,0:T(8,128)S(1)} %get-tuple-element.67.g2, bf16[1024,384]{1,0:T(8,128)(2,1)S(1)} %get-tuple-element.83.own_turned, bf16[1024,384]{1,0:T(8,128)(2,1)S(1)} %get-tuple-element.84.other_turned, ...), custom_call_target="tpu_custom_call", output_to_operand_aliasing={{}: (8, {})} | custom-call | flops 4831838208 | bytes 8388608 | tf_op jit(solution)/shard_map/pallas_call | solution.py:866
  278.4 0.0 copy-start.17
  278.5 0.9 copy-done.17
  279.4 1.1 copy-done.18
  280.5 40.8 %shard_map.260 = (f32[384,1024]{1,0:T(8,128)}, f32[520,768]{1,0:T(8,128)S(1)}, bf16[520,768]{1,0:T(8,128)(2,1)}, bf16[256,256,256]{2,1,0:T(8,128)(2,1)}) custom-call(s32[515]{0:T(1024)S(1)} %concatenate.3.where, bf16[384,1024]{1,0:T(8,128)(2,1)S(1)} %copy-done.1, f32[384,1024]{1,0:T(8,128)S(1)} %get-tuple-element.67.g2, ...), custom_call_target="tpu_custom_call", output_to_operand_aliasing={{3}: (28, {})} | custom-call | flops 19327352832 | bytes 8388608 | tf_op jit(solution)/shard_map/pallas_call | solution.py:866
  321.3 1.8 collective-permute-start.2
  323.1 0.2 fusion
  323.3 0.1 copy.31
  323.4 0.7 broadcast_in_dim.11.rates
  324.1 162.7 %shard_map.261 = (f32[8,256,256]{2,1,0:T(8,128)}, f32[8,256,256]{2,1,0:T(8,128)}, f32[8,256,256]{2,1,0:T(8,128)}, f32[8,256,256]{2,1,0:T(8,128)}, bf16[8,256,256]{2,1,0:T(8,128)(2,1)}) custom-call(bf16[2,8,16,256,256]{4,3,2,1,0:T(8,128)(2,1)} %bitcast.128, f32[8,256,256]{2,1,0:T(8,128)} %first.1, f32[8,256,256]{2,1,0:T(8,128)} %second.1, ...), custom_call_target="tpu_custom_call" | custom-call | tf_op jit(solution)/shard_map/pallas_call | solution.py:341
  486.8 7.5 %shard_map.262 = (f32[8,256,256]{2,1,0:T(8,128)}, f32[8,256,256]{2,1,0:T(8,128)}, f32[8,256,256]{2,1,0:T(8,128)}, f32[8,256,256]{2,1,0:T(8,128)}, bf16[8,256,256]{2,1,0:T(8,128)(2,1)}) custom-call(f32[8,256,256]{2,1,0:T(8,128)} %get-tuple-element.94.refs_0_, f32[8,256,256]{2,1,0:T(8,128)} %get-tuple-element.95.refs_1_, ...), custom_call_target="tpu_custom_call" | custom-call | tf_op jit(solution)/shard_map/pallas_call | solution.py:1158
  494.3 1.3 convert_add_fusion
  (41 shorter events, 0.1 us)
Async XLA Ops:
  0.6 154.6 %copy-start.1 = (bf16[384,1024]{1,0:T(8,128)(2,1)S(1)}, bf16[384,1024]{1,0:T(8,128)(2,1)}, u32[]{:S(2)}) copy-start(bf16[384,1024]{1,0:T(8,128)(2,1)} %x.3) | copy-start | bytes 2359300
  0.6 154.6 %copy-start = (f32[16,6,1024]{2,0,1:T(8,128)S(1)}, f32[16,6,1024]{2,0,1:T(8,128)}, u32[]{:S(2)}) copy-start(f32[16,6,1024]{2,0,1:T(8,128)} %param.23) | copy-start | bytes 1179652
  0.7 154.5 %copy-start.22 = (s32[16]{0:T(128)S(1)}, s32[16]{0:T(128)}, u32[]{:S(2)}) copy-start(s32[16]{0:T(128)} %param.24) | copy-start | bytes 196
  155.3 1.4 copy-start.13
  156.7 1.1 copy-start.19
  157.8 21.7 %copy-start.2 = (bf16[384,1024]{1,0:T(8,128)(2,1)S(1)}, bf16[384,1024]{1,0:T(8,128)(2,1)}, u32[]{:S(2)}) copy-start(bf16[384,1024]{1,0:T(8,128)(2,1)} %cotangent.5) | copy-start | bytes 2359300
  179.4 9.3 %copy-start.10 = (bf16[1040,1024]{1,0:T(8,128)(2,1)}, bf16[1040,1024]{1,0:T(8,128)(2,1)S(1)}, u32[]{:S(2)}) copy-start(bf16[1040,1024]{1,0:T(8,128)(2,1)S(1)} %get-tuple-element.79.ck) | copy-start | bytes 6389764
  179.4 9.3 %copy-start.11 = (bf16[1040,1024]{1,0:T(8,128)(2,1)}, bf16[1040,1024]{1,0:T(8,128)(2,1)S(1)}, u32[]{:S(2)}) copy-start(bf16[1040,1024]{1,0:T(8,128)(2,1)S(1)} %get-tuple-element.80.cv) | copy-start | bytes 6389764
  179.4 9.3 %copy-start.15 = (bf16[384,1024]{1,0:T(8,128)(2,1)}, bf16[384,1024]{1,0:T(8,128)(2,1)S(1)}, u32[]{:S(2)}) copy-start(bf16[384,1024]{1,0:T(8,128)(2,1)S(1)} %get-tuple-element.81.co) | copy-start | bytes 2359300
  179.4 20.3 %copy-start.4 = (f32[384,1024]{1,0:T(8,128)}, f32[384,1024]{1,0:T(8,128)S(1)}, u32[]{:S(2)}) copy-start(f32[384,1024]{1,0:T(8,128)S(1)} %get-tuple-element.59.x1) | copy-start | bytes 4718596
  179.4 20.3 %collective-permute-start = (bf16[384,1024]{1,0:T(8,128)(2,1)}, bf16[384,1024]{1,0:T(8,128)(2,1)}, u32[]{:S(2)}, u32[]{:S(2)}) collective-permute-start(bf16[384,1024]{1,0:T(8,128)(2,1)} %get-tuple-element.60.mine), channel_id=1, source_target_pairs={{0,1},{1,0},{2,3},{3,2},{4,5},{5,4},{6,7},{7,6},{8,9},{9,8},{10,11... | collective-permute-start | bytes 2359304 | tf_op jit(solution)/shard_map/ppermute | solution.py:1170
  199.0 12.8 %copy-start.6 = (bf16[384,1024]{1,0:T(8,128)(2,1)}, bf16[384,1024]{1,0:T(8,128)(2,1)S(1)}, u32[]{:S(2)}) copy-start(bf16[384,1024]{1,0:T(8,128)(2,1)S(1)} %get-tuple-element.61.sq) | copy-start | bytes 2359300
  199.7 12.1 %copy-start.3 = (bf16[384,1024]{1,0:T(8,128)(2,1)S(1)}, bf16[384,1024]{1,0:T(8,128)(2,1)}, u32[]{:S(2)}) copy-start(bf16[384,1024]{1,0:T(8,128)(2,1)} %cotangent.5) | copy-start | bytes 2359300
  211.8 20.6 %copy-start.8 = (bf16[384,1024]{1,0:T(8,128)(2,1)}, bf16[384,1024]{1,0:T(8,128)(2,1)S(1)}, u32[]{:S(2)}) copy-start(bf16[384,1024]{1,0:T(8,128)(2,1)S(1)} %get-tuple-element.65.n3) | copy-start | bytes 2359300
  211.8 20.6 %copy-start.7 = (bf16[384,1024]{1,0:T(8,128)(2,1)S(1)}, bf16[384,1024]{1,0:T(8,128)(2,1)}, u32[]{:S(2)}) copy-start(bf16[384,1024]{1,0:T(8,128)(2,1)} %copy-done.6) | copy-start | bytes 2359300
  232.4 22.4 %copy-start.9 = (bf16[384,1024]{1,0:T(8,128)(2,1)S(1)}, bf16[384,1024]{1,0:T(8,128)(2,1)}, u32[]{:S(2)}) copy-start(bf16[384,1024]{1,0:T(8,128)(2,1)} %copy-done.8) | copy-start | bytes 2359300
  254.5 24.0 %collective-permute-start.1 = (bf16[384,1024]{1,0:T(8,128)(2,1)S(1)}, bf16[384,1024]{1,0:T(8,128)(2,1)S(1)}, u32[]{:S(2)}, u32[]{:S(2)}) collective-permute-start(bf16[384,1024]{1,0:T(8,128)(2,1)S(1)} %get-tuple-element.75), channel_id=1, source_target_pairs={{0,1},{1,0},{2,3},{3,2},{4,5},{5,4},{6,7},{7,6},{8,9},{9,8},{10,11... | collective-permute-start | bytes 2359304 | tf_op jit(solution)/shard_map/ppermute | solution.py:1170
  268.5 10.8 %copy-start.5 = (f32[384,1024]{1,0:T(8,128)S(1)}, f32[384,1024]{1,0:T(8,128)}, u32[]{:S(2)}) copy-start(f32[384,1024]{1,0:T(8,128)} %copy-done.4) | copy-start | bytes 4718596
  268.5 10.8 %copy-start.12 = (bf16[768,1152]{1,0:T(8,128)(2,1)S(1)}, bf16[768,1152]{1,0:T(8,128)(2,1)}, u32[]{:S(2)}) copy-start(bf16[768,1152]{1,0:T(8,128)(2,1)} %get-tuple-element.76.turned) | copy-start | bytes 5308420
  268.5 10.8 %copy-start.14 = (bf16[1024,384]{1,0:T(8,128)(2,1)S(1)}, bf16[1024,384]{1,0:T(8,128)(2,1)}, u32[]{:S(2)}) copy-start(bf16[1024,384]{1,0:T(8,128)(2,1)} %get-tuple-element.77.normed_turned) | copy-start | bytes 2359300
  268.6 10.8 %copy-start.16 = (bf16[384,1024]{1,0:T(8,128)(2,1)S(1)}, bf16[384,1024]{1,0:T(8,128)(2,1)}, u32[]{:S(2)}) copy-start(bf16[384,1024]{1,0:T(8,128)(2,1)} %copy-done.15) | copy-start | bytes 2359300
  278.4 0.9 copy-start.17
  279.3 1.1 copy-start.18
  280.5 42.6 %copy-start.20 = (s32[248]{0:T(256)S(1)}, s32[248]{0:T(256)}, u32[]{:S(2)}) copy-start(s32[248]{0:T(256)} %param.25) | copy-start | bytes 2980
  280.5 42.6 %copy-start.21 = (f32[248]{0:T(256)S(1)}, f32[248]{0:T(256)}, u32[]{:S(2)}) copy-start(f32[248]{0:T(256)} %constant.161.clone) | copy-start | bytes 2980
  321.3 173.0 %collective-permute-start.2 = (bf16[520,768]{1,0:T(8,128)(2,1)}, bf16[520,768]{1,0:T(8,128)(2,1)S(1)}, u32[]{:S(2)}, u32[]{:S(2)}) collective-permute-start(bf16[520,768]{1,0:T(8,128)(2,1)} %get-tuple-element.92), channel_id=1, source_target_pairs={{0,1},{1,0},{2,3},{3,2},{4,5},{5,4},{6,7},{7,6},{8,9},{9,8},{10,11... | collective-permute-start | bytes 2396168 | tf_op jit(solution)/shard_map/ppermute | solution.py:1170
